TPU v7x, 32 devices: a whole 2x2x4 slice. The times are simulated.
32 devices in a mesh: elem: 8 (over z, y), lev: 4 (over x, core).
Axes of the slice: x: 2, y: 2, z: 4, core: 2. Of those that a mesh axis runs over, the one named last changes fastest.
Arguments:
- tracers: bfloat16 [1024, 16, 1024], P('elem', 'lev'), may hold values from -6 to 6
- velocity: float32 [3, 16, 16, 1024], P(None, None, 'lev', 'elem'), may hold values from -6 to 6
- node_mass: float32 [16, 1024], P(None, 'elem'), may hold values from 0.5 to 2
- source: int32 [1024], P('elem'), may hold values from 0 to 1023, as said below
Outputs:
- advected: bfloat16 [1024, 16, 1024], P('elem', 'lev')
Inputs may be any that keep to these rules, and one draw needn't show every extreme that they name: The source of element e lies at most 64 elements before or after e along the curve, cyclically over 1024 elements. Within each aligned run of 128 elements, only the first 32 may take a source before the run and only the last 32 one after it; in every draw some run has all of its first 32 elements taking sources 64 elements before them, and some run all of its last 32 elements taking sources 64 elements after them.
All inputs are finite; a program needn't handle non-finite values.
Results may differ from a plain program's by a relative error of at most 0.006.
Values may be sent and summed in bfloat16 or wider, within the bound.
No kernel may reach another device: no remote copies, remote signals or barrier semaphores. Data moves between devices by JAX's collectives and lax.ppermute only.
A program may use at most 64 MiB of HBM per device.

v0:
```python
import jax
import jax.numpy as jnp
import numpy as np
from jax import lax
from jax.sharding import PartitionSpec as P

gll_points = (-1.0, -0.4472135954999579, 0.4472135954999579, 1.0)
east_nodes = np.array([3, 7, 11, 15])
west_nodes = np.array([0, 4, 8, 12])
courant = 0.15


def passed_along(value, axis, steps):
    count = lax.axis_size(axis)
    first, last = (max(0, -steps), min(count, count - steps))
    return lax.ppermute(value, axis, [(source, source + steps) for source in range(first, last)])


def from_behind(array, axis, by):
    peers = lax.axis_size(axis)
    return lax.ppermute(array, axis, [(i, (i + by) % peers) for i in range(peers)])


def lagrange(position):
    columns = []
    for column in range(4):
        factor = jnp.ones_like(position)
        for other in range(4):
            if other != column:
                factor = (
                    factor
                    * (position - gll_points[other])
                    / (gll_points[column] - gll_points[other])
                )
        columns.append(factor)
    return jnp.stack(columns, axis=0)


def weights(horizontal):
    along_nodes = jnp.array([gll_points[node % 4] for node in range(16)], jnp.float32)[
        :, None, None
    ]
    across_nodes = jnp.array([gll_points[node // 4] for node in range(16)], jnp.float32)[
        :, None, None
    ]
    along_basis = lagrange(along_nodes - courant * horizontal[0])
    across_basis = lagrange(across_nodes - courant * horizontal[1])
    table = across_basis[:, None] * along_basis[None, :]
    return table.reshape((16,) + table.shape[2:]).astype(jnp.bfloat16)


def share_wind(field, mass_east, mass_west, prev_east, prev_mass, next_west, next_mass):
    east = field[:, east_nodes]
    west = field[:, west_nodes]
    west_after = jnp.concatenate([west[..., 1:], next_west], axis=-1)
    mass_after = jnp.concatenate([mass_west[..., 1:], next_mass], axis=-1)
    shared = (mass_east * east + mass_after * west_after) / (mass_east + mass_after)
    east_before = jnp.concatenate([prev_east, east[..., :-1]], axis=-1)
    mass_before = jnp.concatenate([prev_mass, mass_east[..., :-1]], axis=-1)
    shared_west = (mass_before * east_before + mass_west * west) / (mass_before + mass_west)
    field = field.at[:, east_nodes].set(shared)
    return field.at[:, west_nodes].set(shared_west)


def share_columns(field, width, mass_east, mass_west, prev_east, prev_mass, next_west, next_mass):
    east = field[..., 3 * width :]
    west = field[..., :width]
    west_after = jnp.concatenate([west[1:], next_west], axis=0)
    mass_after = jnp.concatenate([mass_west[1:], next_mass], axis=0)
    shared = (mass_east * east + mass_after * west_after) / (mass_east + mass_after)
    east_before = jnp.concatenate([prev_east, east[:-1]], axis=0)
    mass_before = jnp.concatenate([prev_mass, mass_east[:-1]], axis=0)
    shared_west = (mass_before * east_before + mass_west * west) / (mass_before + mass_west)
    return jnp.concatenate([shared_west, field[..., width : 3 * width], shared], axis=-1)


def on_device(tracers, velocity, node_mass, source):
    elements, levels_here, columns_all = tracers.shape
    tracer_count = columns_all // 16
    total = elements * lax.axis_size("elem")
    start = lax.axis_index("elem") * elements
    shape_four = (elements, levels_here, 16, tracer_count)
    top_row = passed_along(tracers[:, levels_here - 1 :, :], "lev", 1)
    upper = jnp.concatenate([top_row, tracers[:, : levels_here - 1, :]], axis=1)
    descent = jnp.transpose(jax.nn.sigmoid(velocity[2]), (2, 1, 0))[..., None]
    descent_wide = jnp.broadcast_to(descent, shape_four).reshape(elements, levels_here, columns_all)
    lifted = (
        (1.0 - descent_wide) * tracers.astype(jnp.float32)
        + descent_wide * upper.astype(jnp.float32)
    ).astype(jnp.bfloat16)
    horizontal = velocity[:2]
    mass_east = node_mass[east_nodes]
    mass_west = node_mass[west_nodes]
    mass_east_wide = jnp.broadcast_to(mass_east[None, :, None, :], (1, 4, levels_here, elements))
    mass_west_wide = jnp.broadcast_to(mass_west[None, :, None, :], (1, 4, levels_here, elements))
    east_pack = jnp.concatenate(
        [horizontal[:, east_nodes, :, elements - 1 :], mass_east_wide[..., elements - 1 :]], axis=0
    )
    west_pack = jnp.concatenate([horizontal[:, west_nodes, :, :1], mass_west_wide[..., :1]], axis=0)
    wind_received = []
    for offset, packed in ((1, east_pack), (-1, west_pack)):
        wind_received.append(from_behind(packed, "elem", offset))
    prev_pack, next_pack = wind_received
    horizontal = share_wind(
        horizontal,
        mass_east_wide,
        mass_west_wide,
        prev_pack[:2],
        prev_pack[2:3],
        next_pack[:2],
        next_pack[2:3],
    )
    table = weights(horizontal)
    relative = (source - start) % total
    span = elements // 2
    cap = elements // 4
    local_blocks = jnp.take(lifted, jnp.minimum(relative, elements - 1), axis=0)
    head_relative = relative[:cap]
    tail_relative = relative[elements - cap :]
    need_before = head_relative >= total - span
    need_after = (tail_relative >= elements) & (tail_relative < elements + span)
    ask_before = jnp.where(need_before, head_relative + elements - total, 0)
    ask_after = jnp.where(need_after, tail_relative - elements, 0)
    answers = []
    for offset, asked in ((-1, ask_before), (1, ask_after)):
        wanted = from_behind(asked, "elem", offset)
        served = jnp.take(lifted, wanted, axis=0)
        answers.append(from_behind(served, "elem", -offset))
    head = jnp.where(need_before[:, None, None], answers[0], local_blocks[:cap])
    tail = jnp.where(need_after[:, None, None], answers[1], local_blocks[elements - cap :])
    blocks = jnp.concatenate([head, local_blocks[cap : elements - cap], tail], axis=0)
    moved = jnp.einsum(
        "mnke,ekmt->eknt", table, blocks.reshape(shape_four), preferred_element_type=jnp.float32
    ).astype(jnp.bfloat16)
    moved = moved.reshape(elements, levels_here, 4, 4 * tracer_count)
    east_last = moved[elements - 1 :, :, :, 3 * tracer_count :]
    west_first = moved[:1, :, :, :tracer_count]
    edge_received = []
    for offset, packed in ((1, east_last), (-1, west_first)):
        edge_received.append(from_behind(packed, "elem", offset))
    mass_east_rows = jnp.transpose(mass_east)[:, None, :, None]
    mass_west_rows = jnp.transpose(mass_west)[:, None, :, None]
    prev_mass_rows = prev_pack[2, :, 0, 0].reshape(1, 1, 4, 1)
    next_mass_rows = next_pack[2, :, 0, 0].reshape(1, 1, 4, 1)
    final = share_columns(
        moved.astype(jnp.float32),
        tracer_count,
        mass_east_rows,
        mass_west_rows,
        edge_received[0].astype(jnp.float32),
        prev_mass_rows,
        edge_received[1].astype(jnp.float32),
        next_mass_rows,
    )
    return final.astype(jnp.bfloat16).reshape(elements, levels_here, columns_all)


def solution(mesh):
    placed = (P("elem", "lev", None), P(None, None, "lev", "elem"), P(None, "elem"), P("elem"))
    return jax.shard_map(
        on_device, mesh=mesh, in_specs=placed, out_specs=P("elem", "lev", None), check_vma=False
    )
```

profile of v0, /device:TPU:0, one launch (start us, length us, event | category | flops | bytes accessed | tf_op | source)
XLA Modules:
  0.0 92.8 jit_solution(18167879308941584049)
XLA Ops:
  0.0 0.7 compare_and_fusion.3
  0.8 6.0 %collective-permute-start.3 = (s32[32]{0:T(128)S(1)}, s32[32]{0:T(128)S(1)}, u32[]{:S(2)}, u32[]{:S(2)}) collective-permute-start(s32[32]{0:T(128)S(1)} %get-tuple-element.41), channel_id=1, source_target_pairs={{0,28},{4,0},{8,4},{12,8},{16,12},{20,16},{24,20},{28,24},{1,29},{... | collective-permute-start | bytes 392 | tf_op jit(solution)/shard_map/ppermute | solution.py:21
  6.8 2.6 %slice.133 = bf16[128,1,1024]{2,1,0:T(2,128)(2,1)} slice(bf16[128,4,1024]{2,1,0:T(4,128)(2,1)} %param.18), slice={[0:128], [3:4], [0:1024]} | slice | bytes 524288 | tf_op jit(solution)/shard_map/slice | solution.py:83
  9.4 2.2 %collective-permute-start.2 = (bf16[128,1,1024]{2,1,0:T(2,128)(2,1)}, bf16[128,1,1024]{2,1,0:T(2,128)(2,1)}, u32[]{:S(2)}, u32[]{:S(2)}) collective-permute-start(bf16[128,1,1024]{2,1,0:T(2,128)(2,1)} %slice.133), channel_id=1, source_target_pairs={{0,1},{1,2},{2,3},{4,5},{5,6},{6,7},{8,9},{9,10},{10,11},{12,13},{... | collective-permute-start | bytes 786440 | tf_op jit(solution)/shard_map/ppermute | solution.py:16
  11.6 0.7 pad_clamp_fusion.4
  13.1 0.8 slice.113
  13.9 1.1 %copy.170 = f32[2,16,4,128]{2,0,3,1:T(2,128)S(1)} copy(f32[2,16,4,128]{3,2,1,0:T(4,128)S(1)} %slice.113) | data formatting | bytes 131072
  17.1 4.7 %collective-permute-start.1 = (f32[3,4,4,1]{2,1,0,3:T(4,128)S(1)}, f32[3,4,4,1]{2,1,0,3:T(4,128)S(1)}, u32[]{:S(2)}, u32[]{:S(2)}) collective-permute-start(f32[3,4,4,1]{2,1,0,3:T(4,128)S(1)} %pad_maximum_fusion.5), channel_id=1, source_target_pairs={{0,28},{4,0},{8,4},{12,8},{16,12},{20,16},{24,20},{28,24},{1,29},{... | collective-permute-start | bytes 584 | tf_op jit(solution)/shard_map/ppermute | solution.py:21
  21.9 1.1 %gather_fusion.5 = f32[4,2,4,128]{2,1,3,0:T(2,128)S(1)} fusion(f32[2,16,4,128]{2,0,3,1:T(2,128)S(1)} %copy.170, s32[1024]{0:T(1024)S(1)} %pad_clamp_fusion.3), kind=kCustom, calls=%fused_computation.7 | custom fusion | bytes 32784 | tf_op jit(solution)/shard_map/gather | solution.py:54
  23.0 1.1 %gather_fusion.2 = f32[4,2,4,128]{2,1,3,0:T(2,128)S(1)} fusion(f32[2,16,4,128]{2,0,3,1:T(2,128)S(1)} %copy.170, s32[1024]{0:T(1024)S(1)} %pad_clamp_fusion.4), kind=kCustom, calls=%fused_computation.4 | custom fusion | bytes 32784 | tf_op jit(solution)/shard_map/gather | solution.py:53
  24.4 2.1 %copy.160 = f32[128,4,1024]{2,1,0:T(4,128)} copy(f32[128,4,1024]{0,2,1:T(8,128)S(1)} %bitcast.62) | data formatting | bytes 4194304 | tf_op jit(solution)/shard_map/reshape | solution.py:86
  30.3 0.7 scatter_fusion
  31.7 0.7 scatter_fusion.1
  32.8 3.0 %copy.163 = bf16[16,16,4,128]{0,1,2,3:T(8,128)(2,1)S(1)} copy(bf16[16,16,4,128]{3,1,2,0:T(8,128)(2,1)S(1)} %bitcast.70) | data formatting | bytes 524288 | tf_op jit(solution)/shard_map/convert_element_type | solution.py:49
  35.9 4.1 %add_convert_fusion = bf16[128,4,1024]{2,1,0:T(4,128)(2,1)S(1)} fusion(f32[128,4,1024]{2,1,0:T(4,128)} %copy.160, bf16[128,4,1024]{2,1,0:T(4,128)(2,1)} %param.18, bf16[128,3,1024]{2,1,0:T(4,128)(2,1)} %bitcast.63, bf16[128,1,1024]{2,1,0:T(2,128)(2,1)} %collective-permute-done.2), kind=kLoop, calls=%fused_computation.11 | loop fusion | flops 5242880 | bytes 5242880 | tf_op jit(solution)/shard_map/convert_element_type | solution.py:90
  40.0 0.8 gather_fusion.8
  40.8 1.5 %gather_fusion.7 = bf16[32,4,1024]{2,1,0:T(4,128)(2,1)} fusion(bf16[128,4,1024]{2,1,0:T(4,128)(2,1)S(1)} %add_convert_fusion, s32[1024]{0:T(1024)S(1)} %pad_clamp_fusion.2), kind=kCustom, calls=%fused_computation.clone | custom fusion | bytes 524416 | tf_op jit(solution)/shard_map/jit(_take)/gather | solution.py:127
  42.2 2.4 %gather_fusion.6 = bf16[128,4,1024]{2,1,0:T(4,128)(2,1)} fusion(bf16[128,4,1024]{2,1,0:T(4,128)(2,1)S(1)} %add_convert_fusion, s32[1024]{0:T(1024)S(1)} %pad_clamp_fusion.1), kind=kCustom, calls=%fused_computation.8 | custom fusion | bytes 2097664 | tf_op jit(solution)/shard_map/jit(_take)/gather | solution.py:117
  44.6 1.2 %broadcast_select_fusion.2 = bf16[32,4,1024]{2,1,0:T(4,128)(2,1)S(1)} fusion(bf16[32,4,1024]{2,1,0:T(4,128)(2,1)} %gather_fusion.7, pred[32]{0:T(512)(128)(4,1)S(1)} %compare_and_fusion.1), kind=kLoop, calls=%fused_computation.32 | loop fusion | flops 131072 | bytes 524320 | tf_op jit(solution)/shard_map/jit(_take)/select_n | solution.py:127
  46.0 4.9 %collective-permute-start.6 = (bf16[32,4,1024]{2,1,0:T(4,128)(2,1)S(1)}, bf16[32,4,1024]{2,1,0:T(4,128)(2,1)S(1)}, u32[]{:S(2)}, u32[]{:S(2)}) collective-permute-start(bf16[32,4,1024]{2,1,0:T(4,128)(2,1)S(1)} %broadcast_select_fusion.1), channel_id=1, source_target_pairs={{0,28},{4,0},{8,4},{12,8},{16,12},{20,16},{24,20},{28,24},{1,29},{... | collective-permute-start | bytes 786440 | tf_op jit(solution)/shard_map/ppermute | solution.py:21
  51.0 1.8 %broadcast_select_fusion = bf16[128,4,1024]{2,1,0:T(4,128)(2,1)S(1)} fusion(bf16[128,4,1024]{2,1,0:T(4,128)(2,1)} %gather_fusion.6, pred[128]{0:T(512)(128)(4,1)S(1)} %get-tuple-element.6), kind=kLoop, calls=%fused_computation.15 | loop fusion | flops 524288 | bytes 2097280 | tf_op jit(solution)/shard_map/jit(_take)/select_n | solution.py:117
  52.9 4.8 %collective-permute-done.4 = bf16[32,4,1024]{2,1,0:T(4,128)(2,1)S(1)} collective-permute-done((bf16[32,4,1024]{2,1,0:T(4,128)(2,1)S(1)}, bf16[32,4,1024]{2,1,0:T(4,128)(2,1)S(1)}, u32[]{:S(2)}, u32[]{:S(2)}) %collective-permute-start.4) | collective-permute-done | bytes 262176 | tf_op jit(solution)/shard_map/ppermute | solution.py:21
  57.7 3.3 %collective-permute-done.6 = bf16[32,4,1024]{2,1,0:T(4,128)(2,1)S(1)} collective-permute-done((bf16[32,4,1024]{2,1,0:T(4,128)(2,1)S(1)}, bf16[32,4,1024]{2,1,0:T(4,128)(2,1)S(1)}, u32[]{:S(2)}, u32[]{:S(2)}) %collective-permute-start.6) | collective-permute-done | bytes 262176 | tf_op jit(solution)/shard_map/ppermute | solution.py:21
  61.4 1.7 %pad_maximum_fusion = bf16[128,4,1024]{2,1,0:T(4,128)(2,1)} fusion(bf16[32,4,1024]{2,1,0:T(4,128)(2,1)S(1)} %get-tuple-element.16, bf16[64,4,1024]{2,1,0:T(4,128)(2,1)S(1)} %slice.177, bf16[32,4,1024]{2,1,0:T(4,128)(2,1)S(1)} %get-tuple-element.15), kind=kLoop, calls=%fused_computation.13 | loop fusion | flops 1048576 | bytes 2097152 | tf_op jit(solution)/shard_map/concatenate | solution.py:131
  63.1 1.9 %copy.162 = bf16[128,4,1024]{0,2,1:T(8,128)(2,1)S(1)} copy(bf16[128,4,1024]{2,1,0:T(4,128)(2,1)} %pad_maximum_fusion) | data formatting | bytes 2097152 | tf_op jit(solution)/shard_map/concatenate | solution.py:131
  65.1 3.8 %copy.164 = bf16[128,4,16,64]{3,2,1,0:T(8,128)(2,1)} copy(bf16[128,4,16,64]{0,3,2,1:T(8,128)(2,1)S(1)} %bitcast.64) | data formatting | bytes 2097152 | tf_op jit(solution)/shard_map/reshape | solution.py:133
  68.9 4.1 %convolution_convert_fusion = bf16[128,4,16,64]{3,2,1,0:T(8,128)(2,1)} fusion(bf16[16,16,4,128]{0,1,2,3:T(8,128)(2,1)S(1)} %copy.163, bf16[128,4,16,64]{3,2,1,0:T(8,128)(2,1)} %copy.164), kind=kOutput, calls=%fused_computation.12 | convolution fusion | flops 17301504 | bytes 2359296 | tf_op jit(solution)/shard_map/mnke,ekmt->eknt/dot_general | solution.py:132
  73.0 3.3 %copy.165 = bf16[128,4,16,64]{0,3,2,1:T(8,128)(2,1)S(1)} copy(bf16[128,4,16,64]{3,2,1,0:T(8,128)(2,1)} %convolution_convert_fusion) | data formatting | bytes 2097152 | tf_op jit(solution)/shard_map/convert_element_type | solution.py:134
  76.5 4.7 %collective-permute-start.8 = (bf16[1,4,4,64]{0,3,2,1:T(8,128)(2,1)S(1)}, bf16[1,4,4,64]{0,3,2,1:T(8,128)(2,1)S(1)}, u32[]{:S(2)}, u32[]{:S(2)}) collective-permute-start(bf16[1,4,4,64]{0,3,2,1:T(8,128)(2,1)S(1)} %get-tuple-element.14), channel_id=1, source_target_pairs={{0,28},{4,0},{8,4},{12,8},{16,12},{20,16},{24,20},{28,24},{1,29},{... | collective-permute-start | bytes 6152 | tf_op jit(solution)/shard_map/ppermute | solution.py:21
  81.7 6.6 %collective-permute-done.7 = bf16[1,4,4,64]{0,3,2,1:T(8,128)(2,1)S(1)} collective-permute-done((bf16[1,4,4,64]{0,3,2,1:T(8,128)(2,1)S(1)}, bf16[1,4,4,64]{0,3,2,1:T(8,128)(2,1)S(1)}, u32[]{:S(2)}, u32[]{:S(2)}) %collective-permute-start.7) | collective-permute-done | bytes 2080 | tf_op jit(solution)/shard_map/ppermute | solution.py:21
  88.3 2.2 %collective-permute-done.8 = bf16[1,4,4,64]{0,3,2,1:T(8,128)(2,1)S(1)} collective-permute-done((bf16[1,4,4,64]{0,3,2,1:T(8,128)(2,1)S(1)}, bf16[1,4,4,64]{0,3,2,1:T(8,128)(2,1)S(1)}, u32[]{:S(2)}, u32[]{:S(2)}) %collective-permute-start.8) | collective-permute-done | bytes 2080 | tf_op jit(solution)/shard_map/ppermute | solution.py:21
  91.1 1.7 %copy.169 = bf16[128,4,1024]{2,1,0:T(4,128)(2,1)} copy(bf16[128,4,1024]{0,2,1:T(8,128)(2,1)S(1)} %bitcast.65) | data formatting | bytes 2097152 | tf_op jit(solution)/shard_map/convert_element_type | solution.py:155
  (102 shorter events, 10.1 us)
Async XLA Ops:
  0.0 12.3 %copy-start = (f32[16,128]{1,0:T(8,128)S(1)}, f32[16,128]{1,0:T(8,128)}, u32[]{:S(2)}) copy-start(f32[16,128]{1,0:T(8,128)} %param.20) | copy-start | bytes 24580
  0.0 15.0 %copy-start.1 = (s32[4]{0:T(128)S(1)}, s32[4]{0:T(128)}, u32[]{:S(2)}) copy-start(s32[4]{0:T(128)} %constant.178) | copy-start | bytes 52
  0.0 24.2 %slice-start = ((f32[3,16,4,128]{3,2,1,0:T(4,128)}), f32[1,16,4,128]{3,2,1,0:T(4,128)S(1)}, s32[]{:S(2)}) async-start(f32[3,16,4,128]{3,2,1,0:T(4,128)} %param.19), calls=%async_computation | async-start | bytes 65536 | tf_op jit(solution)/shard_map/slice | solution.py:85
  0.8 27.9 %collective-permute-start.3 = (s32[32]{0:T(128)S(1)}, s32[32]{0:T(128)S(1)}, u32[]{:S(2)}, u32[]{:S(2)}) collective-permute-start(s32[32]{0:T(128)S(1)} %get-tuple-element.41), channel_id=1, source_target_pairs={{0,28},{4,0},{8,4},{12,8},{16,12},{20,16},{24,20},{28,24},{1,29},{... | collective-permute-start | bytes 392 | tf_op jit(solution)/shard_map/ppermute | solution.py:21
  6.8 22.0 %collective-permute-start.5 = (s32[32]{0:T(128)S(1)}, s32[32]{0:T(128)S(1)}, u32[]{:S(2)}, u32[]{:S(2)}) collective-permute-start(s32[32]{0:T(128)S(1)} %get-tuple-element.42), channel_id=1, source_target_pairs={{0,4},{4,8},{8,12},{12,16},{16,20},{20,24},{24,28},{28,0},{1,5},{5... | collective-permute-start | bytes 392 | tf_op jit(solution)/shard_map/ppermute | solution.py:21
  9.4 26.5 %collective-permute-start.2 = (bf16[128,1,1024]{2,1,0:T(2,128)(2,1)}, bf16[128,1,1024]{2,1,0:T(2,128)(2,1)}, u32[]{:S(2)}, u32[]{:S(2)}) collective-permute-start(bf16[128,1,1024]{2,1,0:T(2,128)(2,1)} %slice.133), channel_id=1, source_target_pairs={{0,1},{1,2},{2,3},{4,5},{5,6},{6,7},{8,9},{9,10},{10,11},{12,13},{... | collective-permute-start | bytes 786440 | tf_op jit(solution)/shard_map/ppermute | solution.py:16
  15.7 13.1 %collective-permute-start = (f32[3,4,4,1]{2,1,0,3:T(4,128)S(1)}, f32[3,4,4,1]{2,1,0,3:T(4,128)S(1)}, u32[]{:S(2)}, u32[]{:S(2)}) collective-permute-start(f32[3,4,4,1]{2,1,0,3:T(4,128)S(1)} %pad_maximum_fusion.4), channel_id=1, source_target_pairs={{0,4},{4,8},{8,12},{12,16},{16,20},{20,24},{24,28},{28,0},{1,5},{5... | collective-permute-start | bytes 584 | tf_op jit(solution)/shard_map/ppermute | solution.py:21
  17.1 12.1 %collective-permute-start.1 = (f32[3,4,4,1]{2,1,0,3:T(4,128)S(1)}, f32[3,4,4,1]{2,1,0,3:T(4,128)S(1)}, u32[]{:S(2)}, u32[]{:S(2)}) collective-permute-start(f32[3,4,4,1]{2,1,0,3:T(4,128)S(1)} %pad_maximum_fusion.5), channel_id=1, source_target_pairs={{0,28},{4,0},{8,4},{12,8},{16,12},{20,16},{24,20},{28,24},{1,29},{... | collective-permute-start | bytes 584 | tf_op jit(solution)/shard_map/ppermute | solution.py:21
  28.0 2.3 %copy-start.2 = (s32[4]{0:T(128)S(1)}, s32[4]{0:T(128)}, u32[]{:S(2)}) copy-start(s32[4]{0:T(128)} %constant.179) | copy-start | bytes 52
  28.3 4.2 %copy-start.3 = (f32[16]{0:T(128)S(1)}, f32[16]{0:T(128)}, u32[]{:S(2)}) copy-start(f32[16]{0:T(128)} %constant.138.clone) | copy-start | bytes 196
  28.3 4.2 %copy-start.4 = (f32[16]{0:T(128)S(1)}, f32[16]{0:T(128)}, u32[]{:S(2)}) copy-start(f32[16]{0:T(128)} %constant.137.clone) | copy-start | bytes 196
  45.7 12.0 %collective-permute-start.4 = (bf16[32,4,1024]{2,1,0:T(4,128)(2,1)S(1)}, bf16[32,4,1024]{2,1,0:T(4,128)(2,1)S(1)}, u32[]{:S(2)}, u32[]{:S(2)}) collective-permute-start(bf16[32,4,1024]{2,1,0:T(4,128)(2,1)S(1)} %broadcast_select_fusion.2), channel_id=1, source_target_pairs={{0,4},{4,8},{8,12},{12,16},{16,20},{20,24},{24,28},{28,0},{1,5},{5... | collective-permute-start | bytes 786440 | tf_op jit(solution)/shard_map/ppermute | solution.py:21
  46.0 15.0 %collective-permute-start.6 = (bf16[32,4,1024]{2,1,0:T(4,128)(2,1)S(1)}, bf16[32,4,1024]{2,1,0:T(4,128)(2,1)S(1)}, u32[]{:S(2)}, u32[]{:S(2)}) collective-permute-start(bf16[32,4,1024]{2,1,0:T(4,128)(2,1)S(1)} %broadcast_select_fusion.1), channel_id=1, source_target_pairs={{0,28},{4,0},{8,4},{12,8},{16,12},{20,16},{24,20},{28,24},{1,29},{... | collective-permute-start | bytes 786440 | tf_op jit(solution)/shard_map/ppermute | solution.py:21
  76.4 11.8 %collective-permute-start.7 = (bf16[1,4,4,64]{0,3,2,1:T(8,128)(2,1)S(1)}, bf16[1,4,4,64]{0,3,2,1:T(8,128)(2,1)S(1)}, u32[]{:S(2)}, u32[]{:S(2)}) collective-permute-start(bf16[1,4,4,64]{0,3,2,1:T(8,128)(2,1)S(1)} %get-tuple-element.13), channel_id=1, source_target_pairs={{0,4},{4,8},{8,12},{12,16},{16,20},{20,24},{24,28},{28,0},{1,5},{5... | collective-permute-start | bytes 6152 | tf_op jit(solution)/shard_map/ppermute | solution.py:21
  76.5 14.0 %collective-permute-start.8 = (bf16[1,4,4,64]{0,3,2,1:T(8,128)(2,1)S(1)}, bf16[1,4,4,64]{0,3,2,1:T(8,128)(2,1)S(1)}, u32[]{:S(2)}, u32[]{:S(2)}) collective-permute-start(bf16[1,4,4,64]{0,3,2,1:T(8,128)(2,1)S(1)} %get-tuple-element.14), channel_id=1, source_target_pairs={{0,28},{4,0},{8,4},{12,8},{16,12},{20,16},{24,20},{28,24},{1,29},{... | collective-permute-start | bytes 6152 | tf_op jit(solution)/shard_map/ppermute | solution.py:21
where the time goes:
time: 93.2 us; the launch traced here: 92.8 us
  local copies, waits for them, and re-layouts  34.8 us (37%)
  starting transfers between devices  22.7 us (24%)
  waiting for transfers between devices  16.8 us (18%)
  other arithmetic  13.8 us (15%)
  matrix products  4.12 us (4%)
    ppermute x8, starting transfers between devices, from_behind(): lax.ppermute(array, axis, [(i, (i + by) % peers) for i in range(peers)])  20.5 us
    ppermute x8, waiting for transfers between devices, from_behind(): lax.ppermute(array, axis, [(i, (i + by) % peers) for i in range(peers)])  16.8 us
    dot_general x1, matrix products, on_device(): jnp.einsum('mnke,ekmt->eknt', table, blocks.reshape(shape_four), preferre...  4.12 us
    convert_element_type x1, other arithmetic, on_device(): lifted = ((1.0 - descent_wide) * tracers.astype(jnp.float32) + descent_wi...  4.08 us
    reshape x1, local copies, waits for them, and re-layouts, on_device(): blocks.reshape(shape_four)  3.8 us
    convert_element_type x1, local copies, waits for them, and re-layouts, on_device(): moved = jnp.einsum('mnke,ekmt->eknt', table, blocks.reshape(shape_four),...  3.32 us
    convert_element_type x1, local copies, waits for them, and re-layouts, weights(): return table.reshape((16,) + table.shape[2:]).astype(jnp.bfloat16)  3.02 us
    slice x1, local copies, waits for them, and re-layouts, on_device(): top_row = passed_along(tracers[:, levels_here - 1:, :], 'lev', 1)  2.6 us
  transfers between devices with their start and end apart: 9, of which 4 were waited for; matrix products, arithmetic and copies ran while one was open for 26% of the time, Pallas kernels for 0%

commit v1 on v0

v1 whole, which is shorter than its diff:
```python
import functools

import jax
import jax.numpy as jnp
from jax import lax
from jax.experimental import pallas as pl
from jax.experimental.pallas import tpu as pltpu
from jax.sharding import PartitionSpec as P

gll_points = (-1.0, -0.4472135954999579, 0.4472135954999579, 1.0)
courant = 0.15
f32 = jnp.float32
bf16 = jnp.bfloat16
VMEM_LIMIT = 40 << 20
CHUNK = 16

MASS, NEAR, NEAR_MASS, SOURCE, PACKET = 32, 48, 56, 60, 64


def params():
    return pltpu.CompilerParams(vmem_limit_bytes=VMEM_LIMIT)


def ring(array, axis, by):
    peers = lax.axis_size(axis)
    return lax.ppermute(array, axis, [(i, (i + by) % peers) for i in range(peers)])


def interleave(groups, members):
    size = groups * members
    row = lax.broadcasted_iota(jnp.int32, (size, size), 0)
    column = lax.broadcasted_iota(jnp.int32, (size, size), 1)
    same = (row // groups == column % members) & (row % groups == column // members)
    return jnp.where(same, 1.0, 0.0).astype(bf16)


def basis(position):
    out = []
    for a in range(4):
        scale = 1.0
        factor = None
        for other in range(4):
            if other != a:
                scale /= gll_points[a] - gll_points[other]
                term = position - gll_points[other]
                factor = term if factor is None else factor * term
        out.append(factor * scale)
    return out


def node_rows(rows, lanes, of_i):
    row = lax.broadcasted_iota(jnp.int32, (rows, lanes), 0)
    index = row // 4 if of_i else row % 4
    out = jnp.full((rows, lanes), gll_points[0], f32)
    for a in range(1, 4):
        out = jnp.where(index == a, gll_points[a], out)
    return out


def table(winds, coefficient):
    rows, lanes = winds[0].shape
    along = basis(node_rows(rows, lanes, True) - courant * winds[0])
    across_position = node_rows(rows, lanes, False) - courant * winds[1]
    across = [factor * coefficient for factor in basis(across_position)]
    return along, across


def pack_kernel(velocity_ref, mass_ref, source_ref, head_ref, tail_ref):
    _, _, levels, elements = velocity_ref.shape
    cap = elements // levels
    runs = lax.axis_size("elem")
    start = lax.axis_index("elem") * elements
    total = runs * elements
    for out_ref, low, nodes, step in (
        (head_ref, 0, 0, 1),
        (tail_ref, elements - cap, 3, -1),
    ):
        def lanes(pieces, shift=0):
            return jnp.concatenate([x[:, low + shift : low + shift + cap] for x in pieces], axis=1)

        for c in range(2):
            pieces = [velocity_ref[c, :, k, :] for k in range(levels)]
            out_ref[16 * c : 16 * c + 16, :] = lanes(pieces)
            near = lanes(pieces, step)
            for j in range(4):
                out_ref[NEAR + 4 * c + j : NEAR + 4 * c + j + 1, :] = near[4 * j + nodes : 4 * j + nodes + 1]
        mass = mass_ref[...]
        out_ref[MASS : MASS + 16, :] = lanes([mass] * levels)
        near = lanes([mass] * levels, step)
        for j in range(4):
            out_ref[NEAR_MASS + j : NEAR_MASS + j + 1, :] = near[4 * j + nodes : 4 * j + nodes + 1]
        relative = source_ref[...] - start + (elements if step == 1 else -elements)
        relative = jnp.where(relative < 0, relative + total, relative)
        relative = jnp.where(relative < 0, relative + total, relative)
        relative = jnp.where(relative >= total, relative - total, relative)
        out_ref[SOURCE : SOURCE + 1, :] = lanes([relative.astype(f32)] * levels)
        out_ref[SOURCE + 1 :, :] = jnp.zeros((PACKET - SOURCE - 1, elements), f32)


def transpose_kernel(tracers_ref, out_ref, lowest_ref):
    elements, levels, columns = tracers_ref.shape
    order = interleave(levels, elements)
    x = tracers_ref[...].reshape(elements * levels, columns)
    step = 256
    for c in range(0, columns, step):
        y = lax.dot_general(
            x[:, c : c + step], order, (((0,), (0,)), ((), ())), preferred_element_type=f32
        ).astype(bf16)
        out_ref[c : c + step, :] = y
        lowest_ref[c : c + step, :] = y[:, (levels - 1) * elements :]


def lift_kernel(here_ref, above_ref, velocity_ref, out_ref):
    _, nodes, levels, elements = velocity_ref.shape
    tracers = here_ref.shape[0] // nodes
    for k in range(levels):
        descent = 1.0 / (1.0 + jnp.exp(-velocity_ref[0, :, k, :]))
        lanes = slice(k * elements, (k + 1) * elements)
        for m in range(nodes):
            rows = slice(m * tracers, (m + 1) * tracers)
            here = here_ref[rows, lanes].astype(f32)
            if k == 0:
                upper = above_ref[rows, :].astype(f32)
            else:
                upper = here_ref[rows, (k - 1) * elements : k * elements].astype(f32)
            d = descent[m : m + 1]
            out_ref[rows, lanes] = ((1.0 - d) * here + d * upper).astype(bf16)


def by_i(ref, first, nodes=16):
    return [ref[pl.ds(first + i, 4, stride=4), :] for i in range(4)]


def shared(mass_left, left, mass_right, right):
    return (mass_left * left + mass_right * right) / (mass_left + mass_right)


def interpolate(weights_ref, blocks_ref, node, rows, lanes):
    total = None
    for m in range(16):
        term = weights_ref[m, node : node + 1, :] * blocks_ref[m, rows, lanes]
        total = term if total is None else total + term
    return total


def remote_kernel(ahead, packet_ref, own_ref, lifted_ref, out_ref, blocks_ref, weights_ref, extra_ref):
    levels = lifted_ref.shape[1] // packet_ref.shape[1]
    lanes_all = packet_ref.shape[1]
    elements = lanes_all
    cap = elements // levels
    tracers = lifted_ref.shape[0] // 16
    total = lax.axis_size("elem") * elements
    lane = lax.broadcasted_iota(jnp.int32, (1, lanes_all), 1)
    level, place = lane // cap, lane % cap
    edge = place == (0 if ahead else cap - 1)

    def beside(values, own):
        if ahead:
            return jnp.where(edge, pltpu.roll(own, lanes_all - (cap - 1), 1), pltpu.roll(values, 1, 1))
        return jnp.where(edge, pltpu.roll(own, cap - 1, 1), pltpu.roll(values, lanes_all - 1, 1))

    mass = by_i(packet_ref, MASS)
    own_mass = by_i(own_ref, MASS)
    near_mass = packet_ref[NEAR_MASS : NEAR_MASS + 4, :]
    if ahead:
        mass_before, mass_after = beside(mass[3], own_mass[3]), near_mass
    else:
        mass_before, mass_after = near_mass, beside(mass[0], own_mass[0])
    share_west = mass[0] / (mass_before + mass[0])
    share_east = mass[3] / (mass[3] + mass_after)
    winds = []
    edge_winds = []
    for c in range(2):
        wind = by_i(packet_ref, 16 * c)
        own = by_i(own_ref, 16 * c)
        near = packet_ref[NEAR + 4 * c : NEAR + 4 * c + 4, :]
        if ahead:
            before, after = beside(wind[3], own[3]), near
        else:
            before, after = near, beside(wind[0], own[0])
        west = shared(mass_before, before, mass[0], wind[0])
        east = shared(mass[3], wind[3], mass_after, after)
        winds.append(jnp.concatenate([west, wind[1], wind[2], east], axis=0))
        edge_winds.append(west if ahead else east)
    ones = jnp.ones((8, lanes_all), f32)
    along, across = table(winds, jnp.concatenate([share_west, ones, share_east], axis=0))
    for b in range(4):
        for a in range(4):
            weights_ref[4 * b + a] = along[a] * across[b]
    edge_share = 1.0 - (share_west if ahead else share_east)
    extra_along = basis(gll_points[3 if ahead else 0] - courant * edge_winds[0])
    across_position = node_rows(4, lanes_all, False) - courant * edge_winds[1]
    extra_across = [factor * edge_share for factor in basis(across_position)]
    for b in range(4):
        for a in range(4):
            extra_ref[4 * b + a, 0:4] = extra_along[a] * extra_across[b]

    source = packet_ref[SOURCE : SOURCE + 1, :].astype(jnp.int32)
    own_source = own_ref[SOURCE : SOURCE + 1, :].astype(jnp.int32) + (elements if ahead else -elements)
    own_source = jnp.where(own_source >= total, own_source - total, own_source)
    own_source = jnp.where(own_source < 0, own_source + total, own_source)
    own_source = pltpu.roll(own_source, lanes_all - (cap - 1) if ahead else cap - 1, 1)
    row = lax.broadcasted_iota(jnp.int32, (levels * elements, lanes_all), 0)
    same = row // elements == level
    first = jnp.where(same & (row % elements == source), 1.0, 0.0).astype(bf16)
    second = jnp.where(same & edge & (row % elements == own_source), 1.0, 0.0).astype(bf16)
    chosen = jnp.concatenate([first, second], axis=1)
    step = 4
    for m in range(0, 16, step):
        y = jnp.dot(lifted_ref[m * tracers : (m + step) * tracers, :], chosen, preferred_element_type=f32)
        blocks_ref[m : m + step] = y.reshape(step, tracers, 2 * lanes_all)

    def one(index, carry):
        t = pl.multiple_of(index * CHUNK, CHUNK)
        rows = pl.ds(t, CHUNK)
        lanes = slice(0, lanes_all)
        for j in range(4):
            moved = [interpolate(weights_ref, blocks_ref, 4 * i + j, rows, lanes) for i in range(4)]
            own = interpolate(extra_ref, blocks_ref, j, rows, slice(lanes_all, 2 * lanes_all))
            if ahead:
                west = moved[0] + jnp.where(edge, own, pltpu.roll(moved[3], 1, 1))
                east = jnp.where(place == cap - 1, moved[3], pltpu.roll(west, lanes_all - 1, 1))
            else:
                east = moved[3] + jnp.where(edge, own, pltpu.roll(moved[0], lanes_all - 1, 1))
                west = jnp.where(place == 0, moved[0], pltpu.roll(east, 1, 1))
            for i, value in enumerate((west, moved[1], moved[2], east)):
                out_ref[pl.ds(t + (4 * j + i) * tracers, CHUNK), :] = value.astype(bf16)
        return carry

    lax.fori_loop(0, tracers // CHUNK, one, 0)


def local_kernel(velocity_ref, mass_ref, source_ref, lifted_ref, out_ref, blocks_ref, weights_ref, wind_ref, moved_ref):
    _, _, levels, elements = velocity_ref.shape
    columns = out_ref.shape[2]
    tracers = columns // 16
    start = lax.axis_index("elem") * elements
    lane = lax.broadcasted_iota(jnp.int32, (1, elements), 1)
    mass = by_i(mass_ref, 0)
    mass_before = pltpu.roll(mass[3], 1, 1)
    mass_after = pltpu.roll(mass[0], elements - 1, 1)
    share_west = mass[0] / (mass_before + mass[0])
    share_east = mass[3] / (mass[3] + mass_after)
    coefficient = jnp.concatenate([share_west, jnp.ones((8, elements), f32), share_east], axis=0)
    row = lax.broadcasted_iota(jnp.int32, (elements, elements), 0)
    chosen = jnp.where(row == source_ref[...] - start, 1.0, 0.0).astype(bf16)
    for k in range(levels):
        winds = []
        for c in range(2):
            wind_ref[c] = velocity_ref[c, :, k, :]
            wind = [wind_ref[c, pl.ds(i, 4, stride=4), :] for i in range(4)]
            west = shared(mass_before, pltpu.roll(wind[3], 1, 1), mass[0], wind[0])
            east = shared(mass[3], wind[3], mass_after, pltpu.roll(wind[0], elements - 1, 1))
            winds.append(jnp.concatenate([west, wind[1], wind[2], east], axis=0))
        along, across = table(winds, coefficient)
        for b in range(4):
            for a in range(4):
                weights_ref[4 * b + a] = along[a] * across[b]
        lanes = slice(k * elements, (k + 1) * elements)
        y = jnp.dot(lifted_ref[:, lanes], chosen, preferred_element_type=f32)
        blocks_ref[...] = y.reshape(16, tracers, elements)

        def one(index, carry):
            t = pl.multiple_of(index * CHUNK, CHUNK)
            rows = pl.ds(t, CHUNK)
            for j in range(4):
                moved = [
                    interpolate(weights_ref, blocks_ref, 4 * i + j, rows, slice(0, elements)) for i in range(4)
                ]
                west = jnp.where(lane == 0, 0.0, moved[0] + pltpu.roll(moved[3], 1, 1))
                east = pltpu.roll(west, elements - 1, 1)
                for i, value in enumerate((west, moved[1], moved[2], east)):
                    moved_ref[pl.ds(t + (4 * j + i) * tracers, CHUNK), lanes] = value.astype(bf16)
            return carry

        lax.fori_loop(0, tracers // CHUNK, one, 0)
    order = interleave(levels, elements)
    step = 256
    for c in range(0, columns, step):
        y = lax.dot_general(
            order, moved_ref[c : c + step, :], (((1,), (1,)), ((), ())), preferred_element_type=f32
        )
        out_ref[:, :, c : c + step] = y.reshape(elements, levels, step).astype(bf16)


def combine_kernel(part_ref, head_ref, tail_ref, ahead_ref, back_ref, out_ref, first_ref, last_ref, sems):
    elements, levels, columns = out_ref.shape
    lanes_all = head_ref.shape[1]
    cap = elements // levels
    tracers = columns // 16
    span = 4 * tracers
    spots = ((first_ref, pl.ds(0, cap + 1)), (last_ref, pl.ds(elements - cap - 1, cap + 1)))
    loads = [pltpu.make_async_copy(out_ref.at[rows], ref, sems.at[n]) for n, (ref, rows) in enumerate(spots)]
    for load in loads:
        load.start()
    place = lax.broadcasted_iota(jnp.int32, (1, lanes_all), 1) % cap
    column = lax.broadcasted_iota(jnp.int32, (1, columns), 1) % span
    order = interleave(levels, cap)
    stores = []
    for n, (ref, rows) in enumerate(spots):
        received_ref = (head_ref, tail_ref)[n]
        pieces = []
        for node in range(16):
            value = received_ref[node * tracers : (node + 1) * tracers, :]
            if n == 0 and node % 4 == 0:
                own = back_ref[(node + 3) * tracers : (node + 4) * tracers, :].astype(f32)
                own = pltpu.roll(own, lanes_all - (cap - 1), 1)
                value = (value.astype(f32) + jnp.where(place == 0, own, 0.0)).astype(bf16)
            if n == 1 and node % 4 == 3:
                own = ahead_ref[(node - 3) * tracers : (node - 2) * tracers, :].astype(f32)
                own = pltpu.roll(own, cap - 1, 1)
                value = (value.astype(f32) + jnp.where(place == cap - 1, own, 0.0)).astype(bf16)
            pieces.append(value)
        received = jnp.concatenate(pieces, axis=0)
        y = lax.dot_general(order, received, (((1,), (1,)), ((), ())), preferred_element_type=f32)
        y = y.reshape(cap, levels, columns)
        loads[n].wait()
        if n == 0:
            ref[0:cap] = (ref[0:cap].astype(f32) + y).astype(bf16)
            east = pltpu.roll(y[cap - 1], columns - 3 * tracers, 1)
            ref[cap] = (ref[cap].astype(f32) + jnp.where(column < tracers, east, 0.0)).astype(bf16)
        else:
            ref[1 : cap + 1] = (ref[1 : cap + 1].astype(f32) + y).astype(bf16)
            west = pltpu.roll(y[0], 3 * tracers, 1)
            ref[0] = (ref[0].astype(f32) + jnp.where(column >= 3 * tracers, west, 0.0)).astype(bf16)
        store = pltpu.make_async_copy(ref, out_ref.at[rows], sems.at[2 + n])
        store.start()
        stores.append(store)
    for store in stores:
        store.wait()


def on_device(tracers, velocity, node_mass, source):
    elements, levels, columns = tracers.shape
    count = columns // 16
    lanes = levels * elements
    shape = jax.ShapeDtypeStruct
    source = source.reshape(1, elements)
    packet = shape((PACKET, elements), f32)
    head, tail = pl.pallas_call(
        pack_kernel, out_shape=(packet, packet), compiler_params=params(), name="pack"
    )(velocity, node_mass, source)
    next_head = ring(head, "elem", -1)
    prev_tail = ring(tail, "elem", 1)
    here, lowest = pl.pallas_call(
        transpose_kernel,
        out_shape=(shape((columns, lanes), bf16), shape((columns, elements), bf16)),
        compiler_params=params(),
        name="transpose",
    )(tracers)
    blocks = lax.axis_size("lev")
    above = lax.ppermute(lowest, "lev", [(i, i + 1) for i in range(blocks - 1)])
    lifted = pl.pallas_call(
        lift_kernel, out_shape=shape((columns, lanes), bf16), compiler_params=params(), name="lift"
    )(here, above, velocity[2:])

    def contributions(ahead, packet, own):
        return pl.pallas_call(
            functools.partial(remote_kernel, ahead),
            out_shape=shape((columns, elements), bf16),
            scratch_shapes=[
                pltpu.VMEM((16, count, 2 * elements), f32),
                pltpu.VMEM((16, 16, elements), f32),
                pltpu.VMEM((16, 8, elements), f32),
            ],
            compiler_params=params(),
            name="remote_ahead" if ahead else "remote_back",
        )(packet, own, lifted)

    ahead = contributions(True, next_head, tail)
    back = contributions(False, prev_tail, head)
    from_prev = ring(ahead, "elem", 1)
    from_next = ring(back, "elem", -1)
    part = pl.pallas_call(
        local_kernel,
        out_shape=shape((elements, levels, columns), bf16),
        scratch_shapes=[
            pltpu.VMEM((16, count, elements), f32),
            pltpu.VMEM((16, 16, elements), f32),
            pltpu.VMEM((2, 16, elements), f32),
            pltpu.VMEM((columns, lanes), bf16),
        ],
        compiler_params=params(),
        name="local",
    )(velocity, node_mass, source, lifted)
    cap = elements // levels
    vmem = pl.BlockSpec(memory_space=pltpu.VMEM)
    anywhere = pl.BlockSpec(memory_space=pl.ANY)
    return pl.pallas_call(
        combine_kernel,
        out_shape=shape((elements, levels, columns), bf16),
        in_specs=[anywhere, vmem, vmem, vmem, vmem],
        out_specs=anywhere,
        scratch_shapes=[
            pltpu.VMEM((cap + 1, levels, columns), bf16),
            pltpu.VMEM((cap + 1, levels, columns), bf16),
            pltpu.SemaphoreType.DMA((4,)),
        ],
        input_output_aliases={0: 0},
        compiler_params=params(),
        name="combine",
    )(part, from_prev, from_next, ahead, back)


def solution(mesh):
    placed = (P("elem", "lev", None), P(None, None, "lev", "elem"), P(None, "elem"), P("elem"))
    return jax.shard_map(
        on_device, mesh=mesh, in_specs=placed, out_specs=P("elem", "lev", None), check_vma=False
    )
```

time: 93.2 us -> 33.3 us (0.36)
  local copies, waits for them, and re-layouts: 34.8 us -> 1.24 us
  other arithmetic: 13.8 us -> 0 us
  starting transfers between devices: 22.7 us -> 9.47 us
  Pallas kernels: 0 us -> 12.4 us
  waiting for transfers between devices: 16.8 us -> 9.95 us
  matrix products: 4.12 us -> 0 us
    ppermute x9 -> x5, starting transfers between devices: 22.7 us -> 9.47 us  [the longest x4 7.11 us: ring(): lax.ppermute(array, axis, [(i, (i + by) % peers) for i in range(peers)])]
    pallas_call x0 -> x7, Pallas kernels: none -> 12.4 us  [the longest x1 5.89 us: on_device(): pl.pallas_call(local_kernel, out_shape=shape((elements, levels, columns),...]
    gather x11 -> x0, local copies, waits for them, and re-layouts: 9.08 us -> none  [the longest x1 2.35 us: on_device(): local_blocks = jnp.take(lifted, jnp.minimum(relative, elements - 1), axis=0)]
    convert_element_type x3 -> x0, local copies, waits for them, and re-layouts: 8.02 us -> none  [the longest x1 3.32 us: on_device(): moved = jnp.einsum('mnke,ekmt->eknt', table, blocks.reshape(shape_four),...]
    ppermute x9 -> x5, waiting for transfers between devices: 16.8 us -> 9.95 us  [the longest x4 9.95 us: ring(): lax.ppermute(array, axis, [(i, (i + by) % peers) for i in range(peers)])]
    reshape x2 -> x0, local copies, waits for them, and re-layouts: 5.87 us -> none  [the longest x1 3.8 us: on_device(): blocks.reshape(shape_four)]
    slice x26 -> x1, local copies, waits for them, and re-layouts: 5.49 us -> 0.01 us  [on_device(): velocity[2:]]
    convert_element_type x5 -> x0, other arithmetic: 4.42 us -> none  [the longest x1 4.08 us: on_device(): lifted = ((1.0 - descent_wide) * tracers.astype(jnp.float32) + descent_wi...]
  transfers between devices with their start and end apart: 9 -> 5, of which waited for: 4 -> 4; matrix products, arithmetic and copies ran while one was open for 26% -> 0% of each run, Pallas kernels for 0% -> 28%
where the time goes in v1:
time: 33.3 us; the launch traced here: 33.1 us
  Pallas kernels  12.4 us (37%)
  waiting for transfers between devices  9.95 us (30%)
  starting transfers between devices  9.47 us (28%)
  local copies, waits for them, and re-layouts  1.24 us (4%)
    ppermute x4, waiting for transfers between devices, ring(): lax.ppermute(array, axis, [(i, (i + by) % peers) for i in range(peers)])  9.95 us
    ppermute x4, starting transfers between devices, ring(): lax.ppermute(array, axis, [(i, (i + by) % peers) for i in range(peers)])  7.11 us
    pallas_call x1, Pallas kernels, on_device(): pl.pallas_call(local_kernel, out_shape=shape((elements, levels, columns),...  5.89 us
    pallas_call x2, Pallas kernels, contributions(): pl.pallas_call(functools.partial(remote_kernel, ahead), out_shape=shape((...  2.62 us
    ppermute x1, starting transfers between devices, on_device(): above = lax.ppermute(lowest, 'lev', [(i, i + 1) for i in range(blocks - 1)])  2.36 us
    pallas_call x1, Pallas kernels, on_device(): pl.pallas_call(combine_kernel, out_shape=shape((elements, levels, columns...  2.32 us
    unnamed x8, local copies, waits for them, and re-layouts  1.24 us
    pallas_call x1, Pallas kernels, on_device(): pl.pallas_call(transpose_kernel, out_shape=(shape((columns, lanes), bf16)...  0.85 us
  transfers between devices with their start and end apart: 5, of which 4 were waited for; matrix products, arithmetic and copies ran while one was open for 0% of the time, Pallas kernels for 28%

profile of v1, /device:TPU:0, one launch (start us, length us, event | category | flops | bytes accessed | tf_op | source)
XLA Modules:
  0.0 33.1 jit_solution(17717781159757368810)
XLA Ops:
  0.0 0.0 copy-start
  0.0 1.2 %copy-done = bf16[128,4,1024]{2,1,0:T(4,128)(2,1)S(1)} copy-done((bf16[128,4,1024]{2,1,0:T(4,128)(2,1)S(1)}, bf16[128,4,1024]{2,1,0:T(4,128)(2,1)}, u32[]{:S(2)}) %copy-start) | copy-done | bytes 1048600
  1.2 0.0 copy-start.1
  1.2 0.0 copy-start.2
  1.2 0.9 %transpose.1 = (bf16[1024,512]{1,0:T(8,128)(2,1)S(1)}, bf16[1024,128]{1,0:T(8,128)(2,1)S(1)}) custom-call(bf16[128,4,1024]{2,1,0:T(4,128)(2,1)S(1)} %copy-done), custom_call_target="tpu_custom_call" | custom-call | tf_op jit(solution)/shard_map/transpose/pallas_call | solution.py:345
  2.1 0.0 copy-start.3
  2.1 2.4 %collective-permute-start = (bf16[1024,128]{1,0:T(8,128)(2,1)S(1)}, bf16[1024,128]{1,0:T(8,128)(2,1)S(1)}, u32[]{:S(2)}, u32[]{:S(2)}) collective-permute-start(bf16[1024,128]{1,0:T(8,128)(2,1)S(1)} %get-tuple-element.10), channel_id=1, source_target_pairs={{0,1},{1,2},{2,3},{4,5},{5,6},{6,7},{8,9},{9,10},{10,11},{12,13},{... | collective-permute-start | bytes 786440 | tf_op jit(solution)/shard_map/ppermute | solution.py:352
  4.5 0.0 copy-done.1
  4.5 0.0 copy-done.2
  4.5 0.0 copy-done.3
  4.5 0.2 pack.1
  4.7 5.5 %collective-permute-start.1 = (f32[64,128]{1,0:T(8,128)S(1)}, f32[64,128]{1,0:T(8,128)S(1)}, u32[]{:S(2)}, u32[]{:S(2)}) collective-permute-start(f32[64,128]{1,0:T(8,128)S(1)} %get-tuple-element.11.own_ref), channel_id=1, source_target_pairs={{0,28},{4,0},{8,4},{12,8},{16,12},{20,16},{24,20},{28,24},{1,29},{... | collective-permute-start | bytes 98312 | tf_op jit(solution)/shard_map/ppermute | solution.py:26
  10.1 0.0 collective-permute-start.3
  10.1 0.0 collective-permute-done.above_ref
  10.1 0.5 %lift.1.lifted_ref = bf16[1024,512]{1,0:T(8,128)(2,1)S(1)} custom-call(bf16[1024,512]{1,0:T(8,128)(2,1)S(1)} %get-tuple-element.9.here_ref, bf16[1024,128]{1,0:T(8,128)(2,1)S(1)} %collective-permute-done.above_ref, f32[1,16,4,128]{3,2,1,0:T(4,128)S(1)} %slice.3.velocity_ref), custom_call_target="tpu_custom_call" | custom-call | tf_op jit(solution)/shard_map/lift/pallas_call | solution.py:353
  10.7 1.1 %collective-permute-done.1.packet_ref = f32[64,128]{1,0:T(8,128)S(1)} collective-permute-done((f32[64,128]{1,0:T(8,128)S(1)}, f32[64,128]{1,0:T(8,128)S(1)}, u32[]{:S(2)}, u32[]{:S(2)}) %collective-permute-start.1) | collective-permute-done | bytes 32800 | tf_op jit(solution)/shard_map/ppermute | solution.py:26
  11.7 1.3 %remote_ahead.1.ahead_ref = bf16[1024,128]{1,0:T(8,128)(2,1)S(1)} custom-call(f32[64,128]{1,0:T(8,128)S(1)} %collective-permute-done.1.packet_ref, f32[64,128]{1,0:T(8,128)S(1)} %get-tuple-element.12.own_ref, bf16[1024,512]{1,0:T(8,128)(2,1)S(1)} %lift.1.lifted_ref), custom_call_target="tpu_custom_call" | custom-call | tf_op jit(solution)/shard_map/remote_ahead/pallas_call | solution.py:358
  13.0 0.2 collective-permute-start.2
  13.3 3.5 %collective-permute-done.3.packet_ref = f32[64,128]{1,0:T(8,128)S(1)} collective-permute-done((f32[64,128]{1,0:T(8,128)S(1)}, f32[64,128]{1,0:T(8,128)S(1)}, u32[]{:S(2)}, u32[]{:S(2)}) %collective-permute-start.3) | collective-permute-done | bytes 32800 | tf_op jit(solution)/shard_map/ppermute | solution.py:26
  16.7 1.3 %remote_back.1.back_ref = bf16[1024,128]{1,0:T(8,128)(2,1)S(1)} custom-call(f32[64,128]{1,0:T(8,128)S(1)} %collective-permute-done.3.packet_ref, f32[64,128]{1,0:T(8,128)S(1)} %get-tuple-element.11.own_ref, bf16[1024,512]{1,0:T(8,128)(2,1)S(1)} %lift.1.lifted_ref), custom_call_target="tpu_custom_call" | custom-call | tf_op jit(solution)/shard_map/remote_back/pallas_call | solution.py:358
  18.1 1.4 %collective-permute-start.4 = (bf16[1024,128]{1,0:T(8,128)(2,1)S(1)}, bf16[1024,128]{1,0:T(8,128)(2,1)S(1)}, u32[]{:S(2)}, u32[]{:S(2)}) collective-permute-start(bf16[1024,128]{1,0:T(8,128)(2,1)S(1)} %remote_back.1.back_ref), channel_id=1, source_target_pairs={{0,28},{4,0},{8,4},{12,8},{16,12},{20,16},{24,20},{28,24},{1,29},{... | collective-permute-start | bytes 786440 | tf_op jit(solution)/shard_map/ppermute | solution.py:26
  19.5 5.9 %local.1.part_ref = bf16[128,4,1024]{2,1,0:T(4,128)(2,1)} custom-call(f32[3,16,4,128]{3,2,1,0:T(4,128)S(1)} %copy-done.1, f32[16,128]{1,0:T(8,128)S(1)} %copy-done.2, s32[1,128]{1,0:T(1,128)S(1)} %bitcast.2, bf16[1024,512]{1,0:T(8,128)(2,1)S(1)} %lift.1.lifted_ref), custom_call_target="tpu_custom_call" | custom-call | tf_op jit(solution)/shard_map/local/pallas_call | solution.py:374
  25.4 0.1 collective-permute-done.2.head_ref
  25.5 5.3 %collective-permute-done.4.tail_ref = bf16[1024,128]{1,0:T(8,128)(2,1)S(1)} collective-permute-done((bf16[1024,128]{1,0:T(8,128)(2,1)S(1)}, bf16[1024,128]{1,0:T(8,128)(2,1)S(1)}, u32[]{:S(2)}, u32[]{:S(2)}) %collective-permute-start.4) | collective-permute-done | bytes 262176 | tf_op jit(solution)/shard_map/ppermute | solution.py:26
  30.8 2.3 %combine.1 = bf16[128,4,1024]{2,1,0:T(4,128)(2,1)} custom-call(bf16[128,4,1024]{2,1,0:T(4,128)(2,1)} %local.1.part_ref, bf16[1024,128]{1,0:T(8,128)(2,1)S(1)} %collective-permute-done.2.head_ref, bf16[1024,128]{1,0:T(8,128)(2,1)S(1)} %collective-permute-done.4.tail_ref, bf16[1024,128]{1,0:T(8,128)(2,1)S(1)} %remote_ahead.1.ahead_ref, ...), custom_call_target="tpu_custom_call", output_to_operand_aliasing={{}: (0, {})} | custom-call | tf_op jit(solution)/shard_map/combine/pallas_call | solution.py:389
  (1 shorter events, 0.0 us)
Async XLA Ops:
  0.0 1.2 %copy-start = (bf16[128,4,1024]{2,1,0:T(4,128)(2,1)S(1)}, bf16[128,4,1024]{2,1,0:T(4,128)(2,1)}, u32[]{:S(2)}) copy-start(bf16[128,4,1024]{2,1,0:T(4,128)(2,1)} %tracers_ref.1) | copy-start | bytes 3145732
  1.2 3.2 %copy-start.1 = (f32[3,16,4,128]{3,2,1,0:T(4,128)S(1)}, f32[3,16,4,128]{3,2,1,0:T(4,128)}, u32[]{:S(2)}) copy-start(f32[3,16,4,128]{3,2,1,0:T(4,128)} %velocity_ref.3) | copy-start | bytes 294916
  1.2 3.3 %copy-start.2 = (f32[16,128]{1,0:T(8,128)S(1)}, f32[16,128]{1,0:T(8,128)}, u32[]{:S(2)}) copy-start(f32[16,128]{1,0:T(8,128)} %mass_ref.3) | copy-start | bytes 24580
  2.1 2.4 %copy-start.3 = (s32[128]{0:T(128)S(1)}, s32[128]{0:T(128)}, u32[]{:S(2)}) copy-start(s32[128]{0:T(128)} %param.7) | copy-start | bytes 1540
  2.1 8.0 %collective-permute-start = (bf16[1024,128]{1,0:T(8,128)(2,1)S(1)}, bf16[1024,128]{1,0:T(8,128)(2,1)S(1)}, u32[]{:S(2)}, u32[]{:S(2)}) collective-permute-start(bf16[1024,128]{1,0:T(8,128)(2,1)S(1)} %get-tuple-element.10), channel_id=1, source_target_pairs={{0,1},{1,2},{2,3},{4,5},{5,6},{6,7},{8,9},{9,10},{10,11},{12,13},{... | collective-permute-start | bytes 786440 | tf_op jit(solution)/shard_map/ppermute | solution.py:352
  4.7 7.1 %collective-permute-start.1 = (f32[64,128]{1,0:T(8,128)S(1)}, f32[64,128]{1,0:T(8,128)S(1)}, u32[]{:S(2)}, u32[]{:S(2)}) collective-permute-start(f32[64,128]{1,0:T(8,128)S(1)} %get-tuple-element.11.own_ref), channel_id=1, source_target_pairs={{0,28},{4,0},{8,4},{12,8},{16,12},{20,16},{24,20},{28,24},{1,29},{... | collective-permute-start | bytes 98312 | tf_op jit(solution)/shard_map/ppermute | solution.py:26
  10.1 6.6 %collective-permute-start.3 = (f32[64,128]{1,0:T(8,128)S(1)}, f32[64,128]{1,0:T(8,128)S(1)}, u32[]{:S(2)}, u32[]{:S(2)}) collective-permute-start(f32[64,128]{1,0:T(8,128)S(1)} %get-tuple-element.12.own_ref), channel_id=1, source_target_pairs={{0,4},{4,8},{8,12},{12,16},{16,20},{20,24},{24,28},{28,0},{1,5},{5... | collective-permute-start | bytes 98312 | tf_op jit(solution)/shard_map/ppermute | solution.py:26
  13.0 12.5 %collective-permute-start.2 = (bf16[1024,128]{1,0:T(8,128)(2,1)S(1)}, bf16[1024,128]{1,0:T(8,128)(2,1)S(1)}, u32[]{:S(2)}, u32[]{:S(2)}) collective-permute-start(bf16[1024,128]{1,0:T(8,128)(2,1)S(1)} %remote_ahead.1.ahead_ref), channel_id=1, source_target_pairs={{0,4},{4,8},{8,12},{12,16},{16,20},{20,24},{24,28},{28,0},{1,5},{5... | collective-permute-start | bytes 786440 | tf_op jit(solution)/shard_map/ppermute | solution.py:26
  18.1 12.7 %collective-permute-start.4 = (bf16[1024,128]{1,0:T(8,128)(2,1)S(1)}, bf16[1024,128]{1,0:T(8,128)(2,1)S(1)}, u32[]{:S(2)}, u32[]{:S(2)}) collective-permute-start(bf16[1024,128]{1,0:T(8,128)(2,1)S(1)} %remote_back.1.back_ref), channel_id=1, source_target_pairs={{0,28},{4,0},{8,4},{12,8},{16,12},{20,16},{24,20},{28,24},{1,29},{... | collective-permute-start | bytes 786440 | tf_op jit(solution)/shard_map/ppermute | solution.py:26

commit v2 on v1

--- a/solution.py
+++ b/solution.py
@@ -19,11 +19,6 @@
 
 def params():
     return pltpu.CompilerParams(vmem_limit_bytes=VMEM_LIMIT)
-
-
-def ring(array, axis, by):
-    peers = lax.axis_size(axis)
-    return lax.ppermute(array, axis, [(i, (i + by) % peers) for i in range(peers)])
 
 
 def interleave(groups, members):
@@ -65,7 +60,17 @@
     return along, across
 
 
-def pack_kernel(velocity_ref, mass_ref, source_ref, head_ref, tail_ref):
+def is_even():
+    return lax.axis_index("elem") % 2 == 0
+
+
+def pack_kernel(velocity_ref, mass_ref, source_ref, pair_ref, cross_ref):
+    even = is_even()
+    pl.when(even)(lambda: pack(velocity_ref, mass_ref, source_ref, cross_ref, pair_ref))
+    pl.when(jnp.logical_not(even))(lambda: pack(velocity_ref, mass_ref, source_ref, pair_ref, cross_ref))
+
+
+def pack(velocity_ref, mass_ref, source_ref, head_ref, tail_ref):
     _, _, levels, elements = velocity_ref.shape
     cap = elements // levels
     runs = lax.axis_size("elem")
@@ -143,7 +148,14 @@
     return total
 
 
-def remote_kernel(ahead, packet_ref, own_ref, lifted_ref, out_ref, blocks_ref, weights_ref, extra_ref):
+def remote_kernel(pair, *refs):
+    even = is_even()
+    ahead = even if pair else jnp.logical_not(even)
+    pl.when(ahead)(lambda: remote(True, *refs))
+    pl.when(jnp.logical_not(ahead))(lambda: remote(False, *refs))
+
+
+def remote(ahead, packet_ref, own_ref, lifted_ref, out_ref, blocks_ref, weights_ref, extra_ref, edge_ref):
     levels = lifted_ref.shape[1] // packet_ref.shape[1]
     lanes_all = packet_ref.shape[1]
     elements = lanes_all
@@ -219,19 +231,31 @@
             own = interpolate(extra_ref, blocks_ref, j, rows, slice(lanes_all, 2 * lanes_all))
             if ahead:
                 west = moved[0] + jnp.where(edge, own, pltpu.roll(moved[3], 1, 1))
-                east = jnp.where(place == cap - 1, moved[3], pltpu.roll(west, lanes_all - 1, 1))
+                values, far = (west, moved[1], moved[2]), moved[3]
             else:
                 east = moved[3] + jnp.where(edge, own, pltpu.roll(moved[0], lanes_all - 1, 1))
-                west = jnp.where(place == 0, moved[0], pltpu.roll(east, 1, 1))
-            for i, value in enumerate((west, moved[1], moved[2], east)):
-                out_ref[pl.ds(t + (4 * j + i) * tracers, CHUNK), :] = value.astype(bf16)
+                values, far = (moved[1], moved[2], east), moved[0]
+            for i, value in enumerate(values):
+                out_ref[pl.ds(t + (3 * j + i) * tracers, CHUNK), :] = value.astype(bf16)
+            edge_ref[pl.ds(t + j * tracers, CHUNK), :] = far.astype(bf16)
         return carry
 
     lax.fori_loop(0, tracers // CHUNK, one, 0)
-
-
-def local_kernel(velocity_ref, mass_ref, source_ref, lifted_ref, out_ref, blocks_ref, weights_ref, wind_ref, moved_ref):
+    row = lax.broadcasted_iota(jnp.int32, (8, lanes_all), 0)
+    far_place = cap - 1 if ahead else 0
+    pick = jnp.where(lane == row * cap + far_place, 1.0, 0.0).astype(bf16)
+    far = lax.dot_general(pick, edge_ref[...], (((1,), (1,)), ((), ())), preferred_element_type=f32)
+    far = [far[:, n : n + lanes_all] for n in range(0, 4 * tracers, lanes_all)]
+    out_ref[12 * tracers :, :] = jnp.concatenate(far, axis=0).astype(bf16)
+
+
+def local_kernel(
+    velocity_ref, mass_ref, source_ref, lifted_ref,
+    out_ref, ends_ref, sides_ref,
+    blocks_ref, weights_ref, wind_ref, moved_ref, inner_ref, sem,
+):
     _, _, levels, elements = velocity_ref.shape
+    cap = elements // levels
     columns = out_ref.shape[2]
     tracers = columns // 16
     start = lax.axis_index("elem") * elements
@@ -274,74 +298,113 @@
             return carry
 
         lax.fori_loop(0, tracers // CHUNK, one, 0)
-    order = interleave(levels, elements)
+    inner = elements - 2 * cap
+    row = lax.broadcasted_iota(jnp.int32, (inner * levels, elements * levels), 0)
+    column = lax.broadcasted_iota(jnp.int32, (inner * levels, elements * levels), 1)
+    same = (row // levels + cap == column % elements) & (row % levels == column // elements)
+    order = jnp.where(same, 1.0, 0.0).astype(bf16)
     step = 256
     for c in range(0, columns, step):
         y = lax.dot_general(
             order, moved_ref[c : c + step, :], (((1,), (1,)), ((), ())), preferred_element_type=f32
         )
-        out_ref[:, :, c : c + step] = y.reshape(elements, levels, step).astype(bf16)
-
-
-def combine_kernel(part_ref, head_ref, tail_ref, ahead_ref, back_ref, out_ref, first_ref, last_ref, sems):
+        inner_ref[:, :, c : c + step] = y.reshape(inner, levels, step).astype(bf16)
+    store = pltpu.make_async_copy(
+        inner_ref.at[pl.ds(1, inner - 2)], out_ref.at[pl.ds(cap + 1, inner - 2)], sem
+    )
+    store.start()
+    sides_ref[0] = inner_ref[0]
+    sides_ref[1] = inner_ref[inner - 1]
+    for n, low in enumerate((0, elements - cap)):
+        ends_ref[n] = jnp.concatenate(
+            [moved_ref[:, k * elements + low : k * elements + low + cap] for k in range(levels)], axis=1
+        )
+    store.wait()
+
+
+def combine_kernel(pair, part_ref, ends_ref, sides_ref, received_ref, sent_ref, out_ref, rows_ref, sem):
+    del part_ref
+    refs = (ends_ref, sides_ref, received_ref, sent_ref, out_ref, rows_ref, sem)
+    even = is_even()
+    head = jnp.logical_not(even) if pair else even
+    pl.when(head)(lambda: combine(True, *refs))
+    pl.when(jnp.logical_not(head))(lambda: combine(False, *refs))
+
+
+def combine(head, ends_ref, sides_ref, received_ref, sent_ref, out_ref, rows_ref, sem):
     elements, levels, columns = out_ref.shape
-    lanes_all = head_ref.shape[1]
+    lanes_all = received_ref.shape[1]
     cap = elements // levels
     tracers = columns // 16
-    span = 4 * tracers
-    spots = ((first_ref, pl.ds(0, cap + 1)), (last_ref, pl.ds(elements - cap - 1, cap + 1)))
-    loads = [pltpu.make_async_copy(out_ref.at[rows], ref, sems.at[n]) for n, (ref, rows) in enumerate(spots)]
-    for load in loads:
-        load.start()
+    end = 0 if head else 1
     place = lax.broadcasted_iota(jnp.int32, (1, lanes_all), 1) % cap
-    column = lax.broadcasted_iota(jnp.int32, (1, columns), 1) % span
     order = interleave(levels, cap)
-    stores = []
-    for n, (ref, rows) in enumerate(spots):
-        received_ref = (head_ref, tail_ref)[n]
-        pieces = []
-        for node in range(16):
-            value = received_ref[node * tracers : (node + 1) * tracers, :]
-            if n == 0 and node % 4 == 0:
-                own = back_ref[(node + 3) * tracers : (node + 4) * tracers, :].astype(f32)
-                own = pltpu.roll(own, lanes_all - (cap - 1), 1)
-                value = (value.astype(f32) + jnp.where(place == 0, own, 0.0)).astype(bf16)
-            if n == 1 and node % 4 == 3:
-                own = ahead_ref[(node - 3) * tracers : (node - 2) * tracers, :].astype(f32)
-                own = pltpu.roll(own, cap - 1, 1)
-                value = (value.astype(f32) + jnp.where(place == cap - 1, own, 0.0)).astype(bf16)
-            pieces.append(value)
-        received = jnp.concatenate(pieces, axis=0)
-        y = lax.dot_general(order, received, (((1,), (1,)), ((), ())), preferred_element_type=f32)
-        y = y.reshape(cap, levels, columns)
-        loads[n].wait()
-        if n == 0:
-            ref[0:cap] = (ref[0:cap].astype(f32) + y).astype(bf16)
-            east = pltpu.roll(y[cap - 1], columns - 3 * tracers, 1)
-            ref[cap] = (ref[cap].astype(f32) + jnp.where(column < tracers, east, 0.0)).astype(bf16)
+
+    def rows(ref, block):
+        return ref[block * tracers : (block + 1) * tracers, :].astype(f32)
+
+    pieces = []
+    for j in range(4):
+        got = [rows(received_ref, 3 * j + i) for i in range(3)]
+        if head:
+            own = pltpu.roll(rows(sent_ref, 3 * j + 2), lanes_all - (cap - 1), 1)
+            west = got[0] + jnp.where(place == 0, own, 0.0)
+            east = jnp.where(place == cap - 1, 0.0, pltpu.roll(got[0], lanes_all - 1, 1))
+            got = [west, got[1], got[2], east]
         else:
-            ref[1 : cap + 1] = (ref[1 : cap + 1].astype(f32) + y).astype(bf16)
-            west = pltpu.roll(y[0], 3 * tracers, 1)
-            ref[0] = (ref[0].astype(f32) + jnp.where(column >= 3 * tracers, west, 0.0)).astype(bf16)
-        store = pltpu.make_async_copy(ref, out_ref.at[rows], sems.at[2 + n])
-        store.start()
-        stores.append(store)
-    for store in stores:
-        store.wait()
+            own = pltpu.roll(rows(sent_ref, 3 * j), cap - 1, 1)
+            east = got[2] + jnp.where(place == cap - 1, own, 0.0)
+            west = jnp.where(place == 0, 0.0, pltpu.roll(got[2], 1, 1))
+            got = [west, got[0], got[1], east]
+        for i, value in enumerate(got):
+            node = 4 * j + i
+            here = ends_ref[end, node * tracers : (node + 1) * tracers, :].astype(f32)
+            pieces.append((here + value).astype(bf16))
+    y = lax.dot_general(
+        order, jnp.concatenate(pieces, axis=0), (((1,), (1,)), ((), ())), preferred_element_type=f32
+    ).reshape(cap, levels, columns)
+    far = received_ref[12 * tracers :, :]
+    far = jnp.concatenate([far[n : n + 8] for n in range(0, far.shape[0], 8)], axis=1)
+    row = lax.broadcasted_iota(jnp.int32, (4 * tracers, columns), 0)
+    column = lax.broadcasted_iota(jnp.int32, (4 * tracers, columns), 1)
+    spread = jnp.where(column == (row // tracers) * 4 * tracers + row % tracers, 1.0, 0.0).astype(bf16)
+    west = jnp.dot(far, spread, preferred_element_type=f32)
+    east = pltpu.roll(west, 3 * tracers, 1)[:levels]
+    west = west[:levels]
+    if head:
+        rows_ref[0 : cap - 1] = y[: cap - 1].astype(bf16)
+        rows_ref[cap - 1] = (y[cap - 1] + east).astype(bf16)
+        rows_ref[cap] = (sides_ref[0].astype(f32) + west).astype(bf16)
+        spot = pl.ds(0, cap + 1)
+    else:
+        rows_ref[2:] = y[1:].astype(bf16)
+        rows_ref[1] = (y[0] + west).astype(bf16)
+        rows_ref[0] = (sides_ref[1].astype(f32) + east).astype(bf16)
+        spot = pl.ds(elements - cap - 1, cap + 1)
+    store = pltpu.make_async_copy(rows_ref, out_ref.at[spot], sem)
+    store.start()
+    store.wait()
 
 
 def on_device(tracers, velocity, node_mass, source):
     elements, levels, columns = tracers.shape
+    cap = elements // 4
+    assert cap * levels == elements
     count = columns // 16
     lanes = levels * elements
+    runs = lax.axis_size("elem")
+    pairing = [(i, i ^ 1) for i in range(runs)]
+    crossing = [(i, (i - 1 if i % 2 == 0 else i + 1) % runs) for i in range(runs)]
     shape = jax.ShapeDtypeStruct
+    vmem = pl.BlockSpec(memory_space=pltpu.VMEM)
+    anywhere = pl.BlockSpec(memory_space=pl.ANY)
     source = source.reshape(1, elements)
     packet = shape((PACKET, elements), f32)
-    head, tail = pl.pallas_call(
+    pair_sent, cross_sent = pl.pallas_call(
         pack_kernel, out_shape=(packet, packet), compiler_params=params(), name="pack"
     )(velocity, node_mass, source)
-    next_head = ring(head, "elem", -1)
-    prev_tail = ring(tail, "elem", 1)
+    cross_packet = lax.ppermute(cross_sent, "elem", crossing)
+    pair_packet = lax.ppermute(pair_sent, "elem", pairing)
     here, lowest = pl.pallas_call(
         transpose_kernel,
         out_shape=(shape((columns, lanes), bf16), shape((columns, elements), bf16)),
@@ -354,52 +417,54 @@
         lift_kernel, out_shape=shape((columns, lanes), bf16), compiler_params=params(), name="lift"
     )(here, above, velocity[2:])
 
-    def contributions(ahead, packet, own):
+    far_rows = 8 * (4 * count // elements)
+
+    def contributions(pair, packet, own):
         return pl.pallas_call(
-            functools.partial(remote_kernel, ahead),
-            out_shape=shape((columns, elements), bf16),
+            functools.partial(remote_kernel, pair),
+            out_shape=shape((12 * count + far_rows, elements), bf16),
             scratch_shapes=[
                 pltpu.VMEM((16, count, 2 * elements), f32),
                 pltpu.VMEM((16, 16, elements), f32),
                 pltpu.VMEM((16, 8, elements), f32),
+                pltpu.VMEM((4 * count, elements), bf16),
             ],
             compiler_params=params(),
-            name="remote_ahead" if ahead else "remote_back",
+            name="remote_pair" if pair else "remote_cross",
         )(packet, own, lifted)
 
-    ahead = contributions(True, next_head, tail)
-    back = contributions(False, prev_tail, head)
-    from_prev = ring(ahead, "elem", 1)
-    from_next = ring(back, "elem", -1)
-    part = pl.pallas_call(
+    cross_out = contributions(False, cross_packet, cross_sent)
+    cross_in = lax.ppermute(cross_out, "elem", crossing)
+    pair_out = contributions(True, pair_packet, pair_sent)
+    pair_in = lax.ppermute(pair_out, "elem", pairing)
+    result = shape((elements, levels, columns), bf16)
+    part, ends, sides = pl.pallas_call(
         local_kernel,
-        out_shape=shape((elements, levels, columns), bf16),
+        out_shape=(result, shape((2, columns, elements), bf16), shape((2, levels, columns), bf16)),
+        out_specs=(anywhere, vmem, vmem),
         scratch_shapes=[
             pltpu.VMEM((16, count, elements), f32),
             pltpu.VMEM((16, 16, elements), f32),
             pltpu.VMEM((2, 16, elements), f32),
             pltpu.VMEM((columns, lanes), bf16),
+            pltpu.VMEM((elements - 2 * cap, levels, columns), bf16),
+            pltpu.SemaphoreType.DMA,
         ],
         compiler_params=params(),
         name="local",
     )(velocity, node_mass, source, lifted)
-    cap = elements // levels
-    vmem = pl.BlockSpec(memory_space=pltpu.VMEM)
-    anywhere = pl.BlockSpec(memory_space=pl.ANY)
-    return pl.pallas_call(
-        combine_kernel,
-        out_shape=shape((elements, levels, columns), bf16),
-        in_specs=[anywhere, vmem, vmem, vmem, vmem],
-        out_specs=anywhere,
-        scratch_shapes=[
-            pltpu.VMEM((cap + 1, levels, columns), bf16),
-            pltpu.VMEM((cap + 1, levels, columns), bf16),
-            pltpu.SemaphoreType.DMA((4,)),
-        ],
-        input_output_aliases={0: 0},
-        compiler_params=params(),
-        name="combine",
-    )(part, from_prev, from_next, ahead, back)
+    for pair, received, sent in ((True, pair_in, pair_out), (False, cross_in, cross_out)):
+        part = pl.pallas_call(
+            functools.partial(combine_kernel, pair),
+            out_shape=result,
+            in_specs=[anywhere, vmem, vmem, vmem, vmem],
+            out_specs=anywhere,
+            scratch_shapes=[pltpu.VMEM((cap + 1, levels, columns), bf16), pltpu.SemaphoreType.DMA],
+            input_output_aliases={0: 0},
+            compiler_params=params(),
+            name="combine_pair" if pair else "combine_cross",
+        )(part, ends, sides, received, sent)
+    return part
 
 
 def solution(mesh):

time: 33.3 us -> 27 us (0.81)
  waiting for transfers between devices: 9.95 us -> 1.11 us
  starting transfers between devices: 9.47 us -> 11.9 us
    ppermute x4, waiting for transfers between devices: 9.95 us -> 1.11 us  [the longest x1 1.1 us: on_device(): cross_packet = lax.ppermute(cross_sent, 'elem', crossing)]
    ppermute x4, starting transfers between devices: 7.11 us -> 9.51 us  [the longest x1 3.55 us: on_device(): cross_in = lax.ppermute(cross_out, 'elem', crossing)]
    pallas_call x4 -> x5, Pallas kernels: 10.8 us -> 10.9 us  [the longest x1 5.54 us: on_device(): pl.pallas_call(local_kernel, out_shape=(result, shape((2, columns, elemen...]
  transfers between devices with their start and end apart: 5 -> 5, of which waited for: 4 -> 1; matrix products, arithmetic and copies ran while one was open for 0% -> 0% of each run, Pallas kernels for 28% -> 39%
where the time goes in v2:
time: 27 us; the launch traced here: 26.8 us
  Pallas kernels  12.5 us (46%)
  starting transfers between devices  11.9 us (44%)
  local copies, waits for them, and re-layouts  1.24 us (5%)
  waiting for transfers between devices  1.11 us (4%)
    pallas_call x1, Pallas kernels, on_device(): pl.pallas_call(local_kernel, out_shape=(result, shape((2, columns, elemen...  5.54 us
    ppermute x1, starting transfers between devices, on_device(): cross_in = lax.ppermute(cross_out, 'elem', crossing)  3.55 us
    ppermute x1, starting transfers between devices, on_device(): cross_packet = lax.ppermute(cross_sent, 'elem', crossing)  3.54 us
    pallas_call x2, Pallas kernels, contributions(): pl.pallas_call(functools.partial(remote_kernel, pair), out_shape=shape((1...  2.81 us
    pallas_call x2, Pallas kernels, on_device(): pl.pallas_call(functools.partial(combine_kernel, pair), out_shape=result,...  2.55 us
    ppermute x1, starting transfers between devices, on_device(): pair_packet = lax.ppermute(pair_sent, 'elem', pairing)  2.42 us
    ppermute x1, starting transfers between devices, on_device(): above = lax.ppermute(lowest, 'lev', [(i, i + 1) for i in range(blocks - 1)])  2.36 us
    unnamed x8, local copies, waits for them, and re-layouts  1.24 us
  transfers between devices with their start and end apart: 5, of which 1 were waited for; matrix products, arithmetic and copies ran while one was open for 0% of the time, Pallas kernels for 39%

profile of v2, /device:TPU:0, one launch (start us, length us, event | category | flops | bytes accessed | tf_op | source)
XLA Modules:
  0.0 26.8 jit_solution(13075801540668382667)
XLA Ops:
  0.0 0.0 copy-start
  0.0 1.2 %copy-done = bf16[128,4,1024]{2,1,0:T(4,128)(2,1)S(1)} copy-done((bf16[128,4,1024]{2,1,0:T(4,128)(2,1)S(1)}, bf16[128,4,1024]{2,1,0:T(4,128)(2,1)}, u32[]{:S(2)}) %copy-start) | copy-done | bytes 1048600
  1.2 0.0 copy-start.1
  1.2 0.0 copy-start.2
  1.2 0.9 %transpose.1 = (bf16[1024,512]{1,0:T(8,128)(2,1)S(1)}, bf16[1024,128]{1,0:T(8,128)(2,1)S(1)}) custom-call(bf16[128,4,1024]{2,1,0:T(4,128)(2,1)S(1)} %copy-done), custom_call_target="tpu_custom_call" | custom-call | tf_op jit(solution)/shard_map/transpose/pallas_call | solution.py:408
  2.1 0.0 copy-start.3
  2.1 2.4 %collective-permute-start = (bf16[1024,128]{1,0:T(8,128)(2,1)S(1)}, bf16[1024,128]{1,0:T(8,128)(2,1)S(1)}, u32[]{:S(2)}, u32[]{:S(2)}) collective-permute-start(bf16[1024,128]{1,0:T(8,128)(2,1)S(1)} %get-tuple-element.13), channel_id=1, source_target_pairs={{0,1},{1,2},{2,3},{4,5},{5,6},{6,7},{8,9},{9,10},{10,11},{12,13},{... | collective-permute-start | bytes 786440 | tf_op jit(solution)/shard_map/ppermute | solution.py:415
  4.5 0.0 copy-done.1
  4.5 0.0 copy-done.2
  4.5 0.0 copy-done.3
  4.5 0.2 pack.1
  4.7 2.4 %collective-permute-start.1 = (f32[64,128]{1,0:T(8,128)S(1)}, f32[64,128]{1,0:T(8,128)S(1)}, u32[]{:S(2)}, u32[]{:S(2)}) collective-permute-start(f32[64,128]{1,0:T(8,128)S(1)} %get-tuple-element.17.refs_1_), channel_id=1, source_target_pairs={{0,4},{4,0},{8,12},{12,8},{16,20},{20,16},{24,28},{28,24},{1,5},{5... | collective-permute-start | bytes 98312 | tf_op jit(solution)/shard_map/ppermute | solution.py:407
  7.1 3.5 %collective-permute-start.3 = (f32[64,128]{1,0:T(8,128)S(1)}, f32[64,128]{1,0:T(8,128)S(1)}, u32[]{:S(2)}, u32[]{:S(2)}) collective-permute-start(f32[64,128]{1,0:T(8,128)S(1)} %get-tuple-element.18.refs_1_), channel_id=1, source_target_pairs={{0,28},{4,8},{8,4},{12,16},{16,12},{20,24},{24,20},{28,0},{1,29},{... | collective-permute-start | bytes 98312 | tf_op jit(solution)/shard_map/ppermute | solution.py:406
  10.7 0.0 collective-permute-done.above_ref
  10.7 0.5 %lift.1.lifted_ref.refs_2_ = bf16[1024,512]{1,0:T(8,128)(2,1)S(1)} custom-call(bf16[1024,512]{1,0:T(8,128)(2,1)S(1)} %get-tuple-element.12.here_ref, bf16[1024,128]{1,0:T(8,128)(2,1)S(1)} %collective-permute-done.above_ref, f32[1,16,4,128]{3,2,1,0:T(4,128)S(1)} %slice.3.velocity_ref), custom_call_target="tpu_custom_call" | custom-call | tf_op jit(solution)/shard_map/lift/pallas_call | solution.py:416
  11.2 0.0 collective-permute-done.1.refs_0_
  11.2 1.4 %remote_pair.1.sent_ref = bf16[784,128]{1,0:T(8,128)(2,1)S(1)} custom-call(f32[64,128]{1,0:T(8,128)S(1)} %collective-permute-done.1.refs_0_, f32[64,128]{1,0:T(8,128)S(1)} %get-tuple-element.17.refs_1_, bf16[1024,512]{1,0:T(8,128)(2,1)S(1)} %lift.1.lifted_ref.refs_2_), custom_call_target="tpu_custom_call" | custom-call | tf_op jit(solution)/shard_map/remote_pair/pallas_call | solution.py:423
  12.6 0.0 collective-permute-start.2
  12.6 1.1 %collective-permute-done.3.refs_0_ = f32[64,128]{1,0:T(8,128)S(1)} collective-permute-done((f32[64,128]{1,0:T(8,128)S(1)}, f32[64,128]{1,0:T(8,128)S(1)}, u32[]{:S(2)}, u32[]{:S(2)}) %collective-permute-start.3) | collective-permute-done | bytes 32800 | tf_op jit(solution)/shard_map/ppermute | solution.py:406
  13.7 1.4 %remote_cross.1.sent_ref = bf16[784,128]{1,0:T(8,128)(2,1)S(1)} custom-call(f32[64,128]{1,0:T(8,128)S(1)} %collective-permute-done.3.refs_0_, f32[64,128]{1,0:T(8,128)S(1)} %get-tuple-element.18.refs_1_, bf16[1024,512]{1,0:T(8,128)(2,1)S(1)} %lift.1.lifted_ref.refs_2_), custom_call_target="tpu_custom_call" | custom-call | tf_op jit(solution)/shard_map/remote_cross/pallas_call | solution.py:423
  15.1 3.6 %collective-permute-start.4 = (bf16[784,128]{1,0:T(8,128)(2,1)S(1)}, bf16[784,128]{1,0:T(8,128)(2,1)S(1)}, u32[]{:S(2)}, u32[]{:S(2)}) collective-permute-start(bf16[784,128]{1,0:T(8,128)(2,1)S(1)} %remote_cross.1.sent_ref), channel_id=1, source_target_pairs={{0,28},{4,8},{8,4},{12,16},{16,12},{20,24},{24,20},{28,0},{1,29},{... | collective-permute-start | bytes 602120 | tf_op jit(solution)/shard_map/ppermute | solution.py:437
  18.7 5.5 %local.1 = (bf16[128,4,1024]{2,1,0:T(4,128)(2,1)}, bf16[2,1024,128]{2,1,0:T(8,128)(2,1)S(1)}, bf16[2,4,1024]{2,1,0:T(4,128)(2,1)S(1)}) custom-call(f32[3,16,4,128]{3,2,1,0:T(4,128)S(1)} %copy-done.1, f32[16,128]{1,0:T(8,128)S(1)} %copy-done.2, s32[1,128]{1,0:T(1,128)S(1)} %bitcast.2, bf16[1024,512]{1,0:T(8,128)(2,1)S(1)} %lift.1.lifted_ref.refs_2_), custom_call_target="tpu_custom_call" | custom-call | tf_op jit(solution)/shard_map/local/pallas_call | solution.py:441
  24.2 0.0 collective-permute-done.2.received_ref
  24.3 1.3 %combine_pair.1.part_ref = bf16[128,4,1024]{2,1,0:T(4,128)(2,1)} custom-call(bf16[128,4,1024]{2,1,0:T(4,128)(2,1)} %get-tuple-element.14.part_ref, bf16[2,1024,128]{2,1,0:T(8,128)(2,1)S(1)} %get-tuple-element.15.ends_ref, bf16[2,4,1024]{2,1,0:T(4,128)(2,1)S(1)} %get-tuple-element.16.sides_ref, ...), custom_call_target="tpu_custom_call", output_to_operand_aliasing={{}: (0, {})} | custom-call | tf_op jit(solution)/shard_map/combine_pair/pallas_call | solution.py:457
  25.5 0.0 collective-permute-done.4.received_ref
  25.6 1.3 %combine_cross.1 = bf16[128,4,1024]{2,1,0:T(4,128)(2,1)} custom-call(bf16[128,4,1024]{2,1,0:T(4,128)(2,1)} %combine_pair.1.part_ref, bf16[2,1024,128]{2,1,0:T(8,128)(2,1)S(1)} %get-tuple-element.15.ends_ref, bf16[2,4,1024]{2,1,0:T(4,128)(2,1)S(1)} %get-tuple-element.16.sides_ref, ...), custom_call_target="tpu_custom_call", output_to_operand_aliasing={{}: (0, {})} | custom-call | tf_op jit(solution)/shard_map/combine_cross/pallas_call | solution.py:457
  (1 shorter events, 0.0 us)
Async XLA Ops:
  0.0 1.2 %copy-start = (bf16[128,4,1024]{2,1,0:T(4,128)(2,1)S(1)}, bf16[128,4,1024]{2,1,0:T(4,128)(2,1)}, u32[]{:S(2)}) copy-start(bf16[128,4,1024]{2,1,0:T(4,128)(2,1)} %tracers_ref.1) | copy-start | bytes 3145732
  1.2 3.2 %copy-start.1 = (f32[3,16,4,128]{3,2,1,0:T(4,128)S(1)}, f32[3,16,4,128]{3,2,1,0:T(4,128)}, u32[]{:S(2)}) copy-start(f32[3,16,4,128]{3,2,1,0:T(4,128)} %velocity_ref.3) | copy-start | bytes 294916
  1.2 3.3 %copy-start.2 = (f32[16,128]{1,0:T(8,128)S(1)}, f32[16,128]{1,0:T(8,128)}, u32[]{:S(2)}) copy-start(f32[16,128]{1,0:T(8,128)} %mass_ref.3) | copy-start | bytes 24580
  2.1 2.4 %copy-start.3 = (s32[128]{0:T(128)S(1)}, s32[128]{0:T(128)}, u32[]{:S(2)}) copy-start(s32[128]{0:T(128)} %param.7) | copy-start | bytes 1540
  2.1 8.6 %collective-permute-start = (bf16[1024,128]{1,0:T(8,128)(2,1)S(1)}, bf16[1024,128]{1,0:T(8,128)(2,1)S(1)}, u32[]{:S(2)}, u32[]{:S(2)}) collective-permute-start(bf16[1024,128]{1,0:T(8,128)(2,1)S(1)} %get-tuple-element.13), channel_id=1, source_target_pairs={{0,1},{1,2},{2,3},{4,5},{5,6},{6,7},{8,9},{9,10},{10,11},{12,13},{... | collective-permute-start | bytes 786440 | tf_op jit(solution)/shard_map/ppermute | solution.py:415
  4.7 6.5 %collective-permute-start.1 = (f32[64,128]{1,0:T(8,128)S(1)}, f32[64,128]{1,0:T(8,128)S(1)}, u32[]{:S(2)}, u32[]{:S(2)}) collective-permute-start(f32[64,128]{1,0:T(8,128)S(1)} %get-tuple-element.17.refs_1_), channel_id=1, source_target_pairs={{0,4},{4,0},{8,12},{12,8},{16,20},{20,16},{24,28},{28,24},{1,5},{5... | collective-permute-start | bytes 98312 | tf_op jit(solution)/shard_map/ppermute | solution.py:407
  7.1 6.6 %collective-permute-start.3 = (f32[64,128]{1,0:T(8,128)S(1)}, f32[64,128]{1,0:T(8,128)S(1)}, u32[]{:S(2)}, u32[]{:S(2)}) collective-permute-start(f32[64,128]{1,0:T(8,128)S(1)} %get-tuple-element.18.refs_1_), channel_id=1, source_target_pairs={{0,28},{4,8},{8,4},{12,16},{16,12},{20,24},{24,20},{28,0},{1,29},{... | collective-permute-start | bytes 98312 | tf_op jit(solution)/shard_map/ppermute | solution.py:406
  12.6 11.6 %collective-permute-start.2 = (bf16[784,128]{1,0:T(8,128)(2,1)S(1)}, bf16[784,128]{1,0:T(8,128)(2,1)S(1)}, u32[]{:S(2)}, u32[]{:S(2)}) collective-permute-start(bf16[784,128]{1,0:T(8,128)(2,1)S(1)} %remote_pair.1.sent_ref), channel_id=1, source_target_pairs={{0,4},{4,0},{8,12},{12,8},{16,20},{20,16},{24,28},{28,24},{1,5},{5... | collective-permute-start | bytes 602120 | tf_op jit(solution)/shard_map/ppermute | solution.py:439
  15.1 10.4 %collective-permute-start.4 = (bf16[784,128]{1,0:T(8,128)(2,1)S(1)}, bf16[784,128]{1,0:T(8,128)(2,1)S(1)}, u32[]{:S(2)}, u32[]{:S(2)}) collective-permute-start(bf16[784,128]{1,0:T(8,128)(2,1)S(1)} %remote_cross.1.sent_ref), channel_id=1, source_target_pairs={{0,28},{4,8},{8,4},{12,16},{16,12},{20,24},{24,20},{28,0},{1,29},{... | collective-permute-start | bytes 602120 | tf_op jit(solution)/shard_map/ppermute | solution.py:437

commit v3 on v2

v3 whole, which is shorter than its diff:
```python
import functools

import jax
import jax.numpy as jnp
from jax import lax
from jax.experimental import pallas as pl
from jax.experimental.pallas import tpu as pltpu
from jax.sharding import PartitionSpec as P

gll_points = (-1.0, -0.4472135954999579, 0.4472135954999579, 1.0)
courant = 0.15
f32 = jnp.float32
bf16 = jnp.bfloat16
VMEM_LIMIT = 40 << 20
CHUNK = 16

MASS, NEAR, NEAR_MASS, SOURCE, PACKET = 32, 48, 56, 60, 64


def params():
    return pltpu.CompilerParams(vmem_limit_bytes=VMEM_LIMIT)


def cost(work):
    return pl.CostEstimate(flops=100 * work, bytes_accessed=work, transcendentals=0)


def interleave(groups, members):
    size = groups * members
    row = lax.broadcasted_iota(jnp.int32, (size, size), 0)
    column = lax.broadcasted_iota(jnp.int32, (size, size), 1)
    same = (row // groups == column % members) & (row % groups == column // members)
    return jnp.where(same, 1.0, 0.0).astype(bf16)


def basis(position):
    out = []
    for a in range(4):
        scale = 1.0
        factor = None
        for other in range(4):
            if other != a:
                scale /= gll_points[a] - gll_points[other]
                term = position - gll_points[other]
                factor = term if factor is None else factor * term
        out.append(factor * scale)
    return out


def node_rows(rows, lanes, of_i):
    row = lax.broadcasted_iota(jnp.int32, (rows, lanes), 0)
    index = row // 4 if of_i else row % 4
    out = jnp.full((rows, lanes), gll_points[0], f32)
    for a in range(1, 4):
        out = jnp.where(index == a, gll_points[a], out)
    return out


def table(winds, coefficient):
    rows, lanes = winds[0].shape
    along = basis(node_rows(rows, lanes, True) - courant * winds[0])
    across_position = node_rows(rows, lanes, False) - courant * winds[1]
    across = [factor * coefficient for factor in basis(across_position)]
    return along, across


def is_even():
    return lax.axis_index("elem") % 2 == 0


def prepare_kernel(
    tracers_hbm, velocity_hbm, mass_hbm, source_hbm,
    here_ref, lowest_ref, cross_ref, pair_ref, velocity_ref, mass_ref, source_ref,
    tracers_ref, sems,
):
    elements, levels, columns = tracers_hbm.shape
    step = 256
    copies = [
        pltpu.make_async_copy(here, there, sems.at[n])
        for n, (here, there) in enumerate(
            ((velocity_hbm, velocity_ref), (mass_hbm, mass_ref), (source_hbm, source_ref))
        )
    ]
    copies.append(pltpu.make_async_copy(tracers_hbm, tracers_ref, sems.at[3]))
    for copy in copies:
        copy.start()
    for copy in copies[:3]:
        copy.wait()
    even = is_even()
    refs = (velocity_ref, mass_ref, source_ref)

    def both(head_ref, tail_ref):
        pack(True, *refs, head_ref)
        pack(False, *refs, tail_ref)

    pl.when(even)(lambda: both(cross_ref, pair_ref))
    pl.when(jnp.logical_not(even))(lambda: both(pair_ref, cross_ref))
    order = interleave(levels, elements)
    copies[3].wait()
    x = tracers_ref[...].reshape(elements * levels, columns)
    for n in range(0, columns, step):
        y = lax.dot_general(
            x[:, n : n + step], order, (((0,), (0,)), ((), ())), preferred_element_type=f32
        ).astype(bf16)
        here_ref[n : n + step, :] = y
        lowest_ref[n : n + step, :] = y[:, (levels - 1) * elements :]


def pack(head, velocity_ref, mass_ref, source_ref, out_ref):
    _, _, levels, elements = velocity_ref.shape
    cap = elements // levels
    runs = lax.axis_size("elem")
    start = lax.axis_index("elem") * elements
    total = runs * elements
    low, nodes, step = (0, 0, 1) if head else (elements - cap, 3, -1)

    def lanes(pieces, shift=0):
        return jnp.concatenate([x[:, low + shift : low + shift + cap] for x in pieces], axis=1)

    for c in range(2):
        pieces = [velocity_ref[c, :, k, :] for k in range(levels)]
        out_ref[16 * c : 16 * c + 16, :] = lanes(pieces)
        near = lanes(pieces, step)
        for j in range(4):
            out_ref[NEAR + 4 * c + j : NEAR + 4 * c + j + 1, :] = near[4 * j + nodes : 4 * j + nodes + 1]
    mass = mass_ref[...]
    out_ref[MASS : MASS + 16, :] = lanes([mass] * levels)
    near = lanes([mass] * levels, step)
    for j in range(4):
        out_ref[NEAR_MASS + j : NEAR_MASS + j + 1, :] = near[4 * j + nodes : 4 * j + nodes + 1]
    relative = source_ref[...] - start + step * elements
    relative = jnp.where(relative < 0, relative + total, relative)
    relative = jnp.where(relative < 0, relative + total, relative)
    relative = jnp.where(relative >= total, relative - total, relative)
    out_ref[SOURCE : SOURCE + 1, :] = lanes([relative.astype(f32)] * levels)
    out_ref[SOURCE + 1 :, :] = jnp.zeros((PACKET - SOURCE - 1, elements), f32)


def lift_kernel(here_ref, above_ref, velocity_ref, out_ref):
    _, nodes, levels, elements = velocity_ref.shape
    tracers = here_ref.shape[0] // nodes
    below_top = lax.axis_index("lev") > 0
    for k in range(levels):
        descent = 1.0 / (1.0 + jnp.exp(-velocity_ref[2, :, k, :]))
        lanes = slice(k * elements, (k + 1) * elements)
        for m in range(nodes):
            rows = slice(m * tracers, (m + 1) * tracers)
            here = here_ref[rows, lanes].astype(f32)
            if k == 0:
                upper = jnp.where(below_top, above_ref[rows, :].astype(f32), 0.0)
            else:
                upper = here_ref[rows, (k - 1) * elements : k * elements].astype(f32)
            d = descent[m : m + 1]
            out_ref[m, :, lanes] = ((1.0 - d) * here + d * upper).astype(bf16)


def by_i(ref, first, nodes=16):
    return [ref[pl.ds(first + i, 4, stride=4), :] for i in range(4)]


def shared(mass_left, left, mass_right, right):
    return (mass_left * left + mass_right * right) / (mass_left + mass_right)


def interpolate(weights_ref, blocks_ref, node, rows, lanes, *slot):
    total = None
    for m in range(16):
        term = weights_ref[m, node : node + 1, :] * blocks_ref[(*slot, m, rows, lanes)]
        total = term if total is None else total + term
    return total


def fetch(lifted_ref, t, lanes, chosen):
    x = lifted_ref[:, pl.ds(t, CHUNK), lanes].reshape(16 * CHUNK, chosen.shape[0])
    y = jnp.dot(x, chosen, preferred_element_type=f32)
    return y.reshape(16, CHUNK, chosen.shape[1])


def by_side(pair, body, *args):
    even = is_even()
    ahead = even if pair else jnp.logical_not(even)
    pl.when(ahead)(lambda: body(True, *args))
    pl.when(jnp.logical_not(ahead))(lambda: body(False, *args))


def weigh_kernel(pair, levels, after_ref, packet_ref, own_ref, weights_ref, extra_ref, chosen_ref):
    del after_ref
    by_side(pair, weigh, levels, packet_ref, own_ref, weights_ref, extra_ref, chosen_ref)


def remote_kernel(pair, after_ref, *refs):
    del after_ref
    by_side(pair, remote, *refs)


def weigh(ahead, levels, packet_ref, own_ref, weights_ref, extra_ref, chosen_ref):
    lanes_all = packet_ref.shape[1]
    elements = lanes_all
    cap = elements // levels
    total = lax.axis_size("elem") * elements
    lane = lax.broadcasted_iota(jnp.int32, (1, lanes_all), 1)
    level, place = lane // cap, lane % cap
    edge = place == (0 if ahead else cap - 1)

    def beside(values, own):
        if ahead:
            return jnp.where(edge, pltpu.roll(own, lanes_all - (cap - 1), 1), pltpu.roll(values, 1, 1))
        return jnp.where(edge, pltpu.roll(own, cap - 1, 1), pltpu.roll(values, lanes_all - 1, 1))

    mass = by_i(packet_ref, MASS)
    own_mass = by_i(own_ref, MASS)
    near_mass = packet_ref[NEAR_MASS : NEAR_MASS + 4, :]
    if ahead:
        mass_before, mass_after = beside(mass[3], own_mass[3]), near_mass
    else:
        mass_before, mass_after = near_mass, beside(mass[0], own_mass[0])
    share_west = mass[0] / (mass_before + mass[0])
    share_east = mass[3] / (mass[3] + mass_after)
    winds = []
    edge_winds = []
    for c in range(2):
        wind = by_i(packet_ref, 16 * c)
        own = by_i(own_ref, 16 * c)
        near = packet_ref[NEAR + 4 * c : NEAR + 4 * c + 4, :]
        if ahead:
            before, after = beside(wind[3], own[3]), near
        else:
            before, after = near, beside(wind[0], own[0])
        west = shared(mass_before, before, mass[0], wind[0])
        east = shared(mass[3], wind[3], mass_after, after)
        winds.append(jnp.concatenate([west, wind[1], wind[2], east], axis=0))
        edge_winds.append(west if ahead else east)
    ones = jnp.ones((8, lanes_all), f32)
    along, across = table(winds, jnp.concatenate([share_west, ones, share_east], axis=0))
    for b in range(4):
        for a in range(4):
            weights_ref[4 * b + a] = along[a] * across[b]
    edge_share = 1.0 - (share_west if ahead else share_east)
    extra_along = basis(gll_points[3 if ahead else 0] - courant * edge_winds[0])
    across_position = node_rows(4, lanes_all, False) - courant * edge_winds[1]
    extra_across = [factor * edge_share for factor in basis(across_position)]
    for b in range(4):
        for a in range(4):
            extra_ref[4 * b + a, 0:4] = extra_along[a] * extra_across[b]

    source = packet_ref[SOURCE : SOURCE + 1, :].astype(jnp.int32)
    own_source = own_ref[SOURCE : SOURCE + 1, :].astype(jnp.int32) + (elements if ahead else -elements)
    own_source = jnp.where(own_source >= total, own_source - total, own_source)
    own_source = jnp.where(own_source < 0, own_source + total, own_source)
    own_source = pltpu.roll(own_source, lanes_all - (cap - 1) if ahead else cap - 1, 1)
    row = lax.broadcasted_iota(jnp.int32, (levels * elements, lanes_all), 0)
    same = row // elements == level
    first = jnp.where(same & (row % elements == source), 1.0, 0.0).astype(bf16)
    second = jnp.where(same & edge & (row % elements == own_source), 1.0, 0.0).astype(bf16)
    chosen_ref[...] = jnp.concatenate([first, second], axis=1)


def remote(ahead, lifted_ref, weights_ref, extra_ref, chosen_ref, out_ref, blocks_ref, edge_ref):
    lanes_all = out_ref.shape[1]
    levels = lifted_ref.shape[2] // lanes_all
    cap = lanes_all // levels
    tracers = lifted_ref.shape[1]
    lane = lax.broadcasted_iota(jnp.int32, (1, lanes_all), 1)
    place = lane % cap
    edge = place == (0 if ahead else cap - 1)
    chosen = chosen_ref[...]
    for m in range(0, 16, 4):
        x = lifted_ref[m : m + 4].reshape(4 * tracers, levels * lanes_all)
        y = jnp.dot(x, chosen, preferred_element_type=f32)
        blocks_ref[m : m + 4] = y.reshape(4, tracers, 2 * lanes_all)

    def one(index, carry):
        t = pl.multiple_of(index * CHUNK, CHUNK)
        rows = pl.ds(t, CHUNK)
        lanes = slice(0, lanes_all)
        for j in range(4):
            moved = [interpolate(weights_ref, blocks_ref, 4 * i + j, rows, lanes) for i in range(4)]
            own = interpolate(extra_ref, blocks_ref, j, rows, slice(lanes_all, 2 * lanes_all))
            if ahead:
                west = moved[0] + jnp.where(edge, own, pltpu.roll(moved[3], 1, 1))
                values, far = (west, moved[1], moved[2]), moved[3]
            else:
                east = moved[3] + jnp.where(edge, own, pltpu.roll(moved[0], lanes_all - 1, 1))
                values, far = (moved[1], moved[2], east), moved[0]
            for i, value in enumerate(values):
                out_ref[pl.ds(t + (3 * j + i) * tracers, CHUNK), :] = value.astype(bf16)
            edge_ref[pl.ds(t + j * tracers, CHUNK), :] = far.astype(bf16)
        return carry

    lax.fori_loop(0, tracers // CHUNK, one, 0)
    row = lax.broadcasted_iota(jnp.int32, (8, lanes_all), 0)
    far_place = cap - 1 if ahead else 0
    pick = jnp.where(lane == row * cap + far_place, 1.0, 0.0).astype(bf16)
    far = lax.dot_general(pick, edge_ref[...], (((1,), (1,)), ((), ())), preferred_element_type=f32)
    far = [far[:, n : n + lanes_all] for n in range(0, 4 * tracers, lanes_all)]
    out_ref[12 * tracers :, :] = jnp.concatenate(far, axis=0).astype(bf16)


def local_kernel(
    velocity_ref, mass_ref, source_ref, lifted_ref, after_ref,
    out_ref, ends_ref, sides_ref,
    blocks_ref, weights_ref, wind_ref, moved_ref, inner_ref, sems,
):
    del after_ref
    _, _, levels, elements = velocity_ref.shape
    cap = elements // levels
    columns = out_ref.shape[2]
    tracers = columns // 16
    start = lax.axis_index("elem") * elements
    lane = lax.broadcasted_iota(jnp.int32, (1, elements), 1)
    mass = by_i(mass_ref, 0)
    mass_before = pltpu.roll(mass[3], 1, 1)
    mass_after = pltpu.roll(mass[0], elements - 1, 1)
    share_west = mass[0] / (mass_before + mass[0])
    share_east = mass[3] / (mass[3] + mass_after)
    coefficient = jnp.concatenate([share_west, jnp.ones((8, elements), f32), share_east], axis=0)
    row = lax.broadcasted_iota(jnp.int32, (elements, elements), 0)
    chosen = jnp.where(row == source_ref[...] - start, 1.0, 0.0).astype(bf16)
    blocks_ref[0] = fetch(lifted_ref, 0, slice(0, elements), chosen)
    for k in range(levels):
        winds = []
        for c in range(2):
            wind_ref[c] = velocity_ref[c, :, k, :]
            wind = [wind_ref[c, pl.ds(i, 4, stride=4), :] for i in range(4)]
            west = shared(mass_before, pltpu.roll(wind[3], 1, 1), mass[0], wind[0])
            east = shared(mass[3], wind[3], mass_after, pltpu.roll(wind[0], elements - 1, 1))
            winds.append(jnp.concatenate([west, wind[1], wind[2], east], axis=0))
        along, across = table(winds, coefficient)
        for b in range(4):
            for a in range(4):
                weights_ref[4 * b + a] = along[a] * across[b]
        lanes = slice(k * elements, (k + 1) * elements)

        def one(t, slot, later, later_lanes):
            blocks_ref[1 - slot] = fetch(lifted_ref, later, later_lanes, chosen)
            for j in range(4):
                moved = [
                    interpolate(weights_ref, blocks_ref, 4 * i + j, slice(None), slice(0, elements), slot)
                    for i in range(4)
                ]
                west = jnp.where(lane == 0, 0.0, moved[0] + pltpu.roll(moved[3], 1, 1))
                east = pltpu.roll(west, elements - 1, 1)
                for i, value in enumerate((west, moved[1], moved[2], east)):
                    moved_ref[pl.ds(t + (4 * j + i) * tracers, CHUNK), lanes] = value.astype(bf16)

        def two(index, carry):
            t = pl.multiple_of(index * (2 * CHUNK), 2 * CHUNK)
            later = t + 2 * CHUNK
            over = later >= tracers
            level = jnp.where(over, min(k + 1, levels - 1), k)
            later_lanes = pl.ds(pl.multiple_of(level * elements, elements), elements)
            one(t, 0, t + CHUNK, lanes)
            one(t + CHUNK, 1, pl.multiple_of(jnp.where(over, 0, later), CHUNK), later_lanes)
            return carry

        lax.fori_loop(0, tracers // (2 * CHUNK), two, 0)
    inner = elements - 2 * cap
    row = lax.broadcasted_iota(jnp.int32, (inner * levels, elements * levels), 0)
    column = lax.broadcasted_iota(jnp.int32, (inner * levels, elements * levels), 1)
    same = (row // levels + cap == column % elements) & (row % levels == column // elements)
    order = jnp.where(same, 1.0, 0.0).astype(bf16)
    step = columns // 4
    stores = []
    for n in range(4):
        part = pl.ds(n * step, step)
        y = lax.dot_general(
            order, moved_ref[part, :], (((1,), (1,)), ((), ())), preferred_element_type=f32
        )
        inner_ref[:, :, part] = y.reshape(inner, levels, step).astype(bf16)
        stores.append(pltpu.make_async_copy(
            inner_ref.at[pl.ds(1, inner - 2), :, part], out_ref.at[pl.ds(cap + 1, inner - 2), :, part], sems.at[n]
        ))
        stores[n].start()
    sides_ref[0] = inner_ref[0]
    sides_ref[1] = inner_ref[inner - 1]
    for n, low in enumerate((0, elements - cap)):
        ends_ref[n] = jnp.concatenate(
            [moved_ref[:, k * elements + low : k * elements + low + cap] for k in range(levels)], axis=1
        )
    for store in stores:
        store.wait()


def combine_kernel(pair, part_ref, ends_ref, sides_ref, received_ref, sent_ref, out_ref, rows_ref, sems):
    del part_ref
    refs = (ends_ref, sides_ref, received_ref, sent_ref, out_ref, rows_ref, sems)
    even = is_even()
    head = jnp.logical_not(even) if pair else even
    pl.when(head)(lambda: combine(True, *refs))
    pl.when(jnp.logical_not(head))(lambda: combine(False, *refs))


def combine(head, ends_ref, sides_ref, received_ref, sent_ref, out_ref, rows_ref, sems):
    elements, levels, columns = out_ref.shape
    lanes_all = received_ref.shape[1]
    cap = elements // levels
    tracers = columns // 16
    end = 0 if head else 1
    place = lax.broadcasted_iota(jnp.int32, (1, lanes_all), 1) % cap
    order = interleave(levels, cap)
    span = 4 * tracers
    spot = pl.ds(0, cap + 1) if head else pl.ds(elements - cap - 1, cap + 1)

    def rows(ref, block):
        return ref[block * tracers : (block + 1) * tracers, :].astype(f32)

    stores = []
    for j in range(4):
        got = [rows(received_ref, 3 * j + i) for i in range(3)]
        if head:
            own = pltpu.roll(rows(sent_ref, 3 * j + 2), lanes_all - (cap - 1), 1)
            west = got[0] + jnp.where(place == 0, own, 0.0)
            east = jnp.where(place == cap - 1, 0.0, pltpu.roll(got[0], lanes_all - 1, 1))
            got = [west, got[1], got[2], east]
        else:
            own = pltpu.roll(rows(sent_ref, 3 * j), cap - 1, 1)
            east = got[2] + jnp.where(place == cap - 1, own, 0.0)
            west = jnp.where(place == 0, 0.0, pltpu.roll(got[2], 1, 1))
            got = [west, got[0], got[1], east]
        pieces = []
        for i, value in enumerate(got):
            node = 4 * j + i
            here = ends_ref[end, node * tracers : (node + 1) * tracers, :].astype(f32)
            pieces.append((here + value).astype(bf16))
        y = lax.dot_general(
            order, jnp.concatenate(pieces, axis=0), (((1,), (1,)), ((), ())), preferred_element_type=f32
        ).reshape(cap, levels, span)
        first = 12 * tracers + 8 * (j * tracers // lanes_all)
        low = j * tracers % lanes_all
        far = received_ref[first : first + 8, low : low + tracers].astype(f32)[:levels]
        zeros = jnp.zeros((levels, span - tracers), f32)
        west = jnp.concatenate([far, zeros], axis=1)
        east = jnp.concatenate([zeros, far], axis=1)
        part = slice(j * span, (j + 1) * span)
        if head:
            rows_ref[0 : cap - 1, :, part] = y[: cap - 1].astype(bf16)
            rows_ref[cap - 1, :, part] = (y[cap - 1] + east).astype(bf16)
            rows_ref[cap, :, part] = (sides_ref[0, :, part].astype(f32) + west).astype(bf16)
        else:
            rows_ref[2:, :, part] = y[1:].astype(bf16)
            rows_ref[1, :, part] = (y[0] + west).astype(bf16)
            rows_ref[0, :, part] = (sides_ref[1, :, part].astype(f32) + east).astype(bf16)
        part = pl.ds(j * span, span)
        stores.append(pltpu.make_async_copy(rows_ref.at[:, :, part], out_ref.at[spot, :, part], sems.at[j]))
        stores[j].start()
    for store in stores:
        store.wait()


def on_device(tracers, velocity, node_mass, source):
    elements, levels, columns = tracers.shape
    cap = elements // 4
    assert cap * levels == elements
    count = columns // 16
    lanes = levels * elements
    runs = lax.axis_size("elem")
    pairing = [(i, i ^ 1) for i in range(runs)]
    crossing = [(i, (i - 1 if i % 2 == 0 else i + 1) % runs) for i in range(runs)]
    shape = jax.ShapeDtypeStruct
    vmem = pl.BlockSpec(memory_space=pltpu.VMEM)
    anywhere = pl.BlockSpec(memory_space=pl.ANY)
    source = source.reshape(1, elements)

    packet = shape((PACKET, elements), f32)
    inputs = (tracers, velocity, node_mass, source)
    here, lowest, cross_sent, pair_sent, velocity, node_mass, source = pl.pallas_call(
        prepare_kernel,
        out_shape=(shape((columns, lanes), bf16), shape((columns, elements), bf16), packet, packet)
        + tuple(shape(x.shape, x.dtype) for x in inputs[1:]),
        in_specs=[anywhere] * 4,
        scratch_shapes=[pltpu.VMEM(tracers.shape, bf16), pltpu.SemaphoreType.DMA((4,))],
        compiler_params=params(),
        name="prepare",
    )(*[pltpu.with_memory_space_constraint(x, pltpu.HBM) for x in inputs])
    blocks = lax.axis_size("lev")
    above = lax.ppermute(lowest, "lev", [(i, (i + 1) % blocks) for i in range(blocks)])
    pair_packet = lax.ppermute(pair_sent, "elem", pairing)
    cross_packet = lax.ppermute(cross_sent, "elem", crossing)
    def weighed(pair, packet, own, after):
        return pl.pallas_call(
            functools.partial(weigh_kernel, pair, levels),
            out_shape=(
                shape((16, 16, elements), f32),
                shape((16, 8, elements), f32),
                shape((lanes, 2 * elements), bf16),
            ),
            in_specs=[anywhere, vmem, vmem],
            compiler_params=params(),
            name="weigh_pair" if pair else "weigh_cross",
        )(after, packet, own)

    lifted = pl.pallas_call(
        lift_kernel,
        out_shape=shape((16, count, lanes), bf16),
        compiler_params=params(),
        name="lift",
    )(here, above, velocity)

    far_rows = 8 * (4 * count // elements)

    def contributions(pair, weights, after):
        return pl.pallas_call(
            functools.partial(remote_kernel, pair),
            out_shape=shape((12 * count + far_rows, elements), bf16),
            in_specs=[anywhere] + [vmem] * 4,
            scratch_shapes=[
                pltpu.VMEM((16, count, 2 * elements), f32),
                pltpu.VMEM((4 * count, elements), bf16),
            ],
            compiler_params=params(),
            name="remote_pair" if pair else "remote_cross",
        )(after, lifted, *weights)

    pair_out = contributions(True, weighed(True, pair_packet, pair_sent, lifted), lifted)
    pair_in = lax.ppermute(pair_out, "elem", pairing)
    cross_out = contributions(False, weighed(False, cross_packet, cross_sent, pair_out), pair_out)
    cross_in = lax.ppermute(cross_out, "elem", crossing)
    result = shape((elements, levels, columns), bf16)
    part, ends, sides = pl.pallas_call(
        local_kernel,
        out_shape=(result, shape((2, columns, elements), bf16), shape((2, levels, columns), bf16)),
        in_specs=[vmem] * 4 + [anywhere],
        out_specs=(anywhere, vmem, vmem),
        scratch_shapes=[
            pltpu.VMEM((2, 16, CHUNK, elements), f32),
            pltpu.VMEM((16, 16, elements), f32),
            pltpu.VMEM((2, 16, elements), f32),
            pltpu.VMEM((columns, lanes), bf16),
            pltpu.VMEM((elements - 2 * cap, levels, columns), bf16),
            pltpu.SemaphoreType.DMA((4,)),
        ],
        compiler_params=params(),
        cost_estimate=cost(10**9),
        name="local",
    )(velocity, node_mass, source, lifted, cross_out)
    for pair, received, sent in ((True, pair_in, pair_out), (False, cross_in, cross_out)):
        part = pl.pallas_call(
            functools.partial(combine_kernel, pair),
            out_shape=result,
            in_specs=[anywhere, vmem, vmem, vmem, vmem],
            out_specs=anywhere,
            scratch_shapes=[pltpu.VMEM((cap + 1, levels, columns), bf16), pltpu.SemaphoreType.DMA((4,))],
            input_output_aliases={0: 0},
            compiler_params=params(),
            name="combine_pair" if pair else "combine_cross",
        )(part, ends, sides, received, sent)
    return part


def solution(mesh):
    placed = (P("elem", "lev", None), P(None, None, "lev", "elem"), P(None, "elem"), P("elem"))
    return jax.shard_map(
        on_device, mesh=mesh, in_specs=placed, out_specs=P("elem", "lev", None), check_vma=False
    )
```

time: 27 us -> 25.7 us (0.952)
  local copies, waits for them, and re-layouts: 1.24 us -> 0 us
  waiting for transfers between devices: 1.11 us -> 0.01 us
  Pallas kernels: 12.5 us -> 13.1 us
  starting transfers between devices: 11.9 us -> 12.4 us
    ppermute x1, starting transfers between devices: 0.01 us -> 2.2 us  [on_device(): pair_in = lax.ppermute(pair_out, 'elem', pairing)]
    ppermute x1, starting transfers between devices: 2.36 us -> 0.5 us  [on_device(): lax.ppermute(lowest, 'lev', [(i, (i + 1) % blocks) for i in range(blocks)])]
    pallas_call x3 -> x4, Pallas kernels: 1.58 us -> 3.02 us  [the longest x1 2.12 us: on_device(): pl.pallas_call(prepare_kernel, out_shape=(shape((columns, lanes), bf16),...]
    unnamed x8 -> x0, local copies, waits for them, and re-layouts: 1.24 us -> none
    ppermute x1, waiting for transfers between devices: 1.1 us -> 0.01 us  [on_device(): cross_packet = lax.ppermute(cross_sent, 'elem', crossing)]
    pallas_call x2, Pallas kernels: 2.55 us -> 2.07 us  [on_device(): pl.pallas_call(functools.partial(combine_kernel, pair), out_shape=result,...]
    pallas_call x1, Pallas kernels: 5.54 us -> 5.22 us  [on_device(): pl.pallas_call(local_kernel, out_shape=(result, shape((2, columns, elemen...]
  transfers between devices with their start and end apart: 5 -> 5, of which waited for: 1 -> 0; matrix products, arithmetic and copies ran while one was open for 0% -> 0% of each run, Pallas kernels for 39% -> 39%
where the time goes in v3:
time: 25.7 us; the launch traced here: 25.6 us
  Pallas kernels  13.1 us (51%)
  starting transfers between devices  12.4 us (48%)
    pallas_call x1, Pallas kernels, on_device(): pl.pallas_call(local_kernel, out_shape=(result, shape((2, columns, elemen...  5.22 us
    ppermute x1, starting transfers between devices, on_device(): cross_in = lax.ppermute(cross_out, 'elem', crossing)  3.56 us
    ppermute x1, starting transfers between devices, on_device(): cross_packet = lax.ppermute(cross_sent, 'elem', crossing)  3.55 us
    pallas_call x2, Pallas kernels, contributions(): pl.pallas_call(functools.partial(remote_kernel, pair), out_shape=shape((1...  2.77 us
    ppermute x1, starting transfers between devices, on_device(): pair_packet = lax.ppermute(pair_sent, 'elem', pairing)  2.6 us
    ppermute x1, starting transfers between devices, on_device(): pair_in = lax.ppermute(pair_out, 'elem', pairing)  2.2 us
    pallas_call x1, Pallas kernels, on_device(): pl.pallas_call(prepare_kernel, out_shape=(shape((columns, lanes), bf16),...  2.12 us
    pallas_call x2, Pallas kernels, on_device(): pl.pallas_call(functools.partial(combine_kernel, pair), out_shape=result,...  2.07 us
  transfers between devices with their start and end apart: 5, of which 0 were waited for; matrix products, arithmetic and copies ran while one was open for 0% of the time, Pallas kernels for 39%

profile of v3, /device:TPU:0, one launch (start us, length us, event | category | flops | bytes accessed | tf_op | source)
XLA Modules:
  0.0 25.6 jit_solution(863297455303769210)
XLA Ops:
  0.0 2.1 %prepare.1 = (bf16[1024,512]{1,0:T(8,128)(2,1)S(1)}, bf16[1024,128]{1,0:T(8,128)(2,1)S(1)}, f32[64,128]{1,0:T(8,128)S(1)}, f32[64,128]{1,0:T(8,128)S(1)}, f32[3,...) custom-call(bf16[128,4,1024]{2,1,0:T(4,128)(2,1)} %tracers_hbm.1, ...), custom_call_target="tpu_custom_call" | custom-call | tf_op jit(solution)/shard_map/prepare/pallas_call | solution.py:466
  2.1 0.5 %collective-permute-start = (bf16[1024,128]{1,0:T(8,128)(2,1)S(1)}, bf16[1024,128]{1,0:T(8,128)(2,1)S(1)}, u32[]{:S(2)}, u32[]{:S(2)}) collective-permute-start(bf16[1024,128]{1,0:T(8,128)(2,1)S(1)} %get-tuple-element.25), channel_id=1, source_target_pairs={{0,1},{1,2},{2,3},{3,0},{4,5},{5,6},{6,7},{7,4},{8,9},{9,10},{10,1... | collective-permute-start | bytes 786440 | tf_op jit(solution)/shard_map/ppermute | solution.py:476
  2.6 2.6 %collective-permute-start.1 = (f32[64,128]{1,0:T(8,128)S(1)}, f32[64,128]{1,0:T(8,128)S(1)}, u32[]{:S(2)}, u32[]{:S(2)}) collective-permute-start(f32[64,128]{1,0:T(8,128)S(1)} %get-tuple-element.26.own_ref), channel_id=1, source_target_pairs={{0,4},{4,0},{8,12},{12,8},{16,20},{20,16},{24,28},{28,24},{1,5},{5... | collective-permute-start | bytes 98312 | tf_op jit(solution)/shard_map/ppermute | solution.py:477
  5.2 3.5 %collective-permute-start.2 = (f32[64,128]{1,0:T(8,128)S(1)}, f32[64,128]{1,0:T(8,128)S(1)}, u32[]{:S(2)}, u32[]{:S(2)}) collective-permute-start(f32[64,128]{1,0:T(8,128)S(1)} %get-tuple-element.30.own_ref), channel_id=1, source_target_pairs={{0,28},{4,8},{8,4},{12,16},{16,12},{20,24},{24,20},{28,0},{1,29},{... | collective-permute-start | bytes 98312 | tf_op jit(solution)/shard_map/ppermute | solution.py:478
  8.8 0.0 collective-permute-done.above_ref
  8.8 0.5 %lift.1.after_ref.refs_0_.lifted_ref = bf16[16,64,512]{2,1,0:T(8,128)(2,1)S(1)} custom-call(bf16[1024,512]{1,0:T(8,128)(2,1)S(1)} %get-tuple-element.24.here_ref, bf16[1024,128]{1,0:T(8,128)(2,1)S(1)} %collective-permute-done.above_ref, f32[3,16,4,128]{3,2,1,0:T(4,128)S(1)} %get-tuple-element.21.velocity_ref), custom_call_target="tpu_custom_call" | custom-call | tf_op jit(solution)/shard_map/lift/pallas_call | solution.py:492
  9.3 0.0 collective-permute-done.1.packet_ref
  9.3 0.2 weigh_pair.1
  9.5 1.3 %remote_pair.1.after_ref.sent_ref = bf16[784,128]{1,0:T(8,128)(2,1)S(1)} custom-call(bf16[16,64,512]{2,1,0:T(8,128)(2,1)S(1)} %lift.1.after_ref.refs_0_.lifted_ref, bf16[16,64,512]{2,1,0:T(8,128)(2,1)S(1)} %lift.1.after_ref.refs_0_.lifted_ref, f32[16,16,128]{2,1,0:T(8,128)S(1)} %get-tuple-element.27.refs_1_, f32[16,8,128]{2,1,0:T(8,128)S(1)} %get-tuple-element.28.refs_2_, ...), custom_call_target="tpu_custom_call" | custom-call | tf_op jit(solution)/shard_map/remote_pair/pallas_call | solution.py:502
  10.8 2.2 %collective-permute-start.3 = (bf16[784,128]{1,0:T(8,128)(2,1)S(1)}, bf16[784,128]{1,0:T(8,128)(2,1)S(1)}, u32[]{:S(2)}, u32[]{:S(2)}) collective-permute-start(bf16[784,128]{1,0:T(8,128)(2,1)S(1)} %remote_pair.1.after_ref.sent_ref), channel_id=1, source_target_pairs={{0,4},{4,0},{8,12},{12,8},{16,20},{20,16},{24,28},{28,24},{1,5},{5... | collective-permute-start | bytes 602120 | tf_op jit(solution)/shard_map/ppermute | solution.py:515
  13.0 0.0 collective-permute-done.2.packet_ref
  13.0 0.2 weigh_cross.1
  13.2 1.5 %remote_cross.1.after_ref.sent_ref = bf16[784,128]{1,0:T(8,128)(2,1)S(1)} custom-call(bf16[784,128]{1,0:T(8,128)(2,1)S(1)} %remote_pair.1.after_ref.sent_ref, bf16[16,64,512]{2,1,0:T(8,128)(2,1)S(1)} %lift.1.after_ref.refs_0_.lifted_ref, f32[16,16,128]{2,1,0:T(8,128)S(1)} %get-tuple-element.31.refs_1_, f32[16,8,128]{2,1,0:T(8,128)S(1)} %get-tuple-element.32.refs_2_, ...), custom_call_target="tpu_custom_call" | custom-call | tf_op jit(solution)/shard_map/remote_cross/pallas_call | solution.py:502
  14.7 3.6 %collective-permute-start.4 = (bf16[784,128]{1,0:T(8,128)(2,1)S(1)}, bf16[784,128]{1,0:T(8,128)(2,1)S(1)}, u32[]{:S(2)}, u32[]{:S(2)}) collective-permute-start(bf16[784,128]{1,0:T(8,128)(2,1)S(1)} %remote_cross.1.after_ref.sent_ref), channel_id=1, source_target_pairs={{0,28},{4,8},{8,4},{12,16},{16,12},{20,24},{24,20},{28,0},{1,29},{... | collective-permute-start | bytes 602120 | tf_op jit(solution)/shard_map/ppermute | solution.py:517
  18.2 5.2 %local.1 = (bf16[128,4,1024]{2,1,0:T(4,128)(2,1)}, bf16[2,1024,128]{2,1,0:T(8,128)(2,1)S(1)}, bf16[2,4,1024]{2,1,0:T(4,128)(2,1)S(1)}) custom-call(f32[3,16,4,128]{3,2,1,0:T(4,128)S(1)} %get-tuple-element.21.velocity_ref, f32[16,128]{1,0:T(8,128)S(1)} %get-tuple-element.22.mass_ref, s32[1,128]{1,0:T(1,128)S(1)} %get-tuple-element.23.source_ref, ...), custom_call_target="tpu_custom_call" | custom-call | flops 99999997952 | bytes 1000000000 | tf_op jit(solution)/shard_map/local/pallas_call | solution.py:519
  23.5 0.0 collective-permute-done.3.received_ref
  23.5 1.0 %combine_pair.1.part_ref = bf16[128,4,1024]{2,1,0:T(4,128)(2,1)} custom-call(bf16[128,4,1024]{2,1,0:T(4,128)(2,1)} %get-tuple-element.34.part_ref, bf16[2,1024,128]{2,1,0:T(8,128)(2,1)S(1)} %get-tuple-element.35.ends_ref, bf16[2,4,1024]{2,1,0:T(4,128)(2,1)S(1)} %get-tuple-element.36.sides_ref, ...), custom_call_target="tpu_custom_call", output_to_operand_aliasing={{}: (0, {})} | custom-call | tf_op jit(solution)/shard_map/combine_pair/pallas_call | solution.py:537
  24.5 0.0 collective-permute-done.4.received_ref
  24.5 1.0 %combine_cross.1 = bf16[128,4,1024]{2,1,0:T(4,128)(2,1)} custom-call(bf16[128,4,1024]{2,1,0:T(4,128)(2,1)} %combine_pair.1.part_ref, bf16[2,1024,128]{2,1,0:T(8,128)(2,1)S(1)} %get-tuple-element.35.ends_ref, bf16[2,4,1024]{2,1,0:T(4,128)(2,1)S(1)} %get-tuple-element.36.sides_ref, ...), custom_call_target="tpu_custom_call", output_to_operand_aliasing={{}: (0, {})} | custom-call | tf_op jit(solution)/shard_map/combine_cross/pallas_call | solution.py:537
Async XLA Ops:
  2.1 6.6 %collective-permute-start = (bf16[1024,128]{1,0:T(8,128)(2,1)S(1)}, bf16[1024,128]{1,0:T(8,128)(2,1)S(1)}, u32[]{:S(2)}, u32[]{:S(2)}) collective-permute-start(bf16[1024,128]{1,0:T(8,128)(2,1)S(1)} %get-tuple-element.25), channel_id=1, source_target_pairs={{0,1},{1,2},{2,3},{3,0},{4,5},{5,6},{6,7},{7,4},{8,9},{9,10},{10,1... | collective-permute-start | bytes 786440 | tf_op jit(solution)/shard_map/ppermute | solution.py:476
  2.6 6.7 %collective-permute-start.1 = (f32[64,128]{1,0:T(8,128)S(1)}, f32[64,128]{1,0:T(8,128)S(1)}, u32[]{:S(2)}, u32[]{:S(2)}) collective-permute-start(f32[64,128]{1,0:T(8,128)S(1)} %get-tuple-element.26.own_ref), channel_id=1, source_target_pairs={{0,4},{4,0},{8,12},{12,8},{16,20},{20,16},{24,28},{28,24},{1,5},{5... | collective-permute-start | bytes 98312 | tf_op jit(solution)/shard_map/ppermute | solution.py:477
  5.2 7.8 %collective-permute-start.2 = (f32[64,128]{1,0:T(8,128)S(1)}, f32[64,128]{1,0:T(8,128)S(1)}, u32[]{:S(2)}, u32[]{:S(2)}) collective-permute-start(f32[64,128]{1,0:T(8,128)S(1)} %get-tuple-element.30.own_ref), channel_id=1, source_target_pairs={{0,28},{4,8},{8,4},{12,16},{16,12},{20,24},{24,20},{28,0},{1,29},{... | collective-permute-start | bytes 98312 | tf_op jit(solution)/shard_map/ppermute | solution.py:478
  10.8 12.6 %collective-permute-start.3 = (bf16[784,128]{1,0:T(8,128)(2,1)S(1)}, bf16[784,128]{1,0:T(8,128)(2,1)S(1)}, u32[]{:S(2)}, u32[]{:S(2)}) collective-permute-start(bf16[784,128]{1,0:T(8,128)(2,1)S(1)} %remote_pair.1.after_ref.sent_ref), channel_id=1, source_target_pairs={{0,4},{4,0},{8,12},{12,8},{16,20},{20,16},{24,28},{28,24},{1,5},{5... | collective-permute-start | bytes 602120 | tf_op jit(solution)/shard_map/ppermute | solution.py:515
  14.7 9.8 %collective-permute-start.4 = (bf16[784,128]{1,0:T(8,128)(2,1)S(1)}, bf16[784,128]{1,0:T(8,128)(2,1)S(1)}, u32[]{:S(2)}, u32[]{:S(2)}) collective-permute-start(bf16[784,128]{1,0:T(8,128)(2,1)S(1)} %remote_cross.1.after_ref.sent_ref), channel_id=1, source_target_pairs={{0,28},{4,8},{8,4},{12,16},{16,12},{20,24},{24,20},{28,0},{1,29},{... | collective-permute-start | bytes 602120 | tf_op jit(solution)/shard_map/ppermute | solution.py:517

commit v4 on v3

--- a/solution.py
+++ b/solution.py
@@ -12,7 +12,6 @@
 f32 = jnp.float32
 bf16 = jnp.bfloat16
 VMEM_LIMIT = 40 << 20
-CHUNK = 16
 
 MASS, NEAR, NEAR_MASS, SOURCE, PACKET = 32, 48, 56, 60, 64
 
@@ -136,22 +135,36 @@
     out_ref[SOURCE + 1 :, :] = jnp.zeros((PACKET - SOURCE - 1, elements), f32)
 
 
-def lift_kernel(here_ref, above_ref, velocity_ref, out_ref):
+def lift(here, upper, descent):
+    return ((1.0 - descent) * here.astype(f32) + descent * upper.astype(f32)).astype(bf16)
+
+
+def descents(velocity_ref, k):
+    return 1.0 / (1.0 + jnp.exp(-velocity_ref[2, :, k, :]))
+
+
+def lift_rest_kernel(here_ref, velocity_ref, out_ref):
     _, nodes, levels, elements = velocity_ref.shape
     tracers = here_ref.shape[0] // nodes
-    below_top = lax.axis_index("lev") > 0
-    for k in range(levels):
-        descent = 1.0 / (1.0 + jnp.exp(-velocity_ref[2, :, k, :]))
-        lanes = slice(k * elements, (k + 1) * elements)
+    for k in range(1, levels):
+        descent = descents(velocity_ref, k)
         for m in range(nodes):
             rows = slice(m * tracers, (m + 1) * tracers)
-            here = here_ref[rows, lanes].astype(f32)
-            if k == 0:
-                upper = jnp.where(below_top, above_ref[rows, :].astype(f32), 0.0)
-            else:
-                upper = here_ref[rows, (k - 1) * elements : k * elements].astype(f32)
-            d = descent[m : m + 1]
-            out_ref[m, :, lanes] = ((1.0 - d) * here + d * upper).astype(bf16)
+            here = here_ref[rows, k * elements : (k + 1) * elements]
+            upper = here_ref[rows, (k - 1) * elements : k * elements]
+            out_ref[m, :, (k - 1) * elements : k * elements] = lift(here, upper, descent[m : m + 1])
+
+
+def lift_first_kernel(after_ref, here_ref, above_ref, velocity_ref, out_ref):
+    del after_ref
+    _, nodes, _, elements = velocity_ref.shape
+    tracers = above_ref.shape[0] // nodes
+    descent = descents(velocity_ref, 0)
+    below_top = lax.axis_index("lev") > 0
+    for m in range(nodes):
+        rows = slice(m * tracers, (m + 1) * tracers)
+        upper = jnp.where(below_top, above_ref[rows, :].astype(f32), 0.0)
+        out_ref[m] = lift(here_ref[rows, 0:elements], upper, descent[m : m + 1])
 
 
 def by_i(ref, first, nodes=16):
@@ -162,18 +175,14 @@
     return (mass_left * left + mass_right * right) / (mass_left + mass_right)
 
 
-def interpolate(weights_ref, blocks_ref, node, rows, lanes, *slot):
-    total = None
+def interpolate(weights_ref, blocks, nodes):
+    totals = [None] * len(nodes)
     for m in range(16):
-        term = weights_ref[m, node : node + 1, :] * blocks_ref[(*slot, m, rows, lanes)]
-        total = term if total is None else total + term
-    return total
-
-
-def fetch(lifted_ref, t, lanes, chosen):
-    x = lifted_ref[:, pl.ds(t, CHUNK), lanes].reshape(16 * CHUNK, chosen.shape[0])
-    y = jnp.dot(x, chosen, preferred_element_type=f32)
-    return y.reshape(16, CHUNK, chosen.shape[1])
+        block = blocks(m)
+        for n, node in enumerate(nodes):
+            term = weights_ref[m, node : node + 1, :] * block
+            totals[n] = term if totals[n] is None else totals[n] + term
+    return totals
 
 
 def by_side(pair, body, *args):
@@ -235,59 +244,65 @@
     for b in range(4):
         for a in range(4):
             weights_ref[4 * b + a] = along[a] * across[b]
-    edge_share = 1.0 - (share_west if ahead else share_east)
-    extra_along = basis(gll_points[3 if ahead else 0] - courant * edge_winds[0])
-    across_position = node_rows(4, lanes_all, False) - courant * edge_winds[1]
-    extra_across = [factor * edge_share for factor in basis(across_position)]
+    at = 0 if ahead else cap - 1
+
+    def spread(rows):
+        out = jnp.zeros((1, lanes_all), f32)
+        for j in range(4):
+            out = jnp.where(place == j, pltpu.roll(rows[j : j + 1], (j - at) % lanes_all, 1), out)
+        return out
+
+    edge_share = spread(1.0 - (share_west if ahead else share_east))
+    node = jnp.where(place < 2, jnp.where(place == 0, *gll_points[:2]), jnp.where(place == 2, *gll_points[2:]))
+    extra_along = basis(gll_points[3 if ahead else 0] - courant * spread(edge_winds[0]))
+    extra_across = [factor * edge_share for factor in basis(node - courant * spread(edge_winds[1]))]
     for b in range(4):
         for a in range(4):
-            extra_ref[4 * b + a, 0:4] = extra_along[a] * extra_across[b]
+            extra_ref[4 * b + a, 0:1] = extra_along[a] * extra_across[b]
 
     source = packet_ref[SOURCE : SOURCE + 1, :].astype(jnp.int32)
-    own_source = own_ref[SOURCE : SOURCE + 1, :].astype(jnp.int32) + (elements if ahead else -elements)
+    own_source = jnp.where(lane == (cap - 1 if ahead else 0), own_ref[SOURCE : SOURCE + 1, :], 0.0)
+    own_source = jnp.sum(own_source, axis=1, keepdims=True).astype(jnp.int32) + (elements if ahead else -elements)
     own_source = jnp.where(own_source >= total, own_source - total, own_source)
     own_source = jnp.where(own_source < 0, own_source + total, own_source)
-    own_source = pltpu.roll(own_source, lanes_all - (cap - 1) if ahead else cap - 1, 1)
     row = lax.broadcasted_iota(jnp.int32, (levels * elements, lanes_all), 0)
     same = row // elements == level
     first = jnp.where(same & (row % elements == source), 1.0, 0.0).astype(bf16)
-    second = jnp.where(same & edge & (row % elements == own_source), 1.0, 0.0).astype(bf16)
+    second = jnp.where(same & (place < 4) & (row % elements == own_source), 1.0, 0.0).astype(bf16)
     chosen_ref[...] = jnp.concatenate([first, second], axis=1)
 
 
-def remote(ahead, lifted_ref, weights_ref, extra_ref, chosen_ref, out_ref, blocks_ref, edge_ref):
+def remote(ahead, first_ref, rest_ref, weights_ref, extra_ref, chosen_ref, out_ref, blocks_ref, edge_ref):
     lanes_all = out_ref.shape[1]
-    levels = lifted_ref.shape[2] // lanes_all
+    levels = 1 + rest_ref.shape[2] // lanes_all
     cap = lanes_all // levels
-    tracers = lifted_ref.shape[1]
+    tracers = first_ref.shape[1]
     lane = lax.broadcasted_iota(jnp.int32, (1, lanes_all), 1)
     place = lane % cap
     edge = place == (0 if ahead else cap - 1)
     chosen = chosen_ref[...]
     for m in range(0, 16, 4):
-        x = lifted_ref[m : m + 4].reshape(4 * tracers, levels * lanes_all)
-        y = jnp.dot(x, chosen, preferred_element_type=f32)
+        x = first_ref[m : m + 4].reshape(4 * tracers, lanes_all)
+        y = jnp.dot(x, chosen[:lanes_all], preferred_element_type=f32)
+        x = rest_ref[m : m + 4].reshape(4 * tracers, (levels - 1) * lanes_all)
+        y += jnp.dot(x, chosen[lanes_all:], preferred_element_type=f32)
         blocks_ref[m : m + 4] = y.reshape(4, tracers, 2 * lanes_all)
 
-    def one(index, carry):
-        t = pl.multiple_of(index * CHUNK, CHUNK)
-        rows = pl.ds(t, CHUNK)
-        lanes = slice(0, lanes_all)
-        for j in range(4):
-            moved = [interpolate(weights_ref, blocks_ref, 4 * i + j, rows, lanes) for i in range(4)]
-            own = interpolate(extra_ref, blocks_ref, j, rows, slice(lanes_all, 2 * lanes_all))
-            if ahead:
-                west = moved[0] + jnp.where(edge, own, pltpu.roll(moved[3], 1, 1))
-                values, far = (west, moved[1], moved[2]), moved[3]
-            else:
-                east = moved[3] + jnp.where(edge, own, pltpu.roll(moved[0], lanes_all - 1, 1))
-                values, far = (moved[1], moved[2], east), moved[0]
-            for i, value in enumerate(values):
-                out_ref[pl.ds(t + (3 * j + i) * tracers, CHUNK), :] = value.astype(bf16)
-            edge_ref[pl.ds(t + j * tracers, CHUNK), :] = far.astype(bf16)
-        return carry
-
-    lax.fori_loop(0, tracers // CHUNK, one, 0)
+    first = slice(0, lanes_all)
+    (own,) = interpolate(extra_ref, lambda m: blocks_ref[m, :, lanes_all:], (0,))
+    for j in range(4):
+        ends = interpolate(weights_ref, lambda m: blocks_ref[m, :, first], (j, 12 + j))
+        middle = interpolate(weights_ref, lambda m: blocks_ref[m, :, first], (4 + j, 8 + j))
+        own_here = pltpu.roll(own, ((0 if ahead else cap - 1) - j) % lanes_all, 1)
+        if ahead:
+            west = ends[0] + jnp.where(edge, own_here, pltpu.roll(ends[1], 1, 1))
+            values, far = (west, *middle), ends[1]
+        else:
+            east = ends[1] + jnp.where(edge, own_here, pltpu.roll(ends[0], lanes_all - 1, 1))
+            values, far = (*middle, east), ends[0]
+        for i, value in enumerate(values):
+            out_ref[(3 * j + i) * tracers : (3 * j + i + 1) * tracers, :] = value.astype(bf16)
+        edge_ref[j * tracers : (j + 1) * tracers, :] = far.astype(bf16)
     row = lax.broadcasted_iota(jnp.int32, (8, lanes_all), 0)
     far_place = cap - 1 if ahead else 0
     pick = jnp.where(lane == row * cap + far_place, 1.0, 0.0).astype(bf16)
@@ -297,7 +312,7 @@
 
 
 def local_kernel(
-    velocity_ref, mass_ref, source_ref, lifted_ref, after_ref,
+    velocity_ref, mass_ref, source_ref, first_ref, rest_ref, after_ref,
     out_ref, ends_ref, sides_ref,
     blocks_ref, weights_ref, wind_ref, moved_ref, inner_ref, sems,
 ):
@@ -316,7 +331,13 @@
     coefficient = jnp.concatenate([share_west, jnp.ones((8, elements), f32), share_east], axis=0)
     row = lax.broadcasted_iota(jnp.int32, (elements, elements), 0)
     chosen = jnp.where(row == source_ref[...] - start, 1.0, 0.0).astype(bf16)
-    blocks_ref[0] = fetch(lifted_ref, 0, slice(0, elements), chosen)
+
+    def fetch(k):
+        x = rest_ref[:, :, (k - 1) * elements : k * elements] if k else first_ref[...]
+        y = jnp.dot(x.reshape(columns, elements), chosen, preferred_element_type=f32)
+        blocks_ref[k % 2] = y.reshape(16, tracers, elements)
+
+    fetch(0)
     for k in range(levels):
         winds = []
         for c in range(2):
@@ -328,32 +349,19 @@
         along, across = table(winds, coefficient)
         for b in range(4):
             for a in range(4):
-                weights_ref[4 * b + a] = along[a] * across[b]
+                weights_ref[k % 2, 4 * b + a] = along[a] * across[b]
+        if k + 1 < levels:
+            fetch(k + 1)
         lanes = slice(k * elements, (k + 1) * elements)
-
-        def one(t, slot, later, later_lanes):
-            blocks_ref[1 - slot] = fetch(lifted_ref, later, later_lanes, chosen)
-            for j in range(4):
-                moved = [
-                    interpolate(weights_ref, blocks_ref, 4 * i + j, slice(None), slice(0, elements), slot)
-                    for i in range(4)
-                ]
-                west = jnp.where(lane == 0, 0.0, moved[0] + pltpu.roll(moved[3], 1, 1))
-                east = pltpu.roll(west, elements - 1, 1)
-                for i, value in enumerate((west, moved[1], moved[2], east)):
-                    moved_ref[pl.ds(t + (4 * j + i) * tracers, CHUNK), lanes] = value.astype(bf16)
-
-        def two(index, carry):
-            t = pl.multiple_of(index * (2 * CHUNK), 2 * CHUNK)
-            later = t + 2 * CHUNK
-            over = later >= tracers
-            level = jnp.where(over, min(k + 1, levels - 1), k)
-            later_lanes = pl.ds(pl.multiple_of(level * elements, elements), elements)
-            one(t, 0, t + CHUNK, lanes)
-            one(t + CHUNK, 1, pl.multiple_of(jnp.where(over, 0, later), CHUNK), later_lanes)
-            return carry
-
-        lax.fori_loop(0, tracers // (2 * CHUNK), two, 0)
+        table_ref = weights_ref.at[k % 2]
+        for j in range(4):
+            ends = interpolate(table_ref, lambda m: blocks_ref[k % 2, m], (j, 12 + j))
+            middle = interpolate(table_ref, lambda m: blocks_ref[k % 2, m], (4 + j, 8 + j))
+            west = jnp.where(lane == 0, 0.0, ends[0] + pltpu.roll(ends[1], 1, 1))
+            east = pltpu.roll(west, elements - 1, 1)
+            for i, value in enumerate((west, *middle, east)):
+                node = 4 * j + i
+                moved_ref[node * tracers : (node + 1) * tracers, lanes] = value.astype(bf16)
     inner = elements - 2 * cap
     row = lax.broadcasted_iota(jnp.int32, (inner * levels, elements * levels), 0)
     column = lax.broadcasted_iota(jnp.int32, (inner * levels, elements * levels), 1)
@@ -489,12 +497,20 @@
             name="weigh_pair" if pair else "weigh_cross",
         )(after, packet, own)
 
-    lifted = pl.pallas_call(
-        lift_kernel,
-        out_shape=shape((16, count, lanes), bf16),
+    pair_weights = weighed(True, pair_packet, pair_sent, lowest)
+    rest = pl.pallas_call(
+        lift_rest_kernel,
+        out_shape=shape((16, count, lanes - elements), bf16),
         compiler_params=params(),
-        name="lift",
-    )(here, above, velocity)
+        name="lift_rest",
+    )(here, velocity)
+    first = pl.pallas_call(
+        lift_first_kernel,
+        out_shape=shape((16, count, elements), bf16),
+        in_specs=[anywhere] + [vmem] * 3,
+        compiler_params=params(),
+        name="lift_first",
+    )(pair_weights[1], here, above, velocity)
 
     far_rows = 8 * (4 * count // elements)
 
@@ -502,16 +518,16 @@
         return pl.pallas_call(
             functools.partial(remote_kernel, pair),
             out_shape=shape((12 * count + far_rows, elements), bf16),
-            in_specs=[anywhere] + [vmem] * 4,
+            in_specs=[anywhere] + [vmem] * 5,
             scratch_shapes=[
                 pltpu.VMEM((16, count, 2 * elements), f32),
                 pltpu.VMEM((4 * count, elements), bf16),
             ],
             compiler_params=params(),
             name="remote_pair" if pair else "remote_cross",
-        )(after, lifted, *weights)
-
-    pair_out = contributions(True, weighed(True, pair_packet, pair_sent, lifted), lifted)
+        )(after, first, rest, *weights)
+
+    pair_out = contributions(True, pair_weights, first)
     pair_in = lax.ppermute(pair_out, "elem", pairing)
     cross_out = contributions(False, weighed(False, cross_packet, cross_sent, pair_out), pair_out)
     cross_in = lax.ppermute(cross_out, "elem", crossing)
@@ -519,11 +535,11 @@
     part, ends, sides = pl.pallas_call(
         local_kernel,
         out_shape=(result, shape((2, columns, elements), bf16), shape((2, levels, columns), bf16)),
-        in_specs=[vmem] * 4 + [anywhere],
+        in_specs=[vmem] * 5 + [anywhere],
         out_specs=(anywhere, vmem, vmem),
         scratch_shapes=[
-            pltpu.VMEM((2, 16, CHUNK, elements), f32),
-            pltpu.VMEM((16, 16, elements), f32),
+            pltpu.VMEM((2, 16, count, elements), f32),
+            pltpu.VMEM((2, 16, 16, elements), f32),
             pltpu.VMEM((2, 16, elements), f32),
             pltpu.VMEM((columns, lanes), bf16),
             pltpu.VMEM((elements - 2 * cap, levels, columns), bf16),
@@ -532,7 +548,7 @@
         compiler_params=params(),
         cost_estimate=cost(10**9),
         name="local",
-    )(velocity, node_mass, source, lifted, cross_out)
+    )(velocity, node_mass, source, first, rest, cross_out)
     for pair, received, sent in ((True, pair_in, pair_out), (False, cross_in, cross_out)):
         part = pl.pallas_call(
             functools.partial(combine_kernel, pair),

time: 25.7 us -> 24.2 us (0.942)
  Pallas kernels: 13.1 us -> 11.6 us
  starting transfers between devices: 12.4 us -> 11.8 us
  waiting for transfers between devices: 0.01 us -> 0.49 us
    pallas_call x1, Pallas kernels: 5.22 us -> 4.29 us  [on_device(): pl.pallas_call(local_kernel, out_shape=(result, shape((2, columns, elemen...]
    ppermute x1, starting transfers between devices: 2.2 us -> 1.6 us  [on_device(): pair_in = lax.ppermute(pair_out, 'elem', pairing)]
    pallas_call x2, Pallas kernels: 2.77 us -> 2.21 us  [contributions(): pl.pallas_call(functools.partial(remote_kernel, pair), out_shape=shape((1...]
    ppermute x1, waiting for transfers between devices: 0.01 us -> 0.48 us  [on_device(): cross_in = lax.ppermute(cross_out, 'elem', crossing)]
    pallas_call x1 -> x2, Pallas kernels: 0.53 us -> 0.53 us  [the longest x1 0.39 us: on_device(): pl.pallas_call(lift_rest_kernel, out_shape=shape((16, count, lanes - elem...]
  transfers between devices with their start and end apart: 5 -> 5, of which waited for: 0 -> 1; matrix products, arithmetic and copies ran while one was open for 0% -> 0% of each run, Pallas kernels for 39% -> 35%
where the time goes in v4:
time: 24.2 us; the launch traced here: 24 us
  starting transfers between devices  11.8 us (49%)
  Pallas kernels  11.6 us (48%)
  waiting for transfers between devices  0.49 us (2%)
    pallas_call x1, Pallas kernels, on_device(): pl.pallas_call(local_kernel, out_shape=(result, shape((2, columns, elemen...  4.29 us
    ppermute x1, starting transfers between devices, on_device(): cross_in = lax.ppermute(cross_out, 'elem', crossing)  3.59 us
    ppermute x1, starting transfers between devices, on_device(): cross_packet = lax.ppermute(cross_sent, 'elem', crossing)  3.55 us
    ppermute x1, starting transfers between devices, on_device(): pair_packet = lax.ppermute(pair_sent, 'elem', pairing)  2.6 us
    pallas_call x2, Pallas kernels, contributions(): pl.pallas_call(functools.partial(remote_kernel, pair), out_shape=shape((1...  2.21 us
    pallas_call x1, Pallas kernels, on_device(): pl.pallas_call(prepare_kernel, out_shape=(shape((columns, lanes), bf16),...  2.12 us
    pallas_call x2, Pallas kernels, on_device(): pl.pallas_call(functools.partial(combine_kernel, pair), out_shape=result,...  2.05 us
    ppermute x1, starting transfers between devices, on_device(): pair_in = lax.ppermute(pair_out, 'elem', pairing)  1.6 us
  transfers between devices with their start and end apart: 5, of which 1 were waited for; matrix products, arithmetic and copies ran while one was open for 0% of the time, Pallas kernels for 35%

profile of v4, /device:TPU:0, one launch (start us, length us, event | category | flops | bytes accessed | tf_op | source)
XLA Modules:
  0.0 24.0 jit_solution(18045484440295797393)
XLA Ops:
  0.0 2.1 %prepare.1 = (bf16[1024,512]{1,0:T(8,128)(2,1)S(1)}, bf16[1024,128]{1,0:T(8,128)(2,1)S(1)}, f32[64,128]{1,0:T(8,128)S(1)}, f32[64,128]{1,0:T(8,128)S(1)}, f32[3,...) custom-call(bf16[128,4,1024]{2,1,0:T(4,128)(2,1)} %tracers_hbm.1, ...), custom_call_target="tpu_custom_call" | custom-call | tf_op jit(solution)/shard_map/prepare/pallas_call | solution.py:474
  2.1 0.5 %collective-permute-start.1 = (bf16[1024,128]{1,0:T(8,128)(2,1)S(1)}, bf16[1024,128]{1,0:T(8,128)(2,1)S(1)}, u32[]{:S(2)}, u32[]{:S(2)}) collective-permute-start(bf16[1024,128]{1,0:T(8,128)(2,1)S(1)} %get-tuple-element.24.after_ref), channel_id=1, source_target_pairs={{0,1},{1,2},{2,3},{3,0},{4,5},{5,6},{6,7},{7,4},{8,9},{9,10},{10,1... | collective-permute-start | bytes 786440 | tf_op jit(solution)/shard_map/ppermute | solution.py:484
  2.6 2.6 %collective-permute-start = (f32[64,128]{1,0:T(8,128)S(1)}, f32[64,128]{1,0:T(8,128)S(1)}, u32[]{:S(2)}, u32[]{:S(2)}) collective-permute-start(f32[64,128]{1,0:T(8,128)S(1)} %get-tuple-element.25.own_ref), channel_id=1, source_target_pairs={{0,4},{4,0},{8,12},{12,8},{16,20},{20,16},{24,28},{28,24},{1,5},{5... | collective-permute-start | bytes 98312 | tf_op jit(solution)/shard_map/ppermute | solution.py:485
  5.2 3.5 %collective-permute-start.2 = (f32[64,128]{1,0:T(8,128)S(1)}, f32[64,128]{1,0:T(8,128)S(1)}, u32[]{:S(2)}, u32[]{:S(2)}) collective-permute-start(f32[64,128]{1,0:T(8,128)S(1)} %get-tuple-element.30.own_ref), channel_id=1, source_target_pairs={{0,28},{4,8},{8,4},{12,16},{16,12},{20,24},{24,20},{28,0},{1,29},{... | collective-permute-start | bytes 98312 | tf_op jit(solution)/shard_map/ppermute | solution.py:486
  8.8 0.4 %lift_rest.1.refs_1_.rest_ref = bf16[16,64,384]{2,1,0:T(8,128)(2,1)S(1)} custom-call(bf16[1024,512]{1,0:T(8,128)(2,1)S(1)} %get-tuple-element.27.here_ref, f32[3,16,4,128]{3,2,1,0:T(4,128)S(1)} %get-tuple-element.21.velocity_ref), custom_call_target="tpu_custom_call" | custom-call | tf_op jit(solution)/shard_map/lift_rest/pallas_call | solution.py:501
  9.2 0.0 collective-permute-done.packet_ref
  9.2 0.2 weigh_pair.1
  9.4 0.0 collective-permute-done.1.above_ref
  9.4 0.1 lift_first.1.after_ref.refs_0_.first_ref
  9.6 1.1 %remote_pair.1.after_ref.sent_ref = bf16[784,128]{1,0:T(8,128)(2,1)S(1)} custom-call(bf16[16,64,128]{2,1,0:T(8,128)(2,1)S(1)} %lift_first.1.after_ref.refs_0_.first_ref, bf16[16,64,128]{2,1,0:T(8,128)(2,1)S(1)} %lift_first.1.after_ref.refs_0_.first_ref, bf16[16,64,384]{2,1,0:T(8,128)(2,1)S(1)} %lift_rest.1.refs_1_.rest_ref, ...), custom_call_target="tpu_custom_call" | custom-call | tf_op jit(solution)/shard_map/remote_pair/pallas_call | solution.py:518
  10.7 1.6 %collective-permute-start.3 = (bf16[784,128]{1,0:T(8,128)(2,1)S(1)}, bf16[784,128]{1,0:T(8,128)(2,1)S(1)}, u32[]{:S(2)}, u32[]{:S(2)}) collective-permute-start(bf16[784,128]{1,0:T(8,128)(2,1)S(1)} %remote_pair.1.after_ref.sent_ref), channel_id=1, source_target_pairs={{0,4},{4,0},{8,12},{12,8},{16,20},{20,16},{24,28},{28,24},{1,5},{5... | collective-permute-start | bytes 602120 | tf_op jit(solution)/shard_map/ppermute | solution.py:531
  12.3 0.0 collective-permute-done.2.packet_ref
  12.3 0.2 weigh_cross.1
  12.5 1.1 %remote_cross.1.after_ref.sent_ref = bf16[784,128]{1,0:T(8,128)(2,1)S(1)} custom-call(bf16[784,128]{1,0:T(8,128)(2,1)S(1)} %remote_pair.1.after_ref.sent_ref, bf16[16,64,128]{2,1,0:T(8,128)(2,1)S(1)} %lift_first.1.after_ref.refs_0_.first_ref, bf16[16,64,384]{2,1,0:T(8,128)(2,1)S(1)} %lift_rest.1.refs_1_.rest_ref, ...), custom_call_target="tpu_custom_call" | custom-call | tf_op jit(solution)/shard_map/remote_cross/pallas_call | solution.py:518
  13.6 3.6 %collective-permute-start.4 = (bf16[784,128]{1,0:T(8,128)(2,1)S(1)}, bf16[784,128]{1,0:T(8,128)(2,1)S(1)}, u32[]{:S(2)}, u32[]{:S(2)}) collective-permute-start(bf16[784,128]{1,0:T(8,128)(2,1)S(1)} %remote_cross.1.after_ref.sent_ref), channel_id=1, source_target_pairs={{0,28},{4,8},{8,4},{12,16},{16,12},{20,24},{24,20},{28,0},{1,29},{... | collective-permute-start | bytes 602120 | tf_op jit(solution)/shard_map/ppermute | solution.py:533
  17.2 4.3 %local.1 = (bf16[128,4,1024]{2,1,0:T(4,128)(2,1)}, bf16[2,1024,128]{2,1,0:T(8,128)(2,1)S(1)}, bf16[2,4,1024]{2,1,0:T(4,128)(2,1)S(1)}) custom-call(f32[3,16,4,128]{3,2,1,0:T(4,128)S(1)} %get-tuple-element.21.velocity_ref, f32[16,128]{1,0:T(8,128)S(1)} %get-tuple-element.22.mass_ref, s32[1,128]{1,0:T(1,128)S(1)} %get-tuple-element.23.source_ref, ...), custom_call_target="tpu_custom_call" | custom-call | flops 99999997952 | bytes 1000000000 | tf_op jit(solution)/shard_map/local/pallas_call | solution.py:535
  21.5 0.0 collective-permute-done.3.received_ref
  21.5 1.0 %combine_pair.1.part_ref = bf16[128,4,1024]{2,1,0:T(4,128)(2,1)} custom-call(bf16[128,4,1024]{2,1,0:T(4,128)(2,1)} %get-tuple-element.34.part_ref, bf16[2,1024,128]{2,1,0:T(8,128)(2,1)S(1)} %get-tuple-element.35.ends_ref, bf16[2,4,1024]{2,1,0:T(4,128)(2,1)S(1)} %get-tuple-element.36.sides_ref, ...), custom_call_target="tpu_custom_call", output_to_operand_aliasing={{}: (0, {})} | custom-call | tf_op jit(solution)/shard_map/combine_pair/pallas_call | solution.py:553
  22.5 0.5 %collective-permute-done.4.received_ref = bf16[784,128]{1,0:T(8,128)(2,1)S(1)} collective-permute-done((bf16[784,128]{1,0:T(8,128)(2,1)S(1)}, bf16[784,128]{1,0:T(8,128)(2,1)S(1)}, u32[]{:S(2)}, u32[]{:S(2)}) %collective-permute-start.4) | collective-permute-done | bytes 200736 | tf_op jit(solution)/shard_map/ppermute | solution.py:533
  23.0 1.0 %combine_cross.1 = bf16[128,4,1024]{2,1,0:T(4,128)(2,1)} custom-call(bf16[128,4,1024]{2,1,0:T(4,128)(2,1)} %combine_pair.1.part_ref, bf16[2,1024,128]{2,1,0:T(8,128)(2,1)S(1)} %get-tuple-element.35.ends_ref, bf16[2,4,1024]{2,1,0:T(4,128)(2,1)S(1)} %get-tuple-element.36.sides_ref, ...), custom_call_target="tpu_custom_call", output_to_operand_aliasing={{}: (0, {})} | custom-call | tf_op jit(solution)/shard_map/combine_cross/pallas_call | solution.py:553
Async XLA Ops:
  2.1 7.3 %collective-permute-start.1 = (bf16[1024,128]{1,0:T(8,128)(2,1)S(1)}, bf16[1024,128]{1,0:T(8,128)(2,1)S(1)}, u32[]{:S(2)}, u32[]{:S(2)}) collective-permute-start(bf16[1024,128]{1,0:T(8,128)(2,1)S(1)} %get-tuple-element.24.after_ref), channel_id=1, source_target_pairs={{0,1},{1,2},{2,3},{3,0},{4,5},{5,6},{6,7},{7,4},{8,9},{9,10},{10,1... | collective-permute-start | bytes 786440 | tf_op jit(solution)/shard_map/ppermute | solution.py:484
  2.6 6.5 %collective-permute-start = (f32[64,128]{1,0:T(8,128)S(1)}, f32[64,128]{1,0:T(8,128)S(1)}, u32[]{:S(2)}, u32[]{:S(2)}) collective-permute-start(f32[64,128]{1,0:T(8,128)S(1)} %get-tuple-element.25.own_ref), channel_id=1, source_target_pairs={{0,4},{4,0},{8,12},{12,8},{16,20},{20,16},{24,28},{28,24},{1,5},{5... | collective-permute-start | bytes 98312 | tf_op jit(solution)/shard_map/ppermute | solution.py:485
  5.2 7.0 %collective-permute-start.2 = (f32[64,128]{1,0:T(8,128)S(1)}, f32[64,128]{1,0:T(8,128)S(1)}, u32[]{:S(2)}, u32[]{:S(2)}) collective-permute-start(f32[64,128]{1,0:T(8,128)S(1)} %get-tuple-element.30.own_ref), channel_id=1, source_target_pairs={{0,28},{4,8},{8,4},{12,16},{16,12},{20,24},{24,20},{28,0},{1,29},{... | collective-permute-start | bytes 98312 | tf_op jit(solution)/shard_map/ppermute | solution.py:486
  10.7 10.8 %collective-permute-start.3 = (bf16[784,128]{1,0:T(8,128)(2,1)S(1)}, bf16[784,128]{1,0:T(8,128)(2,1)S(1)}, u32[]{:S(2)}, u32[]{:S(2)}) collective-permute-start(bf16[784,128]{1,0:T(8,128)(2,1)S(1)} %remote_pair.1.after_ref.sent_ref), channel_id=1, source_target_pairs={{0,4},{4,0},{8,12},{12,8},{16,20},{20,16},{24,28},{28,24},{1,5},{5... | collective-permute-start | bytes 602120 | tf_op jit(solution)/shard_map/ppermute | solution.py:531
  13.6 9.4 %collective-permute-start.4 = (bf16[784,128]{1,0:T(8,128)(2,1)S(1)}, bf16[784,128]{1,0:T(8,128)(2,1)S(1)}, u32[]{:S(2)}, u32[]{:S(2)}) collective-permute-start(bf16[784,128]{1,0:T(8,128)(2,1)S(1)} %remote_cross.1.after_ref.sent_ref), channel_id=1, source_target_pairs={{0,28},{4,8},{8,4},{12,16},{16,12},{20,24},{24,20},{28,0},{1,29},{... | collective-permute-start | bytes 602120 | tf_op jit(solution)/shard_map/ppermute | solution.py:533

commit v5 on v4

--- a/solution.py
+++ b/solution.py
@@ -69,8 +69,7 @@
 
 def prepare_kernel(
     tracers_hbm, velocity_hbm, mass_hbm, source_hbm,
-    here_ref, lowest_ref, cross_ref, pair_ref, velocity_ref, mass_ref, source_ref,
-    tracers_ref, sems,
+    lowest_ref, cross_ref, pair_ref, tracers_ref, velocity_ref, mass_ref, source_ref, sems,
 ):
     elements, levels, columns = tracers_hbm.shape
     step = 256
@@ -80,7 +79,10 @@
             ((velocity_hbm, velocity_ref), (mass_hbm, mass_ref), (source_hbm, source_ref))
         )
     ]
-    copies.append(pltpu.make_async_copy(tracers_hbm, tracers_ref, sems.at[3]))
+    half = elements // 2
+    for n in range(2):
+        part = pl.ds(n * half, half)
+        copies.append(pltpu.make_async_copy(tracers_hbm.at[part], tracers_ref.at[part], sems.at[3 + n]))
     for copy in copies:
         copy.start()
     for copy in copies[:3]:
@@ -94,15 +96,17 @@
 
     pl.when(even)(lambda: both(cross_ref, pair_ref))
     pl.when(jnp.logical_not(even))(lambda: both(pair_ref, cross_ref))
-    order = interleave(levels, elements)
-    copies[3].wait()
-    x = tracers_ref[...].reshape(elements * levels, columns)
-    for n in range(0, columns, step):
-        y = lax.dot_general(
-            x[:, n : n + step], order, (((0,), (0,)), ((), ())), preferred_element_type=f32
-        ).astype(bf16)
-        here_ref[n : n + step, :] = y
-        lowest_ref[n : n + step, :] = y[:, (levels - 1) * elements :]
+    row = lax.broadcasted_iota(jnp.int32, (half * levels, elements), 0)
+    column = lax.broadcasted_iota(jnp.int32, (half * levels, elements), 1)
+    for n in range(2):
+        copies[3 + n].wait()
+        x = tracers_ref[n * half : (n + 1) * half].reshape(half * levels, columns)
+        pick = jnp.where(row + n * half * levels == column * levels + levels - 1, 1.0, 0.0).astype(bf16)
+        for c in range(0, columns, step):
+            y = lax.dot_general(
+                x[:, c : c + step], pick, (((0,), (0,)), ((), ())), preferred_element_type=f32
+            ).astype(bf16)
+            lowest_ref[c : c + step, n * half : (n + 1) * half] = y[:, n * half : (n + 1) * half]
 
 
 def pack(head, velocity_ref, mass_ref, source_ref, out_ref):
@@ -143,19 +147,44 @@
     return 1.0 / (1.0 + jnp.exp(-velocity_ref[2, :, k, :]))
 
 
-def lift_rest_kernel(here_ref, velocity_ref, out_ref):
-    _, nodes, levels, elements = velocity_ref.shape
-    tracers = here_ref.shape[0] // nodes
+def spread(tracers_ref, velocity_ref, top_ref, rest_ref, here_ref):
+    elements, levels, columns = tracers_ref.shape
+    nodes = velocity_ref.shape[1]
+    tracers = columns // nodes
+    order = interleave(levels, elements)
+    x = tracers_ref[...].reshape(elements * levels, columns)
+    step = 256
+    for n in range(0, columns, step):
+        here_ref[n : n + step, :] = lax.dot_general(
+            x[:, n : n + step], order, (((0,), (0,)), ((), ())), preferred_element_type=f32
+        ).astype(bf16)
+    top_ref[...] = here_ref[:, :elements]
     for k in range(1, levels):
         descent = descents(velocity_ref, k)
         for m in range(nodes):
             rows = slice(m * tracers, (m + 1) * tracers)
             here = here_ref[rows, k * elements : (k + 1) * elements]
             upper = here_ref[rows, (k - 1) * elements : k * elements]
-            out_ref[m, :, (k - 1) * elements : k * elements] = lift(here, upper, descent[m : m + 1])
-
-
-def lift_first_kernel(after_ref, here_ref, above_ref, velocity_ref, out_ref):
+            rest_ref[m, :, (k - 1) * elements : k * elements] = lift(here, upper, descent[m : m + 1])
+
+
+def spread_early_kernel(tracers_ref, velocity_ref, packet_ref, top_ref, rest_ref, sent_ref, here_ref):
+    sent_ref[...] = packet_ref[...]
+    pl.when(lax.axis_index("elem") == 0)(lambda: spread(tracers_ref, velocity_ref, top_ref, rest_ref, here_ref))
+
+
+def spread_kernel(tracers_ref, velocity_ref, early_top_ref, early_rest_ref, top_ref, rest_ref, here_ref):
+    early = lax.axis_index("elem") == 0
+
+    @pl.when(early)
+    def _():
+        top_ref[...] = early_top_ref[...]
+        rest_ref[...] = early_rest_ref[...]
+
+    pl.when(jnp.logical_not(early))(lambda: spread(tracers_ref, velocity_ref, top_ref, rest_ref, here_ref))
+
+
+def lift_first_kernel(after_ref, top_ref, above_ref, velocity_ref, out_ref):
     del after_ref
     _, nodes, _, elements = velocity_ref.shape
     tracers = above_ref.shape[0] // nodes
@@ -164,7 +193,7 @@
     for m in range(nodes):
         rows = slice(m * tracers, (m + 1) * tracers)
         upper = jnp.where(below_top, above_ref[rows, :].astype(f32), 0.0)
-        out_ref[m] = lift(here_ref[rows, 0:elements], upper, descent[m : m + 1])
+        out_ref[m] = lift(top_ref[rows, :], upper, descent[m : m + 1])
 
 
 def by_i(ref, first, nodes=16):
@@ -200,6 +229,20 @@
 def remote_kernel(pair, after_ref, *refs):
     del after_ref
     by_side(pair, remote, *refs)
+
+
+def weigh_remote_kernel(
+    pair, levels, after_ref, packet_ref, own_ref, first_ref, rest_ref,
+    out_ref, blocks_ref, edge_ref, weights_ref, extra_ref, chosen_ref,
+):
+    del after_ref
+    tables = (weights_ref, extra_ref, chosen_ref)
+
+    def both(ahead):
+        weigh(ahead, levels, packet_ref, own_ref, *tables)
+        remote(ahead, first_ref, rest_ref, *tables, out_ref, blocks_ref, edge_ref)
+
+    by_side(pair, both)
 
 
 def weigh(ahead, levels, packet_ref, own_ref, weights_ref, extra_ref, chosen_ref):
@@ -281,28 +324,41 @@
     place = lane % cap
     edge = place == (0 if ahead else cap - 1)
     chosen = chosen_ref[...]
-    for m in range(0, 16, 4):
-        x = first_ref[m : m + 4].reshape(4 * tracers, lanes_all)
-        y = jnp.dot(x, chosen[:lanes_all], preferred_element_type=f32)
-        x = rest_ref[m : m + 4].reshape(4 * tracers, (levels - 1) * lanes_all)
-        y += jnp.dot(x, chosen[lanes_all:], preferred_element_type=f32)
-        blocks_ref[m : m + 4] = y.reshape(4, tracers, 2 * lanes_all)
-
-    first = slice(0, lanes_all)
-    (own,) = interpolate(extra_ref, lambda m: blocks_ref[m, :, lanes_all:], (0,))
-    for j in range(4):
-        ends = interpolate(weights_ref, lambda m: blocks_ref[m, :, first], (j, 12 + j))
-        middle = interpolate(weights_ref, lambda m: blocks_ref[m, :, first], (4 + j, 8 + j))
-        own_here = pltpu.roll(own, ((0 if ahead else cap - 1) - j) % lanes_all, 1)
-        if ahead:
-            west = ends[0] + jnp.where(edge, own_here, pltpu.roll(ends[1], 1, 1))
-            values, far = (west, *middle), ends[1]
-        else:
-            east = ends[1] + jnp.where(edge, own_here, pltpu.roll(ends[0], lanes_all - 1, 1))
-            values, far = (*middle, east), ends[0]
-        for i, value in enumerate(values):
-            out_ref[(3 * j + i) * tracers : (3 * j + i + 1) * tracers, :] = value.astype(bf16)
-        edge_ref[j * tracers : (j + 1) * tracers, :] = far.astype(bf16)
+    lanes = slice(0, lanes_all)
+    half = tracers // 2
+
+    def fetch(n):
+        rows = slice(n * half, (n + 1) * half)
+        for m in range(0, 16, 8):
+            near = jnp.concatenate([first_ref[m : m + 8, rows, :], rest_ref[m : m + 8, rows, lanes]], axis=2)
+            far = rest_ref[m : m + 8, rows, lanes_all:]
+            y = jnp.dot(
+                near.reshape(8 * half, 2 * lanes_all), chosen[: 2 * lanes_all], preferred_element_type=f32
+            ) + jnp.dot(
+                far.reshape(8 * half, (levels - 2) * lanes_all), chosen[2 * lanes_all :], preferred_element_type=f32
+            )
+            blocks_ref[n, m : m + 8] = y.reshape(8, half, 2 * lanes_all)
+
+    fetch(0)
+    for n in range(2):
+        if n == 0:
+            fetch(1)
+        (own,) = interpolate(extra_ref, lambda m: blocks_ref[n, m, :, lanes_all:], (0,))
+        for j in range(4):
+            ends = interpolate(weights_ref, lambda m: blocks_ref[n, m, :, lanes], (j, 12 + j))
+            middle = interpolate(weights_ref, lambda m: blocks_ref[n, m, :, lanes], (4 + j, 8 + j))
+            own_here = pltpu.roll(own, ((0 if ahead else cap - 1) - j) % lanes_all, 1)
+            if ahead:
+                west = ends[0] + jnp.where(edge, own_here, pltpu.roll(ends[1], 1, 1))
+                values, far = (west, *middle), ends[1]
+            else:
+                east = ends[1] + jnp.where(edge, own_here, pltpu.roll(ends[0], lanes_all - 1, 1))
+                values, far = (*middle, east), ends[0]
+            for i, value in enumerate(values):
+                row = (3 * j + i) * tracers + n * half
+                out_ref[row : row + half, :] = value.astype(bf16)
+            row = j * tracers + n * half
+            edge_ref[row : row + half, :] = far.astype(bf16)
     row = lax.broadcasted_iota(jnp.int32, (8, lanes_all), 0)
     far_place = cap - 1 if ahead else 0
     pick = jnp.where(lane == row * cap + far_place, 1.0, 0.0).astype(bf16)
@@ -471,17 +527,26 @@
 
     packet = shape((PACKET, elements), f32)
     inputs = (tracers, velocity, node_mass, source)
-    here, lowest, cross_sent, pair_sent, velocity, node_mass, source = pl.pallas_call(
+    lowest, cross_sent, pair_sent, tracers, velocity, node_mass, source = pl.pallas_call(
         prepare_kernel,
-        out_shape=(shape((columns, lanes), bf16), shape((columns, elements), bf16), packet, packet)
-        + tuple(shape(x.shape, x.dtype) for x in inputs[1:]),
+        out_shape=(shape((columns, elements), bf16), packet, packet)
+        + tuple(shape(x.shape, x.dtype) for x in inputs),
         in_specs=[anywhere] * 4,
-        scratch_shapes=[pltpu.VMEM(tracers.shape, bf16), pltpu.SemaphoreType.DMA((4,))],
+        scratch_shapes=[pltpu.SemaphoreType.DMA((5,))],
         compiler_params=params(),
         name="prepare",
     )(*[pltpu.with_memory_space_constraint(x, pltpu.HBM) for x in inputs])
     blocks = lax.axis_size("lev")
     above = lax.ppermute(lowest, "lev", [(i, (i + 1) % blocks) for i in range(blocks)])
+    spread_out = (shape((columns, elements), bf16), shape((16, count, lanes - elements), bf16))
+    spread_scratch = [pltpu.VMEM((columns, lanes), bf16)]
+    *early, pair_sent = pl.pallas_call(
+        spread_early_kernel,
+        out_shape=spread_out + (packet,),
+        scratch_shapes=spread_scratch,
+        compiler_params=params(),
+        name="spread_early",
+    )(tracers, velocity, pair_sent)
     pair_packet = lax.ppermute(pair_sent, "elem", pairing)
     cross_packet = lax.ppermute(cross_sent, "elem", crossing)
     def weighed(pair, packet, own, after):
@@ -498,38 +563,46 @@
         )(after, packet, own)
 
     pair_weights = weighed(True, pair_packet, pair_sent, lowest)
-    rest = pl.pallas_call(
-        lift_rest_kernel,
-        out_shape=shape((16, count, lanes - elements), bf16),
+    top, rest = pl.pallas_call(
+        spread_kernel,
+        out_shape=spread_out,
+        scratch_shapes=spread_scratch,
         compiler_params=params(),
-        name="lift_rest",
-    )(here, velocity)
+        name="spread",
+    )(tracers, velocity, *early)
     first = pl.pallas_call(
         lift_first_kernel,
         out_shape=shape((16, count, elements), bf16),
         in_specs=[anywhere] + [vmem] * 3,
         compiler_params=params(),
         name="lift_first",
-    )(pair_weights[1], here, above, velocity)
+    )(pair_weights[1], top, above, velocity)
 
     far_rows = 8 * (4 * count // elements)
 
-    def contributions(pair, weights, after):
-        return pl.pallas_call(
-            functools.partial(remote_kernel, pair),
-            out_shape=shape((12 * count + far_rows, elements), bf16),
-            in_specs=[anywhere] + [vmem] * 5,
-            scratch_shapes=[
-                pltpu.VMEM((16, count, 2 * elements), f32),
-                pltpu.VMEM((4 * count, elements), bf16),
-            ],
-            compiler_params=params(),
-            name="remote_pair" if pair else "remote_cross",
-        )(after, first, rest, *weights)
-
-    pair_out = contributions(True, pair_weights, first)
+    message = shape((12 * count + far_rows, elements), bf16)
+    message_scratch = [pltpu.VMEM((2, 16, count // 2, 2 * elements), f32), pltpu.VMEM((4 * count, elements), bf16)]
+    pair_out = pl.pallas_call(
+        functools.partial(remote_kernel, True),
+        out_shape=message,
+        in_specs=[anywhere] + [vmem] * 5,
+        scratch_shapes=message_scratch,
+        compiler_params=params(),
+        name="remote_pair",
+    )(first, first, rest, *pair_weights)
     pair_in = lax.ppermute(pair_out, "elem", pairing)
-    cross_out = contributions(False, weighed(False, cross_packet, cross_sent, pair_out), pair_out)
+    cross_out = pl.pallas_call(
+        functools.partial(weigh_remote_kernel, False, levels),
+        out_shape=message,
+        in_specs=[anywhere] + [vmem] * 4,
+        scratch_shapes=message_scratch + [
+            pltpu.VMEM((16, 16, elements), f32),
+            pltpu.VMEM((16, 8, elements), f32),
+            pltpu.VMEM((lanes, 2 * elements), bf16),
+        ],
+        compiler_params=params(),
+        name="remote_cross",
+    )(pair_out, cross_packet, cross_sent, first, rest)
     cross_in = lax.ppermute(cross_out, "elem", crossing)
     result = shape((elements, levels, columns), bf16)
     part, ends, sides = pl.pallas_call(

time: 24.2 us -> 23.7 us (0.979)
  starting transfers between devices: 11.8 us -> 11.2 us
    ppermute x1, starting transfers between devices: 2.6 us -> 1.64 us  [on_device(): pair_packet = lax.ppermute(pair_sent, 'elem', pairing)]
    pallas_call x4 -> x5, Pallas kernels: 4.72 us -> 4.98 us  [the longest x1 1.89 us: on_device(): pl.pallas_call(prepare_kernel, out_shape=(shape((columns, elements), bf16...]
    ppermute x1, starting transfers between devices: 1.6 us -> 1.85 us  [on_device(): pair_in = lax.ppermute(pair_out, 'elem', pairing)]
  transfers between devices with their start and end apart: 5 -> 5, of which waited for: 1 -> 1; matrix products, arithmetic and copies ran while one was open for 0% -> 0% of each run, Pallas kernels for 35% -> 37%
where the time goes in v5:
time: 23.7 us; the launch traced here: 23.5 us
  Pallas kernels  11.6 us (49%)
  starting transfers between devices  11.2 us (47%)
  waiting for transfers between devices  0.65 us (3%)
    pallas_call x1, Pallas kernels, on_device(): pl.pallas_call(local_kernel, out_shape=(result, shape((2, columns, elemen...  4.26 us
    ppermute x1, starting transfers between devices, on_device(): cross_in = lax.ppermute(cross_out, 'elem', crossing)  3.61 us
    ppermute x1, starting transfers between devices, on_device(): cross_packet = lax.ppermute(cross_sent, 'elem', crossing)  3.55 us
    pallas_call x2, Pallas kernels, on_device(): pl.pallas_call(functools.partial(combine_kernel, pair), out_shape=result,...  2.04 us
    pallas_call x1, Pallas kernels, on_device(): pl.pallas_call(prepare_kernel, out_shape=(shape((columns, elements), bf16...  1.89 us
    ppermute x1, starting transfers between devices, on_device(): pair_in = lax.ppermute(pair_out, 'elem', pairing)  1.85 us
    ppermute x1, starting transfers between devices, on_device(): pair_packet = lax.ppermute(pair_sent, 'elem', pairing)  1.64 us
    pallas_call x1, Pallas kernels, on_device(): pl.pallas_call(functools.partial(weigh_remote_kernel, False, levels), out...  1.05 us
  transfers between devices with their start and end apart: 5, of which 1 were waited for; matrix products, arithmetic and copies ran while one was open for 0% of the time, Pallas kernels for 37%

profile of v5, /device:TPU:0, one launch (start us, length us, event | category | flops | bytes accessed | tf_op | source)
XLA Modules:
  0.0 23.5 jit_solution(6971590763527149128)
XLA Ops:
  0.0 1.9 %prepare.1 = (bf16[1024,128]{1,0:T(8,128)(2,1)S(1)}, f32[64,128]{1,0:T(8,128)S(1)}, f32[64,128]{1,0:T(8,128)S(1)}, bf16[128,4,1024]{2,1,0:T(4,128)(2,1)S(1)}, f3...) custom-call(bf16[128,4,1024]{2,1,0:T(4,128)(2,1)} %tracers_hbm.1, ...), custom_call_target="tpu_custom_call" | custom-call | tf_op jit(solution)/shard_map/prepare/pallas_call | solution.py:530
  1.9 0.5 %collective-permute-start.1 = (bf16[1024,128]{1,0:T(8,128)(2,1)S(1)}, bf16[1024,128]{1,0:T(8,128)(2,1)S(1)}, u32[]{:S(2)}, u32[]{:S(2)}) collective-permute-start(bf16[1024,128]{1,0:T(8,128)(2,1)S(1)} %get-tuple-element.26.after_ref), channel_id=1, source_target_pairs={{0,1},{1,2},{2,3},{3,0},{4,5},{5,6},{6,7},{7,4},{8,9},{9,10},{10,1... | collective-permute-start | bytes 786440 | tf_op jit(solution)/shard_map/ppermute | solution.py:540
  2.4 1.0 %spread_early.1 = (bf16[1024,128]{1,0:T(8,128)(2,1)S(1)}, bf16[16,64,384]{2,1,0:T(8,128)(2,1)S(1)}, f32[64,128]{1,0:T(8,128)S(1)}) custom-call(bf16[128,4,1024]{2,1,0:T(4,128)(2,1)S(1)} %get-tuple-element.27.tracers_ref, f32[3,16,4,128]{3,2,1,0:T(4,128)S(1)} %get-tuple-element.23.velocity_ref, f32[64,128]{1,0:T(8,128)S(1)} %get-tuple-element.28.packet_ref), custom_call_target="tpu_custom_call" | custom-call | tf_op jit(solution)/shard_map/spread_early/pallas_call | solution.py:543
  3.4 1.6 %collective-permute-start = (f32[64,128]{1,0:T(8,128)S(1)}, f32[64,128]{1,0:T(8,128)S(1)}, u32[]{:S(2)}, u32[]{:S(2)}) collective-permute-start(f32[64,128]{1,0:T(8,128)S(1)} %get-tuple-element.29.own_ref), channel_id=1, source_target_pairs={{0,4},{4,0},{8,12},{12,8},{16,20},{20,16},{24,28},{28,24},{1,5},{5... | collective-permute-start | bytes 98312 | tf_op jit(solution)/shard_map/ppermute | solution.py:550
  5.0 3.5 %collective-permute-start.2 = (f32[64,128]{1,0:T(8,128)S(1)}, f32[64,128]{1,0:T(8,128)S(1)}, u32[]{:S(2)}, u32[]{:S(2)}) collective-permute-start(f32[64,128]{1,0:T(8,128)S(1)} %get-tuple-element.37.own_ref), channel_id=1, source_target_pairs={{0,28},{4,8},{8,4},{12,16},{16,12},{20,24},{24,20},{28,0},{1,29},{... | collective-permute-start | bytes 98312 | tf_op jit(solution)/shard_map/ppermute | solution.py:551
  8.6 0.1 spread.1
  8.7 0.0 collective-permute-done.packet_ref
  8.7 0.2 weigh_pair.1
  8.9 0.0 collective-permute-done.1.above_ref
  8.9 0.1 lift_first.1.after_ref.refs_0_.first_ref
  9.1 1.0 %remote_pair.1.after_ref.sent_ref = bf16[784,128]{1,0:T(8,128)(2,1)S(1)} custom-call(bf16[16,64,128]{2,1,0:T(8,128)(2,1)S(1)} %lift_first.1.after_ref.refs_0_.first_ref, bf16[16,64,128]{2,1,0:T(8,128)(2,1)S(1)} %lift_first.1.after_ref.refs_0_.first_ref, bf16[16,64,384]{2,1,0:T(8,128)(2,1)S(1)} %get-tuple-element.34.refs_1_.rest_ref, ...), custom_call_target="tpu_custom_call" | custom-call | tf_op jit(solution)/shard_map/remote_pair/pallas_call | solution.py:585
  10.0 1.9 %collective-permute-start.3 = (bf16[784,128]{1,0:T(8,128)(2,1)S(1)}, bf16[784,128]{1,0:T(8,128)(2,1)S(1)}, u32[]{:S(2)}, u32[]{:S(2)}) collective-permute-start(bf16[784,128]{1,0:T(8,128)(2,1)S(1)} %remote_pair.1.after_ref.sent_ref), channel_id=1, source_target_pairs={{0,4},{4,0},{8,12},{12,8},{16,20},{20,16},{24,28},{28,24},{1,5},{5... | collective-permute-start | bytes 602120 | tf_op jit(solution)/shard_map/ppermute | solution.py:593
  11.9 0.0 collective-permute-done.2.packet_ref
  11.9 1.1 %remote_cross.1.after_ref.sent_ref = bf16[784,128]{1,0:T(8,128)(2,1)S(1)} custom-call(bf16[784,128]{1,0:T(8,128)(2,1)S(1)} %remote_pair.1.after_ref.sent_ref, f32[64,128]{1,0:T(8,128)S(1)} %collective-permute-done.2.packet_ref, f32[64,128]{1,0:T(8,128)S(1)} %get-tuple-element.37.own_ref, bf16[16,64,128]{2,1,0:T(8,128)(2,1)S(1)} %lift_first.1.after_ref.refs_0_.first_ref, ...), custom_call_target="tpu_custom_call" | custom-call | tf_op jit(solution)/shard_map/remote_cross/pallas_call | solution.py:594
  12.9 3.6 %collective-permute-start.4 = (bf16[784,128]{1,0:T(8,128)(2,1)S(1)}, bf16[784,128]{1,0:T(8,128)(2,1)S(1)}, u32[]{:S(2)}, u32[]{:S(2)}) collective-permute-start(bf16[784,128]{1,0:T(8,128)(2,1)S(1)} %remote_cross.1.after_ref.sent_ref), channel_id=1, source_target_pairs={{0,28},{4,8},{8,4},{12,16},{16,12},{20,24},{24,20},{28,0},{1,29},{... | collective-permute-start | bytes 602120 | tf_op jit(solution)/shard_map/ppermute | solution.py:606
  16.6 4.3 %local.1 = (bf16[128,4,1024]{2,1,0:T(4,128)(2,1)}, bf16[2,1024,128]{2,1,0:T(8,128)(2,1)S(1)}, bf16[2,4,1024]{2,1,0:T(4,128)(2,1)S(1)}) custom-call(f32[3,16,4,128]{3,2,1,0:T(4,128)S(1)} %get-tuple-element.23.velocity_ref, f32[16,128]{1,0:T(8,128)S(1)} %get-tuple-element.24.mass_ref, s32[1,128]{1,0:T(1,128)S(1)} %get-tuple-element.25.source_ref, ...), custom_call_target="tpu_custom_call" | custom-call | flops 99999997952 | bytes 1000000000 | tf_op jit(solution)/shard_map/local/pallas_call | solution.py:608
  20.8 0.0 collective-permute-done.3.received_ref
  20.8 1.0 %combine_pair.1.part_ref = bf16[128,4,1024]{2,1,0:T(4,128)(2,1)} custom-call(bf16[128,4,1024]{2,1,0:T(4,128)(2,1)} %get-tuple-element.38.part_ref, bf16[2,1024,128]{2,1,0:T(8,128)(2,1)S(1)} %get-tuple-element.39.ends_ref, bf16[2,4,1024]{2,1,0:T(4,128)(2,1)S(1)} %get-tuple-element.40.sides_ref, ...), custom_call_target="tpu_custom_call", output_to_operand_aliasing={{}: (0, {})} | custom-call | tf_op jit(solution)/shard_map/combine_pair/pallas_call | solution.py:626
  21.9 0.6 %collective-permute-done.4.received_ref = bf16[784,128]{1,0:T(8,128)(2,1)S(1)} collective-permute-done((bf16[784,128]{1,0:T(8,128)(2,1)S(1)}, bf16[784,128]{1,0:T(8,128)(2,1)S(1)}, u32[]{:S(2)}, u32[]{:S(2)}) %collective-permute-start.4) | collective-permute-done | bytes 200736 | tf_op jit(solution)/shard_map/ppermute | solution.py:606
  22.5 1.0 %combine_cross.1 = bf16[128,4,1024]{2,1,0:T(4,128)(2,1)} custom-call(bf16[128,4,1024]{2,1,0:T(4,128)(2,1)} %combine_pair.1.part_ref, bf16[2,1024,128]{2,1,0:T(8,128)(2,1)S(1)} %get-tuple-element.39.ends_ref, bf16[2,4,1024]{2,1,0:T(4,128)(2,1)S(1)} %get-tuple-element.40.sides_ref, ...), custom_call_target="tpu_custom_call", output_to_operand_aliasing={{}: (0, {})} | custom-call | tf_op jit(solution)/shard_map/combine_cross/pallas_call | solution.py:626
Async XLA Ops:
  1.9 7.0 %collective-permute-start.1 = (bf16[1024,128]{1,0:T(8,128)(2,1)S(1)}, bf16[1024,128]{1,0:T(8,128)(2,1)S(1)}, u32[]{:S(2)}, u32[]{:S(2)}) collective-permute-start(bf16[1024,128]{1,0:T(8,128)(2,1)S(1)} %get-tuple-element.26.after_ref), channel_id=1, source_target_pairs={{0,1},{1,2},{2,3},{3,0},{4,5},{5,6},{6,7},{7,4},{8,9},{9,10},{10,1... | collective-permute-start | bytes 786440 | tf_op jit(solution)/shard_map/ppermute | solution.py:540
  3.4 5.3 %collective-permute-start = (f32[64,128]{1,0:T(8,128)S(1)}, f32[64,128]{1,0:T(8,128)S(1)}, u32[]{:S(2)}, u32[]{:S(2)}) collective-permute-start(f32[64,128]{1,0:T(8,128)S(1)} %get-tuple-element.29.own_ref), channel_id=1, source_target_pairs={{0,4},{4,0},{8,12},{12,8},{16,20},{20,16},{24,28},{28,24},{1,5},{5... | collective-permute-start | bytes 98312 | tf_op jit(solution)/shard_map/ppermute | solution.py:550
  5.0 6.9 %collective-permute-start.2 = (f32[64,128]{1,0:T(8,128)S(1)}, f32[64,128]{1,0:T(8,128)S(1)}, u32[]{:S(2)}, u32[]{:S(2)}) collective-permute-start(f32[64,128]{1,0:T(8,128)S(1)} %get-tuple-element.37.own_ref), channel_id=1, source_target_pairs={{0,28},{4,8},{8,4},{12,16},{16,12},{20,24},{24,20},{28,0},{1,29},{... | collective-permute-start | bytes 98312 | tf_op jit(solution)/shard_map/ppermute | solution.py:551
  10.0 10.8 %collective-permute-start.3 = (bf16[784,128]{1,0:T(8,128)(2,1)S(1)}, bf16[784,128]{1,0:T(8,128)(2,1)S(1)}, u32[]{:S(2)}, u32[]{:S(2)}) collective-permute-start(bf16[784,128]{1,0:T(8,128)(2,1)S(1)} %remote_pair.1.after_ref.sent_ref), channel_id=1, source_target_pairs={{0,4},{4,0},{8,12},{12,8},{16,20},{20,16},{24,28},{28,24},{1,5},{5... | collective-permute-start | bytes 602120 | tf_op jit(solution)/shard_map/ppermute | solution.py:593
  12.9 9.6 %collective-permute-start.4 = (bf16[784,128]{1,0:T(8,128)(2,1)S(1)}, bf16[784,128]{1,0:T(8,128)(2,1)S(1)}, u32[]{:S(2)}, u32[]{:S(2)}) collective-permute-start(bf16[784,128]{1,0:T(8,128)(2,1)S(1)} %remote_cross.1.after_ref.sent_ref), channel_id=1, source_target_pairs={{0,28},{4,8},{8,4},{12,16},{16,12},{20,24},{24,20},{28,0},{1,29},{... | collective-permute-start | bytes 602120 | tf_op jit(solution)/shard_map/ppermute | solution.py:606

commit v6 on v5

--- a/solution.py
+++ b/solution.py
@@ -69,7 +69,7 @@
 
 def prepare_kernel(
     tracers_hbm, velocity_hbm, mass_hbm, source_hbm,
-    lowest_ref, cross_ref, pair_ref, tracers_ref, velocity_ref, mass_ref, source_ref, sems,
+    lowest_ref, cross_ref, pair_ref, tracers_ref, velocity_ref, mass_ref, source_ref, pair_of_levels_ref, sems,
 ):
     elements, levels, columns = tracers_hbm.shape
     step = 256
@@ -79,10 +79,8 @@
             ((velocity_hbm, velocity_ref), (mass_hbm, mass_ref), (source_hbm, source_ref))
         )
     ]
-    half = elements // 2
-    for n in range(2):
-        part = pl.ds(n * half, half)
-        copies.append(pltpu.make_async_copy(tracers_hbm.at[part], tracers_ref.at[part], sems.at[3 + n]))
+    copies.append(pltpu.make_async_copy(tracers_hbm.at[:, pl.ds(levels - 2, 2), :], pair_of_levels_ref, sems.at[3]))
+    copies.append(pltpu.make_async_copy(tracers_hbm, tracers_ref, sems.at[4]))
     for copy in copies:
         copy.start()
     for copy in copies[:3]:
@@ -96,17 +94,16 @@
 
     pl.when(even)(lambda: both(cross_ref, pair_ref))
     pl.when(jnp.logical_not(even))(lambda: both(pair_ref, cross_ref))
-    row = lax.broadcasted_iota(jnp.int32, (half * levels, elements), 0)
-    column = lax.broadcasted_iota(jnp.int32, (half * levels, elements), 1)
-    for n in range(2):
-        copies[3 + n].wait()
-        x = tracers_ref[n * half : (n + 1) * half].reshape(half * levels, columns)
-        pick = jnp.where(row + n * half * levels == column * levels + levels - 1, 1.0, 0.0).astype(bf16)
-        for c in range(0, columns, step):
-            y = lax.dot_general(
-                x[:, c : c + step], pick, (((0,), (0,)), ((), ())), preferred_element_type=f32
-            ).astype(bf16)
-            lowest_ref[c : c + step, n * half : (n + 1) * half] = y[:, n * half : (n + 1) * half]
+    copies[3].wait()
+    row = lax.broadcasted_iota(jnp.int32, (2 * elements, elements), 0)
+    column = lax.broadcasted_iota(jnp.int32, (2 * elements, elements), 1)
+    pick = jnp.where(row == column * 2 + 1, 1.0, 0.0).astype(bf16)
+    x = pair_of_levels_ref[...].reshape(2 * elements, columns)
+    for c in range(0, columns, step):
+        lowest_ref[c : c + step, :] = lax.dot_general(
+            x[:, c : c + step], pick, (((0,), (0,)), ((), ())), preferred_element_type=f32
+        ).astype(bf16)
+    copies[4].wait()
 
 
 def pack(head, velocity_ref, mass_ref, source_ref, out_ref):
@@ -532,7 +529,7 @@
         out_shape=(shape((columns, elements), bf16), packet, packet)
         + tuple(shape(x.shape, x.dtype) for x in inputs),
         in_specs=[anywhere] * 4,
-        scratch_shapes=[pltpu.SemaphoreType.DMA((5,))],
+        scratch_shapes=[pltpu.VMEM((elements, 2, columns), bf16), pltpu.SemaphoreType.DMA((5,))],
         compiler_params=params(),
         name="prepare",
     )(*[pltpu.with_memory_space_constraint(x, pltpu.HBM) for x in inputs])

time: 23.7 us -> 23.3 us (0.983)
  Pallas kernels: 11.6 us -> 11.3 us
    pallas_call x1, Pallas kernels: 1.89 us -> 1.53 us  [on_device(): pl.pallas_call(prepare_kernel, out_shape=(shape((columns, elements), bf16...]
  transfers between devices with their start and end apart: 5 -> 5, of which waited for: 1 -> 1; matrix products, arithmetic and copies ran while one was open for 0% -> 0% of each run, Pallas kernels for 37% -> 38%
where the time goes in v6:
time: 23.3 us; the launch traced here: 23.2 us
  Pallas kernels  11.3 us (48%)
  starting transfers between devices  11.2 us (48%)
  waiting for transfers between devices  0.66 us (3%)
    pallas_call x1, Pallas kernels, on_device(): pl.pallas_call(local_kernel, out_shape=(result, shape((2, columns, elemen...  4.27 us
    ppermute x1, starting transfers between devices, on_device(): cross_in = lax.ppermute(cross_out, 'elem', crossing)  3.61 us
    ppermute x1, starting transfers between devices, on_device(): cross_packet = lax.ppermute(cross_sent, 'elem', crossing)  3.55 us
    pallas_call x2, Pallas kernels, on_device(): pl.pallas_call(functools.partial(combine_kernel, pair), out_shape=result,...  2.04 us
    ppermute x1, starting transfers between devices, on_device(): pair_in = lax.ppermute(pair_out, 'elem', pairing)  1.85 us
    ppermute x1, starting transfers between devices, on_device(): pair_packet = lax.ppermute(pair_sent, 'elem', pairing)  1.66 us
    pallas_call x1, Pallas kernels, on_device(): pl.pallas_call(prepare_kernel, out_shape=(shape((columns, elements), bf16...  1.53 us
    pallas_call x1, Pallas kernels, on_device(): pl.pallas_call(functools.partial(weigh_remote_kernel, False, levels), out...  1.05 us
  transfers between devices with their start and end apart: 5, of which 1 were waited for; matrix products, arithmetic and copies ran while one was open for 0% of the time, Pallas kernels for 38%

profile of v6, /device:TPU:0, one launch (start us, length us, event | category | flops | bytes accessed | tf_op | source)
XLA Modules:
  0.0 23.2 jit_solution(11145159452793680464)
XLA Ops:
  0.0 1.5 %prepare.1 = (bf16[1024,128]{1,0:T(8,128)(2,1)S(1)}, f32[64,128]{1,0:T(8,128)S(1)}, f32[64,128]{1,0:T(8,128)S(1)}, bf16[128,4,1024]{2,1,0:T(4,128)(2,1)S(1)}, f3...) custom-call(bf16[128,4,1024]{2,1,0:T(4,128)(2,1)} %tracers_hbm.1, ...), custom_call_target="tpu_custom_call" | custom-call | tf_op jit(solution)/shard_map/prepare/pallas_call | solution.py:527
  1.5 0.5 %collective-permute-start.1 = (bf16[1024,128]{1,0:T(8,128)(2,1)S(1)}, bf16[1024,128]{1,0:T(8,128)(2,1)S(1)}, u32[]{:S(2)}, u32[]{:S(2)}) collective-permute-start(bf16[1024,128]{1,0:T(8,128)(2,1)S(1)} %get-tuple-element.26.after_ref), channel_id=1, source_target_pairs={{0,1},{1,2},{2,3},{3,0},{4,5},{5,6},{6,7},{7,4},{8,9},{9,10},{10,1... | collective-permute-start | bytes 786440 | tf_op jit(solution)/shard_map/ppermute | solution.py:537
  2.0 1.0 %spread_early.1 = (bf16[1024,128]{1,0:T(8,128)(2,1)S(1)}, bf16[16,64,384]{2,1,0:T(8,128)(2,1)S(1)}, f32[64,128]{1,0:T(8,128)S(1)}) custom-call(bf16[128,4,1024]{2,1,0:T(4,128)(2,1)S(1)} %get-tuple-element.27.tracers_ref, f32[3,16,4,128]{3,2,1,0:T(4,128)S(1)} %get-tuple-element.23.velocity_ref, f32[64,128]{1,0:T(8,128)S(1)} %get-tuple-element.28.packet_ref), custom_call_target="tpu_custom_call" | custom-call | tf_op jit(solution)/shard_map/spread_early/pallas_call | solution.py:540
  3.0 1.7 %collective-permute-start = (f32[64,128]{1,0:T(8,128)S(1)}, f32[64,128]{1,0:T(8,128)S(1)}, u32[]{:S(2)}, u32[]{:S(2)}) collective-permute-start(f32[64,128]{1,0:T(8,128)S(1)} %get-tuple-element.29.own_ref), channel_id=1, source_target_pairs={{0,4},{4,0},{8,12},{12,8},{16,20},{20,16},{24,28},{28,24},{1,5},{5... | collective-permute-start | bytes 98312 | tf_op jit(solution)/shard_map/ppermute | solution.py:547
  4.7 3.5 %collective-permute-start.2 = (f32[64,128]{1,0:T(8,128)S(1)}, f32[64,128]{1,0:T(8,128)S(1)}, u32[]{:S(2)}, u32[]{:S(2)}) collective-permute-start(f32[64,128]{1,0:T(8,128)S(1)} %get-tuple-element.37.own_ref), channel_id=1, source_target_pairs={{0,28},{4,8},{8,4},{12,16},{16,12},{20,24},{24,20},{28,0},{1,29},{... | collective-permute-start | bytes 98312 | tf_op jit(solution)/shard_map/ppermute | solution.py:548
  8.2 0.1 spread.1
  8.3 0.0 collective-permute-done.packet_ref
  8.3 0.2 weigh_pair.1
  8.5 0.0 collective-permute-done.1.above_ref
  8.6 0.1 lift_first.1.after_ref.refs_0_.first_ref
  8.7 1.0 %remote_pair.1.after_ref.sent_ref = bf16[784,128]{1,0:T(8,128)(2,1)S(1)} custom-call(bf16[16,64,128]{2,1,0:T(8,128)(2,1)S(1)} %lift_first.1.after_ref.refs_0_.first_ref, bf16[16,64,128]{2,1,0:T(8,128)(2,1)S(1)} %lift_first.1.after_ref.refs_0_.first_ref, bf16[16,64,384]{2,1,0:T(8,128)(2,1)S(1)} %get-tuple-element.34.refs_1_.rest_ref, ...), custom_call_target="tpu_custom_call" | custom-call | tf_op jit(solution)/shard_map/remote_pair/pallas_call | solution.py:582
  9.7 1.9 %collective-permute-start.3 = (bf16[784,128]{1,0:T(8,128)(2,1)S(1)}, bf16[784,128]{1,0:T(8,128)(2,1)S(1)}, u32[]{:S(2)}, u32[]{:S(2)}) collective-permute-start(bf16[784,128]{1,0:T(8,128)(2,1)S(1)} %remote_pair.1.after_ref.sent_ref), channel_id=1, source_target_pairs={{0,4},{4,0},{8,12},{12,8},{16,20},{20,16},{24,28},{28,24},{1,5},{5... | collective-permute-start | bytes 602120 | tf_op jit(solution)/shard_map/ppermute | solution.py:590
  11.5 0.0 collective-permute-done.2.packet_ref
  11.5 1.1 %remote_cross.1.after_ref.sent_ref = bf16[784,128]{1,0:T(8,128)(2,1)S(1)} custom-call(bf16[784,128]{1,0:T(8,128)(2,1)S(1)} %remote_pair.1.after_ref.sent_ref, f32[64,128]{1,0:T(8,128)S(1)} %collective-permute-done.2.packet_ref, f32[64,128]{1,0:T(8,128)S(1)} %get-tuple-element.37.own_ref, bf16[16,64,128]{2,1,0:T(8,128)(2,1)S(1)} %lift_first.1.after_ref.refs_0_.first_ref, ...), custom_call_target="tpu_custom_call" | custom-call | tf_op jit(solution)/shard_map/remote_cross/pallas_call | solution.py:591
  12.6 3.6 %collective-permute-start.4 = (bf16[784,128]{1,0:T(8,128)(2,1)S(1)}, bf16[784,128]{1,0:T(8,128)(2,1)S(1)}, u32[]{:S(2)}, u32[]{:S(2)}) collective-permute-start(bf16[784,128]{1,0:T(8,128)(2,1)S(1)} %remote_cross.1.after_ref.sent_ref), channel_id=1, source_target_pairs={{0,28},{4,8},{8,4},{12,16},{16,12},{20,24},{24,20},{28,0},{1,29},{... | collective-permute-start | bytes 602120 | tf_op jit(solution)/shard_map/ppermute | solution.py:603
  16.2 4.3 %local.1 = (bf16[128,4,1024]{2,1,0:T(4,128)(2,1)}, bf16[2,1024,128]{2,1,0:T(8,128)(2,1)S(1)}, bf16[2,4,1024]{2,1,0:T(4,128)(2,1)S(1)}) custom-call(f32[3,16,4,128]{3,2,1,0:T(4,128)S(1)} %get-tuple-element.23.velocity_ref, f32[16,128]{1,0:T(8,128)S(1)} %get-tuple-element.24.mass_ref, s32[1,128]{1,0:T(1,128)S(1)} %get-tuple-element.25.source_ref, ...), custom_call_target="tpu_custom_call" | custom-call | flops 99999997952 | bytes 1000000000 | tf_op jit(solution)/shard_map/local/pallas_call | solution.py:605
  20.5 0.0 collective-permute-done.3.received_ref
  20.5 1.0 %combine_pair.1.part_ref = bf16[128,4,1024]{2,1,0:T(4,128)(2,1)} custom-call(bf16[128,4,1024]{2,1,0:T(4,128)(2,1)} %get-tuple-element.38.part_ref, bf16[2,1024,128]{2,1,0:T(8,128)(2,1)S(1)} %get-tuple-element.39.ends_ref, bf16[2,4,1024]{2,1,0:T(4,128)(2,1)S(1)} %get-tuple-element.40.sides_ref, ...), custom_call_target="tpu_custom_call", output_to_operand_aliasing={{}: (0, {})} | custom-call | tf_op jit(solution)/shard_map/combine_pair/pallas_call | solution.py:623
  21.5 0.6 %collective-permute-done.4.received_ref = bf16[784,128]{1,0:T(8,128)(2,1)S(1)} collective-permute-done((bf16[784,128]{1,0:T(8,128)(2,1)S(1)}, bf16[784,128]{1,0:T(8,128)(2,1)S(1)}, u32[]{:S(2)}, u32[]{:S(2)}) %collective-permute-start.4) | collective-permute-done | bytes 200736 | tf_op jit(solution)/shard_map/ppermute | solution.py:603
  22.2 1.0 %combine_cross.1 = bf16[128,4,1024]{2,1,0:T(4,128)(2,1)} custom-call(bf16[128,4,1024]{2,1,0:T(4,128)(2,1)} %combine_pair.1.part_ref, bf16[2,1024,128]{2,1,0:T(8,128)(2,1)S(1)} %get-tuple-element.39.ends_ref, bf16[2,4,1024]{2,1,0:T(4,128)(2,1)S(1)} %get-tuple-element.40.sides_ref, ...), custom_call_target="tpu_custom_call", output_to_operand_aliasing={{}: (0, {})} | custom-call | tf_op jit(solution)/shard_map/combine_cross/pallas_call | solution.py:623
Async XLA Ops:
  1.5 7.0 %collective-permute-start.1 = (bf16[1024,128]{1,0:T(8,128)(2,1)S(1)}, bf16[1024,128]{1,0:T(8,128)(2,1)S(1)}, u32[]{:S(2)}, u32[]{:S(2)}) collective-permute-start(bf16[1024,128]{1,0:T(8,128)(2,1)S(1)} %get-tuple-element.26.after_ref), channel_id=1, source_target_pairs={{0,1},{1,2},{2,3},{3,0},{4,5},{5,6},{6,7},{7,4},{8,9},{9,10},{10,1... | collective-permute-start | bytes 786440 | tf_op jit(solution)/shard_map/ppermute | solution.py:537
  3.0 5.3 %collective-permute-start = (f32[64,128]{1,0:T(8,128)S(1)}, f32[64,128]{1,0:T(8,128)S(1)}, u32[]{:S(2)}, u32[]{:S(2)}) collective-permute-start(f32[64,128]{1,0:T(8,128)S(1)} %get-tuple-element.29.own_ref), channel_id=1, source_target_pairs={{0,4},{4,0},{8,12},{12,8},{16,20},{20,16},{24,28},{28,24},{1,5},{5... | collective-permute-start | bytes 98312 | tf_op jit(solution)/shard_map/ppermute | solution.py:547
  4.7 6.9 %collective-permute-start.2 = (f32[64,128]{1,0:T(8,128)S(1)}, f32[64,128]{1,0:T(8,128)S(1)}, u32[]{:S(2)}, u32[]{:S(2)}) collective-permute-start(f32[64,128]{1,0:T(8,128)S(1)} %get-tuple-element.37.own_ref), channel_id=1, source_target_pairs={{0,28},{4,8},{8,4},{12,16},{16,12},{20,24},{24,20},{28,0},{1,29},{... | collective-permute-start | bytes 98312 | tf_op jit(solution)/shard_map/ppermute | solution.py:548
  9.7 10.8 %collective-permute-start.3 = (bf16[784,128]{1,0:T(8,128)(2,1)S(1)}, bf16[784,128]{1,0:T(8,128)(2,1)S(1)}, u32[]{:S(2)}, u32[]{:S(2)}) collective-permute-start(bf16[784,128]{1,0:T(8,128)(2,1)S(1)} %remote_pair.1.after_ref.sent_ref), channel_id=1, source_target_pairs={{0,4},{4,0},{8,12},{12,8},{16,20},{20,16},{24,28},{28,24},{1,5},{5... | collective-permute-start | bytes 602120 | tf_op jit(solution)/shard_map/ppermute | solution.py:590
  12.6 9.6 %collective-permute-start.4 = (bf16[784,128]{1,0:T(8,128)(2,1)S(1)}, bf16[784,128]{1,0:T(8,128)(2,1)S(1)}, u32[]{:S(2)}, u32[]{:S(2)}) collective-permute-start(bf16[784,128]{1,0:T(8,128)(2,1)S(1)} %remote_cross.1.after_ref.sent_ref), channel_id=1, source_target_pairs={{0,28},{4,8},{8,4},{12,16},{16,12},{20,24},{24,20},{28,0},{1,29},{... | collective-permute-start | bytes 602120 | tf_op jit(solution)/shard_map/ppermute | solution.py:603

commit v7 on v6

--- a/solution.py
+++ b/solution.py
@@ -55,12 +55,15 @@
     return out
 
 
-def table(winds, coefficient):
+def table(winds):
     rows, lanes = winds[0].shape
     along = basis(node_rows(rows, lanes, True) - courant * winds[0])
-    across_position = node_rows(rows, lanes, False) - courant * winds[1]
-    across = [factor * coefficient for factor in basis(across_position)]
+    across = basis(node_rows(rows, lanes, False) - courant * winds[1])
     return along, across
+
+
+def weight(along, across, share):
+    return (along * across).astype(bf16).astype(f32) * share
 
 
 def is_even():
@@ -280,10 +283,11 @@
         winds.append(jnp.concatenate([west, wind[1], wind[2], east], axis=0))
         edge_winds.append(west if ahead else east)
     ones = jnp.ones((8, lanes_all), f32)
-    along, across = table(winds, jnp.concatenate([share_west, ones, share_east], axis=0))
+    along, across = table(winds)
+    share = jnp.concatenate([share_west, ones, share_east], axis=0)
     for b in range(4):
         for a in range(4):
-            weights_ref[4 * b + a] = along[a] * across[b]
+            weights_ref[4 * b + a] = weight(along[a], across[b], share)
     at = 0 if ahead else cap - 1
 
     def spread(rows):
@@ -295,10 +299,10 @@
     edge_share = spread(1.0 - (share_west if ahead else share_east))
     node = jnp.where(place < 2, jnp.where(place == 0, *gll_points[:2]), jnp.where(place == 2, *gll_points[2:]))
     extra_along = basis(gll_points[3 if ahead else 0] - courant * spread(edge_winds[0]))
-    extra_across = [factor * edge_share for factor in basis(node - courant * spread(edge_winds[1]))]
+    extra_across = basis(node - courant * spread(edge_winds[1]))
     for b in range(4):
         for a in range(4):
-            extra_ref[4 * b + a, 0:1] = extra_along[a] * extra_across[b]
+            extra_ref[4 * b + a, 0:1] = weight(extra_along[a], extra_across[b], edge_share)
 
     source = packet_ref[SOURCE : SOURCE + 1, :].astype(jnp.int32)
     own_source = jnp.where(lane == (cap - 1 if ahead else 0), own_ref[SOURCE : SOURCE + 1, :], 0.0)
@@ -399,10 +403,10 @@
             west = shared(mass_before, pltpu.roll(wind[3], 1, 1), mass[0], wind[0])
             east = shared(mass[3], wind[3], mass_after, pltpu.roll(wind[0], elements - 1, 1))
             winds.append(jnp.concatenate([west, wind[1], wind[2], east], axis=0))
-        along, across = table(winds, coefficient)
+        along, across = table(winds)
         for b in range(4):
             for a in range(4):
-                weights_ref[k % 2, 4 * b + a] = along[a] * across[b]
+                weights_ref[k % 2, 4 * b + a] = weight(along[a], across[b], coefficient)
         if k + 1 < levels:
             fetch(k + 1)
         lanes = slice(k * elements, (k + 1) * elements)

time: 23.3 us -> 23.3 us (level)
  no operation moved by 1% of the time
where the time goes in v7:
time: 23.3 us; the launch traced here: 23.2 us
  Pallas kernels  11.3 us (48%)
  starting transfers between devices  11.2 us (48%)
  waiting for transfers between devices  0.61 us (3%)
    pallas_call x1, Pallas kernels, on_device(): pl.pallas_call(local_kernel, out_shape=(result, shape((2, columns, elemen...  4.31 us
    ppermute x1, starting transfers between devices, on_device(): cross_in = lax.ppermute(cross_out, 'elem', crossing)  3.62 us
    ppermute x1, starting transfers between devices, on_device(): cross_packet = lax.ppermute(cross_sent, 'elem', crossing)  3.55 us
    pallas_call x2, Pallas kernels, on_device(): pl.pallas_call(functools.partial(combine_kernel, pair), out_shape=result,...  2.04 us
    ppermute x1, starting transfers between devices, on_device(): pair_in = lax.ppermute(pair_out, 'elem', pairing)  1.85 us
    ppermute x1, starting transfers between devices, on_device(): pair_packet = lax.ppermute(pair_sent, 'elem', pairing)  1.66 us
    pallas_call x1, Pallas kernels, on_device(): pl.pallas_call(prepare_kernel, out_shape=(shape((columns, elements), bf16...  1.53 us
    pallas_call x1, Pallas kernels, on_device(): pl.pallas_call(functools.partial(weigh_remote_kernel, False, levels), out...  1.06 us
  transfers between devices with their start and end apart: 5, of which 1 were waited for; matrix products, arithmetic and copies ran while one was open for 0% of the time, Pallas kernels for 38%

profile of v7, /device:TPU:0, one launch (start us, length us, event | category | flops | bytes accessed | tf_op | source)
XLA Modules:
  0.0 23.2 jit_solution(5244598162439827895)
XLA Ops:
  0.0 1.5 %prepare.1 = (bf16[1024,128]{1,0:T(8,128)(2,1)S(1)}, f32[64,128]{1,0:T(8,128)S(1)}, f32[64,128]{1,0:T(8,128)S(1)}, bf16[128,4,1024]{2,1,0:T(4,128)(2,1)S(1)}, f3...) custom-call(bf16[128,4,1024]{2,1,0:T(4,128)(2,1)} %tracers_hbm.1, ...), custom_call_target="tpu_custom_call" | custom-call | tf_op jit(solution)/shard_map/prepare/pallas_call | solution.py:531
  1.5 0.5 %collective-permute-start.1 = (bf16[1024,128]{1,0:T(8,128)(2,1)S(1)}, bf16[1024,128]{1,0:T(8,128)(2,1)S(1)}, u32[]{:S(2)}, u32[]{:S(2)}) collective-permute-start(bf16[1024,128]{1,0:T(8,128)(2,1)S(1)} %get-tuple-element.26.after_ref), channel_id=1, source_target_pairs={{0,1},{1,2},{2,3},{3,0},{4,5},{5,6},{6,7},{7,4},{8,9},{9,10},{10,1... | collective-permute-start | bytes 786440 | tf_op jit(solution)/shard_map/ppermute | solution.py:541
  2.0 1.0 %spread_early.1 = (bf16[1024,128]{1,0:T(8,128)(2,1)S(1)}, bf16[16,64,384]{2,1,0:T(8,128)(2,1)S(1)}, f32[64,128]{1,0:T(8,128)S(1)}) custom-call(bf16[128,4,1024]{2,1,0:T(4,128)(2,1)S(1)} %get-tuple-element.27.tracers_ref, f32[3,16,4,128]{3,2,1,0:T(4,128)S(1)} %get-tuple-element.23.velocity_ref, f32[64,128]{1,0:T(8,128)S(1)} %get-tuple-element.28.packet_ref), custom_call_target="tpu_custom_call" | custom-call | tf_op jit(solution)/shard_map/spread_early/pallas_call | solution.py:544
  3.0 1.7 %collective-permute-start = (f32[64,128]{1,0:T(8,128)S(1)}, f32[64,128]{1,0:T(8,128)S(1)}, u32[]{:S(2)}, u32[]{:S(2)}) collective-permute-start(f32[64,128]{1,0:T(8,128)S(1)} %get-tuple-element.29.own_ref), channel_id=1, source_target_pairs={{0,4},{4,0},{8,12},{12,8},{16,20},{20,16},{24,28},{28,24},{1,5},{5... | collective-permute-start | bytes 98312 | tf_op jit(solution)/shard_map/ppermute | solution.py:551
  4.7 3.5 %collective-permute-start.2 = (f32[64,128]{1,0:T(8,128)S(1)}, f32[64,128]{1,0:T(8,128)S(1)}, u32[]{:S(2)}, u32[]{:S(2)}) collective-permute-start(f32[64,128]{1,0:T(8,128)S(1)} %get-tuple-element.37.own_ref), channel_id=1, source_target_pairs={{0,28},{4,8},{8,4},{12,16},{16,12},{20,24},{24,20},{28,0},{1,29},{... | collective-permute-start | bytes 98312 | tf_op jit(solution)/shard_map/ppermute | solution.py:552
  8.2 0.1 spread.1
  8.3 0.0 collective-permute-done.packet_ref
  8.3 0.2 weigh_pair.1
  8.5 0.0 collective-permute-done.1.above_ref
  8.6 0.1 lift_first.1.after_ref.refs_0_.first_ref
  8.7 1.0 %remote_pair.1.after_ref.sent_ref = bf16[784,128]{1,0:T(8,128)(2,1)S(1)} custom-call(bf16[16,64,128]{2,1,0:T(8,128)(2,1)S(1)} %lift_first.1.after_ref.refs_0_.first_ref, bf16[16,64,128]{2,1,0:T(8,128)(2,1)S(1)} %lift_first.1.after_ref.refs_0_.first_ref, bf16[16,64,384]{2,1,0:T(8,128)(2,1)S(1)} %get-tuple-element.34.refs_1_.rest_ref, ...), custom_call_target="tpu_custom_call" | custom-call | tf_op jit(solution)/shard_map/remote_pair/pallas_call | solution.py:586
  9.7 1.8 %collective-permute-start.3 = (bf16[784,128]{1,0:T(8,128)(2,1)S(1)}, bf16[784,128]{1,0:T(8,128)(2,1)S(1)}, u32[]{:S(2)}, u32[]{:S(2)}) collective-permute-start(bf16[784,128]{1,0:T(8,128)(2,1)S(1)} %remote_pair.1.after_ref.sent_ref), channel_id=1, source_target_pairs={{0,4},{4,0},{8,12},{12,8},{16,20},{20,16},{24,28},{28,24},{1,5},{5... | collective-permute-start | bytes 602120 | tf_op jit(solution)/shard_map/ppermute | solution.py:594
  11.5 0.0 collective-permute-done.2.packet_ref
  11.5 1.1 %remote_cross.1.after_ref.sent_ref = bf16[784,128]{1,0:T(8,128)(2,1)S(1)} custom-call(bf16[784,128]{1,0:T(8,128)(2,1)S(1)} %remote_pair.1.after_ref.sent_ref, f32[64,128]{1,0:T(8,128)S(1)} %collective-permute-done.2.packet_ref, f32[64,128]{1,0:T(8,128)S(1)} %get-tuple-element.37.own_ref, bf16[16,64,128]{2,1,0:T(8,128)(2,1)S(1)} %lift_first.1.after_ref.refs_0_.first_ref, ...), custom_call_target="tpu_custom_call" | custom-call | tf_op jit(solution)/shard_map/remote_cross/pallas_call | solution.py:595
  12.6 3.6 %collective-permute-start.4 = (bf16[784,128]{1,0:T(8,128)(2,1)S(1)}, bf16[784,128]{1,0:T(8,128)(2,1)S(1)}, u32[]{:S(2)}, u32[]{:S(2)}) collective-permute-start(bf16[784,128]{1,0:T(8,128)(2,1)S(1)} %remote_cross.1.after_ref.sent_ref), channel_id=1, source_target_pairs={{0,28},{4,8},{8,4},{12,16},{16,12},{20,24},{24,20},{28,0},{1,29},{... | collective-permute-start | bytes 602120 | tf_op jit(solution)/shard_map/ppermute | solution.py:607
  16.2 4.3 %local.1 = (bf16[128,4,1024]{2,1,0:T(4,128)(2,1)}, bf16[2,1024,128]{2,1,0:T(8,128)(2,1)S(1)}, bf16[2,4,1024]{2,1,0:T(4,128)(2,1)S(1)}) custom-call(f32[3,16,4,128]{3,2,1,0:T(4,128)S(1)} %get-tuple-element.23.velocity_ref, f32[16,128]{1,0:T(8,128)S(1)} %get-tuple-element.24.mass_ref, s32[1,128]{1,0:T(1,128)S(1)} %get-tuple-element.25.source_ref, ...), custom_call_target="tpu_custom_call" | custom-call | flops 99999997952 | bytes 1000000000 | tf_op jit(solution)/shard_map/local/pallas_call | solution.py:609
  20.5 0.0 collective-permute-done.3.received_ref
  20.5 1.0 %combine_pair.1.part_ref = bf16[128,4,1024]{2,1,0:T(4,128)(2,1)} custom-call(bf16[128,4,1024]{2,1,0:T(4,128)(2,1)} %get-tuple-element.38.part_ref, bf16[2,1024,128]{2,1,0:T(8,128)(2,1)S(1)} %get-tuple-element.39.ends_ref, bf16[2,4,1024]{2,1,0:T(4,128)(2,1)S(1)} %get-tuple-element.40.sides_ref, ...), custom_call_target="tpu_custom_call", output_to_operand_aliasing={{}: (0, {})} | custom-call | tf_op jit(solution)/shard_map/combine_pair/pallas_call | solution.py:627
  21.6 0.6 %collective-permute-done.4.received_ref = bf16[784,128]{1,0:T(8,128)(2,1)S(1)} collective-permute-done((bf16[784,128]{1,0:T(8,128)(2,1)S(1)}, bf16[784,128]{1,0:T(8,128)(2,1)S(1)}, u32[]{:S(2)}, u32[]{:S(2)}) %collective-permute-start.4) | collective-permute-done | bytes 200736 | tf_op jit(solution)/shard_map/ppermute | solution.py:607
  22.2 1.0 %combine_cross.1 = bf16[128,4,1024]{2,1,0:T(4,128)(2,1)} custom-call(bf16[128,4,1024]{2,1,0:T(4,128)(2,1)} %combine_pair.1.part_ref, bf16[2,1024,128]{2,1,0:T(8,128)(2,1)S(1)} %get-tuple-element.39.ends_ref, bf16[2,4,1024]{2,1,0:T(4,128)(2,1)S(1)} %get-tuple-element.40.sides_ref, ...), custom_call_target="tpu_custom_call", output_to_operand_aliasing={{}: (0, {})} | custom-call | tf_op jit(solution)/shard_map/combine_cross/pallas_call | solution.py:627
Async XLA Ops:
  1.5 7.0 %collective-permute-start.1 = (bf16[1024,128]{1,0:T(8,128)(2,1)S(1)}, bf16[1024,128]{1,0:T(8,128)(2,1)S(1)}, u32[]{:S(2)}, u32[]{:S(2)}) collective-permute-start(bf16[1024,128]{1,0:T(8,128)(2,1)S(1)} %get-tuple-element.26.after_ref), channel_id=1, source_target_pairs={{0,1},{1,2},{2,3},{3,0},{4,5},{5,6},{6,7},{7,4},{8,9},{9,10},{10,1... | collective-permute-start | bytes 786440 | tf_op jit(solution)/shard_map/ppermute | solution.py:541
  3.0 5.3 %collective-permute-start = (f32[64,128]{1,0:T(8,128)S(1)}, f32[64,128]{1,0:T(8,128)S(1)}, u32[]{:S(2)}, u32[]{:S(2)}) collective-permute-start(f32[64,128]{1,0:T(8,128)S(1)} %get-tuple-element.29.own_ref), channel_id=1, source_target_pairs={{0,4},{4,0},{8,12},{12,8},{16,20},{20,16},{24,28},{28,24},{1,5},{5... | collective-permute-start | bytes 98312 | tf_op jit(solution)/shard_map/ppermute | solution.py:551
  4.7 6.9 %collective-permute-start.2 = (f32[64,128]{1,0:T(8,128)S(1)}, f32[64,128]{1,0:T(8,128)S(1)}, u32[]{:S(2)}, u32[]{:S(2)}) collective-permute-start(f32[64,128]{1,0:T(8,128)S(1)} %get-tuple-element.37.own_ref), channel_id=1, source_target_pairs={{0,28},{4,8},{8,4},{12,16},{16,12},{20,24},{24,20},{28,0},{1,29},{... | collective-permute-start | bytes 98312 | tf_op jit(solution)/shard_map/ppermute | solution.py:552
  9.7 10.8 %collective-permute-start.3 = (bf16[784,128]{1,0:T(8,128)(2,1)S(1)}, bf16[784,128]{1,0:T(8,128)(2,1)S(1)}, u32[]{:S(2)}, u32[]{:S(2)}) collective-permute-start(bf16[784,128]{1,0:T(8,128)(2,1)S(1)} %remote_pair.1.after_ref.sent_ref), channel_id=1, source_target_pairs={{0,4},{4,0},{8,12},{12,8},{16,20},{20,16},{24,28},{28,24},{1,5},{5... | collective-permute-start | bytes 602120 | tf_op jit(solution)/shard_map/ppermute | solution.py:594
  12.6 9.6 %collective-permute-start.4 = (bf16[784,128]{1,0:T(8,128)(2,1)S(1)}, bf16[784,128]{1,0:T(8,128)(2,1)S(1)}, u32[]{:S(2)}, u32[]{:S(2)}) collective-permute-start(bf16[784,128]{1,0:T(8,128)(2,1)S(1)} %remote_cross.1.after_ref.sent_ref), channel_id=1, source_target_pairs={{0,28},{4,8},{8,4},{12,16},{16,12},{20,24},{24,20},{28,0},{1,29},{... | collective-permute-start | bytes 602120 | tf_op jit(solution)/shard_map/ppermute | solution.py:607

commit v8 on v7

--- a/solution.py
+++ b/solution.py
@@ -184,8 +184,7 @@
     pl.when(jnp.logical_not(early))(lambda: spread(tracers_ref, velocity_ref, top_ref, rest_ref, here_ref))
 
 
-def lift_first_kernel(after_ref, top_ref, above_ref, velocity_ref, out_ref):
-    del after_ref
+def lift_first(top_ref, above_ref, velocity_ref, out_ref):
     _, nodes, _, elements = velocity_ref.shape
     tracers = above_ref.shape[0] // nodes
     descent = descents(velocity_ref, 0)
@@ -226,9 +225,15 @@
     by_side(pair, weigh, levels, packet_ref, own_ref, weights_ref, extra_ref, chosen_ref)
 
 
-def remote_kernel(pair, after_ref, *refs):
-    del after_ref
-    by_side(pair, remote, *refs)
+def pair_kernel(
+    top_ref, above_ref, velocity_ref, rest_ref, weights_ref, extra_ref, chosen_ref,
+    out_ref, first_ref, blocks_ref, edge_ref,
+):
+    def both(ahead):
+        lift_first(top_ref, above_ref, velocity_ref, first_ref)
+        remote(ahead, first_ref, rest_ref, weights_ref, extra_ref, chosen_ref, out_ref, blocks_ref, edge_ref)
+
+    by_side(True, both)
 
 
 def weigh_remote_kernel(
@@ -571,26 +576,17 @@
         compiler_params=params(),
         name="spread",
     )(tracers, velocity, *early)
-    first = pl.pallas_call(
-        lift_first_kernel,
-        out_shape=shape((16, count, elements), bf16),
-        in_specs=[anywhere] + [vmem] * 3,
-        compiler_params=params(),
-        name="lift_first",
-    )(pair_weights[1], top, above, velocity)
-
     far_rows = 8 * (4 * count // elements)
 
     message = shape((12 * count + far_rows, elements), bf16)
     message_scratch = [pltpu.VMEM((2, 16, count // 2, 2 * elements), f32), pltpu.VMEM((4 * count, elements), bf16)]
-    pair_out = pl.pallas_call(
-        functools.partial(remote_kernel, True),
-        out_shape=message,
-        in_specs=[anywhere] + [vmem] * 5,
+    pair_out, first = pl.pallas_call(
+        pair_kernel,
+        out_shape=(message, shape((16, count, elements), bf16)),
         scratch_shapes=message_scratch,
         compiler_params=params(),
         name="remote_pair",
-    )(first, first, rest, *pair_weights)
+    )(top, above, velocity, rest, *pair_weights)
     pair_in = lax.ppermute(pair_out, "elem", pairing)
     cross_out = pl.pallas_call(
         functools.partial(weigh_remote_kernel, False, levels),

time: 23.3 us -> 23.3 us (level)
    pallas_call x2 -> x1, Pallas kernels: 1.13 us -> 1.03 us  [on_device(): pl.pallas_call(pair_kernel, out_shape=(message, shape((16, count, element...]
  transfers between devices with their start and end apart: 5 -> 5, of which waited for: 1 -> 1; matrix products, arithmetic and copies ran while one was open for 0% -> 0% of each run, Pallas kernels for 38% -> 37%
where the time goes in v8:
time: 23.3 us; the launch traced here: 23.2 us
  Pallas kernels  11.2 us (48%)
  starting transfers between devices  11.1 us (48%)
  waiting for transfers between devices  0.75 us (3%)
    pallas_call x1, Pallas kernels, on_device(): pl.pallas_call(local_kernel, out_shape=(result, shape((2, columns, elemen...  4.3 us
    ppermute x1, starting transfers between devices, on_device(): cross_in = lax.ppermute(cross_out, 'elem', crossing)  3.61 us
    ppermute x1, starting transfers between devices, on_device(): cross_packet = lax.ppermute(cross_sent, 'elem', crossing)  3.55 us
    pallas_call x2, Pallas kernels, on_device(): pl.pallas_call(functools.partial(combine_kernel, pair), out_shape=result,...  2.04 us
    ppermute x1, starting transfers between devices, on_device(): pair_in = lax.ppermute(pair_out, 'elem', pairing)  1.84 us
    ppermute x1, starting transfers between devices, on_device(): pair_packet = lax.ppermute(pair_sent, 'elem', pairing)  1.66 us
    pallas_call x1, Pallas kernels, on_device(): pl.pallas_call(prepare_kernel, out_shape=(shape((columns, elements), bf16...  1.53 us
    pallas_call x1, Pallas kernels, on_device(): pl.pallas_call(functools.partial(weigh_remote_kernel, False, levels), out...  1.07 us
  transfers between devices with their start and end apart: 5, of which 1 were waited for; matrix products, arithmetic and copies ran while one was open for 0% of the time, Pallas kernels for 37%

profile of v8, /device:TPU:0, one launch (start us, length us, event | category | flops | bytes accessed | tf_op | source)
XLA Modules:
  0.0 23.2 jit_solution(13730609814286268249)
XLA Ops:
  0.0 1.5 %prepare.1 = (bf16[1024,128]{1,0:T(8,128)(2,1)S(1)}, f32[64,128]{1,0:T(8,128)S(1)}, f32[64,128]{1,0:T(8,128)S(1)}, bf16[128,4,1024]{2,1,0:T(4,128)(2,1)S(1)}, f3...) custom-call(bf16[128,4,1024]{2,1,0:T(4,128)(2,1)} %tracers_hbm.1, ...), custom_call_target="tpu_custom_call" | custom-call | tf_op jit(solution)/shard_map/prepare/pallas_call | solution.py:536
  1.5 0.5 %collective-permute-start = (bf16[1024,128]{1,0:T(8,128)(2,1)S(1)}, bf16[1024,128]{1,0:T(8,128)(2,1)S(1)}, u32[]{:S(2)}, u32[]{:S(2)}) collective-permute-start(bf16[1024,128]{1,0:T(8,128)(2,1)S(1)} %get-tuple-element.33.after_ref), channel_id=1, source_target_pairs={{0,1},{1,2},{2,3},{3,0},{4,5},{5,6},{6,7},{7,4},{8,9},{9,10},{10,1... | collective-permute-start | bytes 786440 | tf_op jit(solution)/shard_map/ppermute | solution.py:546
  2.0 1.0 %spread_early.1 = (bf16[1024,128]{1,0:T(8,128)(2,1)S(1)}, bf16[16,64,384]{2,1,0:T(8,128)(2,1)S(1)}, f32[64,128]{1,0:T(8,128)S(1)}) custom-call(bf16[128,4,1024]{2,1,0:T(4,128)(2,1)S(1)} %get-tuple-element.28.tracers_ref, f32[3,16,4,128]{3,2,1,0:T(4,128)S(1)} %get-tuple-element.25.velocity_ref, f32[64,128]{1,0:T(8,128)S(1)} %get-tuple-element.29.packet_ref), custom_call_target="tpu_custom_call" | custom-call | tf_op jit(solution)/shard_map/spread_early/pallas_call | solution.py:549
  3.0 1.7 %collective-permute-start.1 = (f32[64,128]{1,0:T(8,128)S(1)}, f32[64,128]{1,0:T(8,128)S(1)}, u32[]{:S(2)}, u32[]{:S(2)}) collective-permute-start(f32[64,128]{1,0:T(8,128)S(1)} %get-tuple-element.35.own_ref), channel_id=1, source_target_pairs={{0,4},{4,0},{8,12},{12,8},{16,20},{20,16},{24,28},{28,24},{1,5},{5... | collective-permute-start | bytes 98312 | tf_op jit(solution)/shard_map/ppermute | solution.py:556
  4.7 3.5 %collective-permute-start.2 = (f32[64,128]{1,0:T(8,128)S(1)}, f32[64,128]{1,0:T(8,128)S(1)}, u32[]{:S(2)}, u32[]{:S(2)}) collective-permute-start(f32[64,128]{1,0:T(8,128)S(1)} %get-tuple-element.41.own_ref), channel_id=1, source_target_pairs={{0,28},{4,8},{8,4},{12,16},{16,12},{20,24},{24,20},{28,0},{1,29},{... | collective-permute-start | bytes 98312 | tf_op jit(solution)/shard_map/ppermute | solution.py:557
  8.2 0.1 spread.1
  8.3 0.0 collective-permute-done.1.packet_ref
  8.3 0.2 weigh_pair.1
  8.5 0.0 collective-permute-done.above_ref
  8.6 1.0 %remote_pair.1 = (bf16[784,128]{1,0:T(8,128)(2,1)S(1)}, bf16[16,64,128]{2,1,0:T(8,128)(2,1)S(1)}) custom-call(bf16[1024,128]{1,0:T(8,128)(2,1)S(1)} %get-tuple-element.32.top_ref, bf16[1024,128]{1,0:T(8,128)(2,1)S(1)} %collective-permute-done.above_ref, f32[3,16,4,128]{3,2,1,0:T(4,128)S(1)} %get-tuple-element.25.velocity_ref, ...), custom_call_target="tpu_custom_call" | custom-call | tf_op jit(solution)/shard_map/remote_pair/pallas_call | solution.py:583
  9.6 1.8 %collective-permute-start.3 = (bf16[784,128]{1,0:T(8,128)(2,1)S(1)}, bf16[784,128]{1,0:T(8,128)(2,1)S(1)}, u32[]{:S(2)}, u32[]{:S(2)}) collective-permute-start(bf16[784,128]{1,0:T(8,128)(2,1)S(1)} %get-tuple-element.40.after_ref.sent_ref), channel_id=1, source_target_pairs={{0,4},{4,0},{8,12},{12,8},{16,20},{20,16},{24,28},{28,24},{1,5},{5... | collective-permute-start | bytes 602120 | tf_op jit(solution)/shard_map/ppermute | solution.py:590
  11.4 0.0 collective-permute-done.2.packet_ref
  11.4 1.1 %remote_cross.1.after_ref.sent_ref = bf16[784,128]{1,0:T(8,128)(2,1)S(1)} custom-call(bf16[784,128]{1,0:T(8,128)(2,1)S(1)} %get-tuple-element.40.after_ref.sent_ref, f32[64,128]{1,0:T(8,128)S(1)} %collective-permute-done.2.packet_ref, f32[64,128]{1,0:T(8,128)S(1)} %get-tuple-element.41.own_ref, bf16[16,64,128]{2,1,0:T(8,128)(2,1)S(1)} %get-tuple-element.39.first_ref, ...), custom_call_target="tpu_custom_call" | custom-call | tf_op jit(solution)/shard_map/remote_cross/pallas_call | solution.py:591
  12.5 3.6 %collective-permute-start.4 = (bf16[784,128]{1,0:T(8,128)(2,1)S(1)}, bf16[784,128]{1,0:T(8,128)(2,1)S(1)}, u32[]{:S(2)}, u32[]{:S(2)}) collective-permute-start(bf16[784,128]{1,0:T(8,128)(2,1)S(1)} %remote_cross.1.after_ref.sent_ref), channel_id=1, source_target_pairs={{0,28},{4,8},{8,4},{12,16},{16,12},{20,24},{24,20},{28,0},{1,29},{... | collective-permute-start | bytes 602120 | tf_op jit(solution)/shard_map/ppermute | solution.py:603
  16.1 4.3 %local.1 = (bf16[128,4,1024]{2,1,0:T(4,128)(2,1)}, bf16[2,1024,128]{2,1,0:T(8,128)(2,1)S(1)}, bf16[2,4,1024]{2,1,0:T(4,128)(2,1)S(1)}) custom-call(f32[3,16,4,128]{3,2,1,0:T(4,128)S(1)} %get-tuple-element.25.velocity_ref, f32[16,128]{1,0:T(8,128)S(1)} %get-tuple-element.26.mass_ref, s32[1,128]{1,0:T(1,128)S(1)} %get-tuple-element.27.source_ref, ...), custom_call_target="tpu_custom_call" | custom-call | flops 99999997952 | bytes 1000000000 | tf_op jit(solution)/shard_map/local/pallas_call | solution.py:605
  20.4 0.0 collective-permute-done.3.received_ref
  20.4 1.0 %combine_pair.1.part_ref = bf16[128,4,1024]{2,1,0:T(4,128)(2,1)} custom-call(bf16[128,4,1024]{2,1,0:T(4,128)(2,1)} %get-tuple-element.42.part_ref, bf16[2,1024,128]{2,1,0:T(8,128)(2,1)S(1)} %get-tuple-element.43.ends_ref, bf16[2,4,1024]{2,1,0:T(4,128)(2,1)S(1)} %get-tuple-element.44.sides_ref, ...), custom_call_target="tpu_custom_call", output_to_operand_aliasing={{}: (0, {})} | custom-call | tf_op jit(solution)/shard_map/combine_pair/pallas_call | solution.py:623
  21.4 0.7 %collective-permute-done.4.received_ref = bf16[784,128]{1,0:T(8,128)(2,1)S(1)} collective-permute-done((bf16[784,128]{1,0:T(8,128)(2,1)S(1)}, bf16[784,128]{1,0:T(8,128)(2,1)S(1)}, u32[]{:S(2)}, u32[]{:S(2)}) %collective-permute-start.4) | collective-permute-done | bytes 200736 | tf_op jit(solution)/shard_map/ppermute | solution.py:603
  22.2 1.0 %combine_cross.1 = bf16[128,4,1024]{2,1,0:T(4,128)(2,1)} custom-call(bf16[128,4,1024]{2,1,0:T(4,128)(2,1)} %combine_pair.1.part_ref, bf16[2,1024,128]{2,1,0:T(8,128)(2,1)S(1)} %get-tuple-element.43.ends_ref, bf16[2,4,1024]{2,1,0:T(4,128)(2,1)S(1)} %get-tuple-element.44.sides_ref, ...), custom_call_target="tpu_custom_call", output_to_operand_aliasing={{}: (0, {})} | custom-call | tf_op jit(solution)/shard_map/combine_cross/pallas_call | solution.py:623
Async XLA Ops:
  1.5 7.0 %collective-permute-start = (bf16[1024,128]{1,0:T(8,128)(2,1)S(1)}, bf16[1024,128]{1,0:T(8,128)(2,1)S(1)}, u32[]{:S(2)}, u32[]{:S(2)}) collective-permute-start(bf16[1024,128]{1,0:T(8,128)(2,1)S(1)} %get-tuple-element.33.after_ref), channel_id=1, source_target_pairs={{0,1},{1,2},{2,3},{3,0},{4,5},{5,6},{6,7},{7,4},{8,9},{9,10},{10,1... | collective-permute-start | bytes 786440 | tf_op jit(solution)/shard_map/ppermute | solution.py:546
  3.0 5.3 %collective-permute-start.1 = (f32[64,128]{1,0:T(8,128)S(1)}, f32[64,128]{1,0:T(8,128)S(1)}, u32[]{:S(2)}, u32[]{:S(2)}) collective-permute-start(f32[64,128]{1,0:T(8,128)S(1)} %get-tuple-element.35.own_ref), channel_id=1, source_target_pairs={{0,4},{4,0},{8,12},{12,8},{16,20},{20,16},{24,28},{28,24},{1,5},{5... | collective-permute-start | bytes 98312 | tf_op jit(solution)/shard_map/ppermute | solution.py:556
  4.7 6.8 %collective-permute-start.2 = (f32[64,128]{1,0:T(8,128)S(1)}, f32[64,128]{1,0:T(8,128)S(1)}, u32[]{:S(2)}, u32[]{:S(2)}) collective-permute-start(f32[64,128]{1,0:T(8,128)S(1)} %get-tuple-element.41.own_ref), channel_id=1, source_target_pairs={{0,28},{4,8},{8,4},{12,16},{16,12},{20,24},{24,20},{28,0},{1,29},{... | collective-permute-start | bytes 98312 | tf_op jit(solution)/shard_map/ppermute | solution.py:557
  9.6 10.8 %collective-permute-start.3 = (bf16[784,128]{1,0:T(8,128)(2,1)S(1)}, bf16[784,128]{1,0:T(8,128)(2,1)S(1)}, u32[]{:S(2)}, u32[]{:S(2)}) collective-permute-start(bf16[784,128]{1,0:T(8,128)(2,1)S(1)} %get-tuple-element.40.after_ref.sent_ref), channel_id=1, source_target_pairs={{0,4},{4,0},{8,12},{12,8},{16,20},{20,16},{24,28},{28,24},{1,5},{5... | collective-permute-start | bytes 602120 | tf_op jit(solution)/shard_map/ppermute | solution.py:590
  12.5 9.7 %collective-permute-start.4 = (bf16[784,128]{1,0:T(8,128)(2,1)S(1)}, bf16[784,128]{1,0:T(8,128)(2,1)S(1)}, u32[]{:S(2)}, u32[]{:S(2)}) collective-permute-start(bf16[784,128]{1,0:T(8,128)(2,1)S(1)} %remote_cross.1.after_ref.sent_ref), channel_id=1, source_target_pairs={{0,28},{4,8},{8,4},{12,16},{16,12},{20,24},{24,20},{28,0},{1,29},{... | collective-permute-start | bytes 602120 | tf_op jit(solution)/shard_map/ppermute | solution.py:603

commit v9 on v8

--- a/solution.py
+++ b/solution.py
@@ -75,7 +75,7 @@
     lowest_ref, cross_ref, pair_ref, tracers_ref, velocity_ref, mass_ref, source_ref, pair_of_levels_ref, sems,
 ):
     elements, levels, columns = tracers_hbm.shape
-    step = 256
+    step = 512
     copies = [
         pltpu.make_async_copy(here, there, sems.at[n])
         for n, (here, there) in enumerate(

time: 23.3 us -> 23.4 us (level)
  no operation moved by 1% of the time
where the time goes in v9:
time: 23.4 us; the launch traced here: 23.2 us
  Pallas kernels  11.3 us (48%)
  starting transfers between devices  11.1 us (47%)
  waiting for transfers between devices  0.75 us (3%)
    pallas_call x1, Pallas kernels, on_device(): pl.pallas_call(local_kernel, out_shape=(result, shape((2, columns, elemen...  4.3 us
    ppermute x1, starting transfers between devices, on_device(): cross_in = lax.ppermute(cross_out, 'elem', crossing)  3.59 us
    ppermute x1, starting transfers between devices, on_device(): cross_packet = lax.ppermute(cross_sent, 'elem', crossing)  3.54 us
    pallas_call x2, Pallas kernels, on_device(): pl.pallas_call(functools.partial(combine_kernel, pair), out_shape=result,...  2.05 us
    ppermute x1, starting transfers between devices, on_device(): pair_in = lax.ppermute(pair_out, 'elem', pairing)  1.84 us
    ppermute x1, starting transfers between devices, on_device(): pair_packet = lax.ppermute(pair_sent, 'elem', pairing)  1.66 us
    pallas_call x1, Pallas kernels, on_device(): pl.pallas_call(prepare_kernel, out_shape=(shape((columns, elements), bf16...  1.56 us
    pallas_call x1, Pallas kernels, on_device(): pl.pallas_call(functools.partial(weigh_remote_kernel, False, levels), out...  1.07 us
  transfers between devices with their start and end apart: 5, of which 1 were waited for; matrix products, arithmetic and copies ran while one was open for 0% of the time, Pallas kernels for 37%

profile of v9, /device:TPU:0, one launch (start us, length us, event | category | flops | bytes accessed | tf_op | source)
XLA Modules:
  0.0 23.2 jit_solution(17281936638242610201)
XLA Ops:
  0.0 1.6 %prepare.1 = (bf16[1024,128]{1,0:T(8,128)(2,1)S(1)}, f32[64,128]{1,0:T(8,128)S(1)}, f32[64,128]{1,0:T(8,128)S(1)}, bf16[128,4,1024]{2,1,0:T(4,128)(2,1)S(1)}, f3...) custom-call(bf16[128,4,1024]{2,1,0:T(4,128)(2,1)} %tracers_hbm.1, ...), custom_call_target="tpu_custom_call" | custom-call | tf_op jit(solution)/shard_map/prepare/pallas_call | solution.py:536
  1.6 0.5 %collective-permute-start = (bf16[1024,128]{1,0:T(8,128)(2,1)S(1)}, bf16[1024,128]{1,0:T(8,128)(2,1)S(1)}, u32[]{:S(2)}, u32[]{:S(2)}) collective-permute-start(bf16[1024,128]{1,0:T(8,128)(2,1)S(1)} %get-tuple-element.33.after_ref), channel_id=1, source_target_pairs={{0,1},{1,2},{2,3},{3,0},{4,5},{5,6},{6,7},{7,4},{8,9},{9,10},{10,1... | collective-permute-start | bytes 786440 | tf_op jit(solution)/shard_map/ppermute | solution.py:546
  2.1 1.0 %spread_early.1 = (bf16[1024,128]{1,0:T(8,128)(2,1)S(1)}, bf16[16,64,384]{2,1,0:T(8,128)(2,1)S(1)}, f32[64,128]{1,0:T(8,128)S(1)}) custom-call(bf16[128,4,1024]{2,1,0:T(4,128)(2,1)S(1)} %get-tuple-element.28.tracers_ref, f32[3,16,4,128]{3,2,1,0:T(4,128)S(1)} %get-tuple-element.25.velocity_ref, f32[64,128]{1,0:T(8,128)S(1)} %get-tuple-element.29.packet_ref), custom_call_target="tpu_custom_call" | custom-call | tf_op jit(solution)/shard_map/spread_early/pallas_call | solution.py:549
  3.0 1.7 %collective-permute-start.1 = (f32[64,128]{1,0:T(8,128)S(1)}, f32[64,128]{1,0:T(8,128)S(1)}, u32[]{:S(2)}, u32[]{:S(2)}) collective-permute-start(f32[64,128]{1,0:T(8,128)S(1)} %get-tuple-element.35.own_ref), channel_id=1, source_target_pairs={{0,4},{4,0},{8,12},{12,8},{16,20},{20,16},{24,28},{28,24},{1,5},{5... | collective-permute-start | bytes 98312 | tf_op jit(solution)/shard_map/ppermute | solution.py:556
  4.7 3.5 %collective-permute-start.2 = (f32[64,128]{1,0:T(8,128)S(1)}, f32[64,128]{1,0:T(8,128)S(1)}, u32[]{:S(2)}, u32[]{:S(2)}) collective-permute-start(f32[64,128]{1,0:T(8,128)S(1)} %get-tuple-element.41.own_ref), channel_id=1, source_target_pairs={{0,28},{4,8},{8,4},{12,16},{16,12},{20,24},{24,20},{28,0},{1,29},{... | collective-permute-start | bytes 98312 | tf_op jit(solution)/shard_map/ppermute | solution.py:557
  8.2 0.1 spread.1
  8.3 0.0 collective-permute-done.1.packet_ref
  8.3 0.2 weigh_pair.1
  8.6 0.0 collective-permute-done.above_ref
  8.6 1.0 %remote_pair.1 = (bf16[784,128]{1,0:T(8,128)(2,1)S(1)}, bf16[16,64,128]{2,1,0:T(8,128)(2,1)S(1)}) custom-call(bf16[1024,128]{1,0:T(8,128)(2,1)S(1)} %get-tuple-element.32.top_ref, bf16[1024,128]{1,0:T(8,128)(2,1)S(1)} %collective-permute-done.above_ref, f32[3,16,4,128]{3,2,1,0:T(4,128)S(1)} %get-tuple-element.25.velocity_ref, ...), custom_call_target="tpu_custom_call" | custom-call | tf_op jit(solution)/shard_map/remote_pair/pallas_call | solution.py:583
  9.6 1.8 %collective-permute-start.3 = (bf16[784,128]{1,0:T(8,128)(2,1)S(1)}, bf16[784,128]{1,0:T(8,128)(2,1)S(1)}, u32[]{:S(2)}, u32[]{:S(2)}) collective-permute-start(bf16[784,128]{1,0:T(8,128)(2,1)S(1)} %get-tuple-element.40.after_ref.sent_ref), channel_id=1, source_target_pairs={{0,4},{4,0},{8,12},{12,8},{16,20},{20,16},{24,28},{28,24},{1,5},{5... | collective-permute-start | bytes 602120 | tf_op jit(solution)/shard_map/ppermute | solution.py:590
  11.4 0.0 collective-permute-done.2.packet_ref
  11.4 1.1 %remote_cross.1.after_ref.sent_ref = bf16[784,128]{1,0:T(8,128)(2,1)S(1)} custom-call(bf16[784,128]{1,0:T(8,128)(2,1)S(1)} %get-tuple-element.40.after_ref.sent_ref, f32[64,128]{1,0:T(8,128)S(1)} %collective-permute-done.2.packet_ref, f32[64,128]{1,0:T(8,128)S(1)} %get-tuple-element.41.own_ref, bf16[16,64,128]{2,1,0:T(8,128)(2,1)S(1)} %get-tuple-element.39.first_ref, ...), custom_call_target="tpu_custom_call" | custom-call | tf_op jit(solution)/shard_map/remote_cross/pallas_call | solution.py:591
  12.5 3.6 %collective-permute-start.4 = (bf16[784,128]{1,0:T(8,128)(2,1)S(1)}, bf16[784,128]{1,0:T(8,128)(2,1)S(1)}, u32[]{:S(2)}, u32[]{:S(2)}) collective-permute-start(bf16[784,128]{1,0:T(8,128)(2,1)S(1)} %remote_cross.1.after_ref.sent_ref), channel_id=1, source_target_pairs={{0,28},{4,8},{8,4},{12,16},{16,12},{20,24},{24,20},{28,0},{1,29},{... | collective-permute-start | bytes 602120 | tf_op jit(solution)/shard_map/ppermute | solution.py:603
  16.1 4.3 %local.1 = (bf16[128,4,1024]{2,1,0:T(4,128)(2,1)}, bf16[2,1024,128]{2,1,0:T(8,128)(2,1)S(1)}, bf16[2,4,1024]{2,1,0:T(4,128)(2,1)S(1)}) custom-call(f32[3,16,4,128]{3,2,1,0:T(4,128)S(1)} %get-tuple-element.25.velocity_ref, f32[16,128]{1,0:T(8,128)S(1)} %get-tuple-element.26.mass_ref, s32[1,128]{1,0:T(1,128)S(1)} %get-tuple-element.27.source_ref, ...), custom_call_target="tpu_custom_call" | custom-call | flops 99999997952 | bytes 1000000000 | tf_op jit(solution)/shard_map/local/pallas_call | solution.py:605
  20.4 0.0 collective-permute-done.3.received_ref
  20.4 1.0 %combine_pair.1.part_ref = bf16[128,4,1024]{2,1,0:T(4,128)(2,1)} custom-call(bf16[128,4,1024]{2,1,0:T(4,128)(2,1)} %get-tuple-element.42.part_ref, bf16[2,1024,128]{2,1,0:T(8,128)(2,1)S(1)} %get-tuple-element.43.ends_ref, bf16[2,4,1024]{2,1,0:T(4,128)(2,1)S(1)} %get-tuple-element.44.sides_ref, ...), custom_call_target="tpu_custom_call", output_to_operand_aliasing={{}: (0, {})} | custom-call | tf_op jit(solution)/shard_map/combine_pair/pallas_call | solution.py:623
  21.5 0.7 %collective-permute-done.4.received_ref = bf16[784,128]{1,0:T(8,128)(2,1)S(1)} collective-permute-done((bf16[784,128]{1,0:T(8,128)(2,1)S(1)}, bf16[784,128]{1,0:T(8,128)(2,1)S(1)}, u32[]{:S(2)}, u32[]{:S(2)}) %collective-permute-start.4) | collective-permute-done | bytes 200736 | tf_op jit(solution)/shard_map/ppermute | solution.py:603
  22.2 1.0 %combine_cross.1 = bf16[128,4,1024]{2,1,0:T(4,128)(2,1)} custom-call(bf16[128,4,1024]{2,1,0:T(4,128)(2,1)} %combine_pair.1.part_ref, bf16[2,1024,128]{2,1,0:T(8,128)(2,1)S(1)} %get-tuple-element.43.ends_ref, bf16[2,4,1024]{2,1,0:T(4,128)(2,1)S(1)} %get-tuple-element.44.sides_ref, ...), custom_call_target="tpu_custom_call", output_to_operand_aliasing={{}: (0, {})} | custom-call | tf_op jit(solution)/shard_map/combine_cross/pallas_call | solution.py:623
Async XLA Ops:
  1.6 7.0 %collective-permute-start = (bf16[1024,128]{1,0:T(8,128)(2,1)S(1)}, bf16[1024,128]{1,0:T(8,128)(2,1)S(1)}, u32[]{:S(2)}, u32[]{:S(2)}) collective-permute-start(bf16[1024,128]{1,0:T(8,128)(2,1)S(1)} %get-tuple-element.33.after_ref), channel_id=1, source_target_pairs={{0,1},{1,2},{2,3},{3,0},{4,5},{5,6},{6,7},{7,4},{8,9},{9,10},{10,1... | collective-permute-start | bytes 786440 | tf_op jit(solution)/shard_map/ppermute | solution.py:546
  3.0 5.3 %collective-permute-start.1 = (f32[64,128]{1,0:T(8,128)S(1)}, f32[64,128]{1,0:T(8,128)S(1)}, u32[]{:S(2)}, u32[]{:S(2)}) collective-permute-start(f32[64,128]{1,0:T(8,128)S(1)} %get-tuple-element.35.own_ref), channel_id=1, source_target_pairs={{0,4},{4,0},{8,12},{12,8},{16,20},{20,16},{24,28},{28,24},{1,5},{5... | collective-permute-start | bytes 98312 | tf_op jit(solution)/shard_map/ppermute | solution.py:556
  4.7 6.8 %collective-permute-start.2 = (f32[64,128]{1,0:T(8,128)S(1)}, f32[64,128]{1,0:T(8,128)S(1)}, u32[]{:S(2)}, u32[]{:S(2)}) collective-permute-start(f32[64,128]{1,0:T(8,128)S(1)} %get-tuple-element.41.own_ref), channel_id=1, source_target_pairs={{0,28},{4,8},{8,4},{12,16},{16,12},{20,24},{24,20},{28,0},{1,29},{... | collective-permute-start | bytes 98312 | tf_op jit(solution)/shard_map/ppermute | solution.py:557
  9.6 10.8 %collective-permute-start.3 = (bf16[784,128]{1,0:T(8,128)(2,1)S(1)}, bf16[784,128]{1,0:T(8,128)(2,1)S(1)}, u32[]{:S(2)}, u32[]{:S(2)}) collective-permute-start(bf16[784,128]{1,0:T(8,128)(2,1)S(1)} %get-tuple-element.40.after_ref.sent_ref), channel_id=1, source_target_pairs={{0,4},{4,0},{8,12},{12,8},{16,20},{20,16},{24,28},{28,24},{1,5},{5... | collective-permute-start | bytes 602120 | tf_op jit(solution)/shard_map/ppermute | solution.py:590
  12.5 9.7 %collective-permute-start.4 = (bf16[784,128]{1,0:T(8,128)(2,1)S(1)}, bf16[784,128]{1,0:T(8,128)(2,1)S(1)}, u32[]{:S(2)}, u32[]{:S(2)}) collective-permute-start(bf16[784,128]{1,0:T(8,128)(2,1)S(1)} %remote_cross.1.after_ref.sent_ref), channel_id=1, source_target_pairs={{0,28},{4,8},{8,4},{12,16},{16,12},{20,24},{24,20},{28,0},{1,29},{... | collective-permute-start | bytes 602120 | tf_op jit(solution)/shard_map/ppermute | solution.py:603
